TPU v7x, 128 devices: a whole 4x4x4 slice. The times are simulated.
128 devices in a mesh: rep: 4 (over x_lo, core), fsdp: 32 (over z, x_hi, y).
Axes of the slice: x: 4 (x_hi: 2, x_lo: 2; x = x_hi * 2 + x_lo), y: 4, z: 4, core: 2. Of those that a mesh axis runs over, the one named last changes fastest.
Arguments:
- patches: bfloat16 [4, 1, 2, 32, 196, 768], P('rep', None, None, 'fsdp'), may hold values from -6 to 6
- labels: int32 [4, 1, 2, 32], P('rep', None, None, 'fsdp'), may hold values from 0 to 999
- counts: int32 [4, 1, 2], P('rep'), may hold values from 17 to 32
- weights: float32 [8593408], P('fsdp')
- first_moments: float32 [4, 8593408], P('rep', 'fsdp')
- second_moments: float32 [4, 8593408], P('rep', 'fsdp')
- outer_momentum: float32 [8593408], P('fsdp')
Outputs:
- averaged_diff: float32 [8593408], P('fsdp')
- momentum_out: float32 [8593408], P('fsdp')
- new_weights: float32 [8593408], P('fsdp')
- first_out: float32 [4, 8593408], P('rep', 'fsdp')
- second_out: float32 [4, 8593408], P('rep', 'fsdp')
- loss_sums: float32 [4, 1], P('rep')
All inputs are finite; a program needn't handle non-finite values.
Results may differ from a plain program's by a relative error of at most 0.013.
Values may be sent and summed in bfloat16 or wider, within the bound.
A program may use at most 320 MiB of HBM per device.

v0:
```python
from functools import partial

import jax
import jax.numpy as jnp
from jax import lax
from jax.sharding import PartitionSpec as P

D = 768
HEADS = 12
HEAD_DIM = 64
FF = 3072
CLS = 1000
PIX = 768
P_SIZE = 196
LAYERS = 1
MB = 2
STEP = 10


NORM_EPS = 1e-06
SMOOTHING = 0.1
BETA_ONE = 0.9
BETA_TWO = 0.95
ADAM_EPS = 1e-08
DECAY = 0.05
INNER_RATE = 0.01
OUTER_RATE = 0.7
OUTER_MU = 0.9


def layout():
    shapes = [(PIX, D), (P_SIZE, D), (2, D), (D, CLS)]
    shapes += [(4, D), (D, 3 * D), (D, D), (D, FF), (FF, D)]
    return shapes


def unflatten(flat):
    pieces = []
    start = 0
    for shape in layout():
        count = shape[0] * shape[1]
        pieces.append(flat[start : start + count].reshape(shape))
        start += count
    return pieces


def normalize(x, gain, shift):
    mean = jnp.mean(x, -1, keepdims=True)
    centred = x - mean
    var = jnp.mean(centred * centred, -1, keepdims=True)
    return centred * lax.rsqrt(var + NORM_EPS) * gain + shift


def pool(h, gain, shift):
    return jnp.mean(normalize(h, gain, shift), 1)


def matmul(left, right):
    return jnp.einsum("bpd,de->bpe", left, right, preferred_element_type=jnp.float32)


def heads_of(mix):
    split = mix.reshape(mix.shape[0], P_SIZE, 3, HEADS, HEAD_DIM)
    return (split[:, :, 0], split[:, :, 1], split[:, :, 2])


def layer_forward(h, layer_weights):
    norms, qkv, out, fc_in, fc_out = layer_weights
    batch = h.shape[0]
    gains = norms.astype(jnp.float32)
    normed = normalize(h, gains[0], gains[1]).astype(jnp.bfloat16)
    mix = matmul(normed, qkv).astype(jnp.bfloat16)
    query, key_rows, value = heads_of(mix)
    scores = jnp.einsum(
        "bqhe,bkhe->bhqk", query, key_rows, preferred_element_type=jnp.float32
    ) * HEAD_DIM ** (-0.5)
    top = jnp.max(scores, -1, keepdims=True)
    expo = jnp.exp(scores - top)
    total = jnp.sum(expo, -1, keepdims=True)
    prob = expo / total
    logsum = top + jnp.log(total)
    mixed = jnp.einsum(
        "bhqk,bkhe->bqhe", prob.astype(jnp.bfloat16), value, preferred_element_type=jnp.float32
    )
    mixed = mixed.reshape(batch, P_SIZE, D).astype(jnp.bfloat16)
    h_mid = h + matmul(mixed, out)
    normed_two = normalize(h_mid, gains[2], gains[3]).astype(jnp.bfloat16)
    pre = matmul(normed_two, fc_in)
    hidden = jax.nn.gelu(pre, approximate=False).astype(jnp.bfloat16)
    h_out = h_mid + matmul(hidden, fc_out)
    return (h_out, (h, normed, mix, logsum, mixed, h_mid, normed_two, pre, hidden))


def layer_backward(d_out, kept, layer_weights):
    norms, qkv, out, fc_in, fc_out = layer_weights
    h, normed, mix, logsum, mixed, h_mid, normed_two, pre, hidden = kept
    batch = h.shape[0]
    gains = norms.astype(jnp.float32)
    scale = HEAD_DIM ** (-0.5)
    d_branch = d_out.astype(jnp.bfloat16)
    d_fc_out = jnp.einsum("bpf,bpd->fd", hidden, d_branch, preferred_element_type=jnp.float32)
    d_hidden = jnp.einsum("bpd,fd->bpf", d_branch, fc_out, preferred_element_type=jnp.float32)
    unused, gelu_pull = jax.vjp(partial(jax.nn.gelu, approximate=False), pre)
    d_pre = gelu_pull(d_hidden)[0].astype(jnp.bfloat16)
    d_fc_in = jnp.einsum("bpd,bpf->df", normed_two, d_pre, preferred_element_type=jnp.float32)
    d_normed_two = jnp.einsum("bpf,df->bpd", d_pre, fc_in, preferred_element_type=jnp.float32)
    unused, norm_pull = jax.vjp(normalize, h_mid, gains[2], gains[3])
    d_mid_norm, d_gain_two, d_shift_two = norm_pull(d_normed_two)
    d_mid = d_out + d_mid_norm
    d_attend = d_mid.astype(jnp.bfloat16)
    d_out_w = jnp.einsum("bpd,bpe->de", mixed, d_attend, preferred_element_type=jnp.float32)
    d_mixed = jnp.einsum("bpe,de->bpd", d_attend, out, preferred_element_type=jnp.float32)
    d_mixed = d_mixed.astype(jnp.bfloat16).reshape(batch, P_SIZE, HEADS, HEAD_DIM)
    query, key_rows, value = heads_of(mix)
    scores = (
        jnp.einsum("bqhe,bkhe->bhqk", query, key_rows, preferred_element_type=jnp.float32) * scale
    )
    prob = jnp.exp(scores - logsum)
    d_value = jnp.einsum(
        "bhqk,bqhe->bkhe", prob.astype(jnp.bfloat16), d_mixed, preferred_element_type=jnp.float32
    )
    d_prob = jnp.einsum("bqhe,bkhe->bhqk", d_mixed, value, preferred_element_type=jnp.float32)
    d_scores = (prob * (d_prob - jnp.sum(prob * d_prob, -1, keepdims=True))).astype(jnp.bfloat16)
    d_query = (
        jnp.einsum("bhqk,bkhe->bqhe", d_scores, key_rows, preferred_element_type=jnp.float32)
        * scale
    )
    d_key = (
        jnp.einsum("bhqk,bqhe->bkhe", d_scores, query, preferred_element_type=jnp.float32) * scale
    )
    d_mix = (
        jnp.stack([d_query, d_key, d_value], 2).reshape(batch, P_SIZE, 3 * D).astype(jnp.bfloat16)
    )
    d_qkv = jnp.einsum("bpd,bpe->de", normed, d_mix, preferred_element_type=jnp.float32)
    d_normed = jnp.einsum("bpe,de->bpd", d_mix, qkv, preferred_element_type=jnp.float32)
    unused, norm_pull = jax.vjp(normalize, h, gains[0], gains[1])
    d_in_norm, d_gain_one, d_shift_one = norm_pull(d_normed)
    d_norms = jnp.stack([d_gain_one, d_shift_one, d_gain_two, d_shift_two])
    return (d_mid + d_in_norm, [d_norms, d_qkv, d_out_w, d_fc_in, d_fc_out])


def image_grads(whole, patches, labels, scale):
    pieces = unflatten(whole)
    embed, pos, final, head = pieces[:4]
    layer_sets = [pieces[4:9]]
    h = jnp.einsum("bpx,xd->bpd", patches, embed, preferred_element_type=jnp.float32) + pos.astype(
        jnp.float32
    )
    layer_weights = layer_sets[0]
    h, keep = layer_forward(h, layer_weights)
    kept = [keep]
    ends = final.astype(jnp.float32)
    pooled, pool_pull = jax.vjp(pool, h, ends[0], ends[1])
    pooled_low = pooled.astype(jnp.bfloat16)
    logits = jnp.dot(pooled_low, head, preferred_element_type=jnp.float32)
    logp = jax.nn.log_softmax(logits, -1)
    classes = lax.broadcasted_iota(jnp.int32, logits.shape, 1)
    target = (1.0 - SMOOTHING) * (classes == labels[:, None]).astype(jnp.float32) + SMOOTHING / CLS
    values = -jnp.sum(target * logp, -1)
    d_logits = (scale[:, None] * (jnp.exp(logp) - target)).astype(jnp.bfloat16)
    d_head = jnp.einsum("bd,bc->dc", pooled_low, d_logits, preferred_element_type=jnp.float32)
    d_pooled = jnp.einsum("bc,dc->bd", d_logits, head, preferred_element_type=jnp.float32)
    d_h, d_gain_end, d_shift_end = pool_pull(d_pooled)
    layer_grads = []
    for n in reversed(range(LAYERS)):
        d_h, grads = layer_backward(d_h, kept[n], layer_sets[n])
        layer_grads = grads + layer_grads
    d_pos = jnp.sum(d_h, 0)
    d_embed = jnp.einsum(
        "bpx,bpd->xd", patches, d_h.astype(jnp.bfloat16), preferred_element_type=jnp.float32
    )
    parts = [d_embed, d_pos, jnp.stack([d_gain_end, d_shift_end]), d_head] + layer_grads
    flat = jnp.concatenate([piece.reshape(-1) for piece in parts])
    return (jnp.pad(flat, (0, whole.shape[0] - flat.shape[0])), values)


def adam_step(master, first, second, grad, number):
    first = BETA_ONE * first + (1.0 - BETA_ONE) * grad
    second = BETA_TWO * second + (1.0 - BETA_TWO) * grad * grad
    fix_one = 1.0 - BETA_ONE**number
    fix_two = 1.0 - BETA_TWO**number
    update = first / fix_one / (jnp.sqrt(second / fix_two) + ADAM_EPS)
    master = master - INNER_RATE * (update + DECAY * master)
    return (master, first, second)


def body(patches, labels, counts, weights, first_moments, second_moments, outer_momentum):
    shard = weights.shape[0]
    per_device = patches.shape[3]
    rank = lax.axis_index("fsdp")
    master = weights
    first = first_moments[0]
    second = second_moments[0]
    lowered = master.astype(jnp.bfloat16)
    total_count = jnp.sum(counts[0, 0]).astype(jnp.float32)
    grad = jnp.zeros((shard,), jnp.float32)
    loss_here = jnp.zeros((), jnp.float32)
    for micro in range(MB):
        whole = lax.all_gather(lowered, "fsdp", axis=0, tiled=True)
        positions = rank * per_device + jnp.arange(per_device, dtype=jnp.int32)
        valid = (positions < counts[0, 0, micro]).astype(jnp.float32)
        flat_grad, values = image_grads(
            whole, patches[0, 0, micro], labels[0, 0, micro], valid / total_count
        )
        loss_here = loss_here + jnp.sum(values * valid)
        grad = grad + lax.psum_scatter(flat_grad, "fsdp", scatter_dimension=0, tiled=True)
    sums = [lax.psum(loss_here, "fsdp")]
    master, first, second = adam_step(master, first, second, grad, STEP)
    averaged = lax.psum(weights - master, "rep") / lax.axis_size("rep")
    momentum = OUTER_MU * outer_momentum + averaged
    new_weights = weights - OUTER_RATE * (averaged + OUTER_MU * momentum)
    return (
        averaged,
        momentum,
        new_weights,
        first[None, :],
        second[None, :],
        jnp.stack(sums)[None, :],
    )


def solution(mesh):
    placed = (
        P("rep", None, None, "fsdp", None, None),
        P("rep", None, None, "fsdp"),
        P("rep", None, None),
        P("fsdp"),
        P("rep", "fsdp"),
        P("rep", "fsdp"),
        P("fsdp"),
    )
    return jax.shard_map(
        body,
        mesh=mesh,
        in_specs=placed,
        out_specs=(
            P("fsdp"),
            P("fsdp"),
            P("fsdp"),
            P("rep", "fsdp"),
            P("rep", "fsdp"),
            P("rep", None),
        ),
        check_vma=False,
    )
```

profile of v0, /device:TPU:0, one launch (start us, length us, event | category | flops | bytes accessed | tf_op | source)
XLA Modules:
  0.0 2414.3 jit_solution(12537335807745265401)
XLA Ops:
  21.6 264.4 %all-gather.3.cloned.1.call-done = bf16[32,1,268544]{2,1,0:T(2,128)(2,1)} async-done(((bf16[1,1,268544]{2,1,0:T(2,128)(2,1)}), bf16[32,1,268544]{2,1,0:T(2,128)(2,1)}) %all-gather.3.cloned.1.call-update) | async-done | bytes 17186832 | tf_op jit(solution)/shard_map/all_gather | solution.py:199
  286.0 339.7 %reduce.98 = bf16[32,268544]{1,0:T(8,128)(2,1)} reduce(bf16[32,1,268544]{2,1,0:T(2,128)(2,1)} %all-gather.3.cloned.1.call-done, bf16[]{:T(256)} %constant.171), dimensions={1}, to_apply=%all-gather.reduce_sub_computation | reduce | bytes 34373632 | tf_op jit(solution)/shard_map/all_gather | solution.py:199
  625.7 42.9 %reshape.1329 = bf16[8593408]{0:T(1024)(128)(2,1)} reshape(bf16[32,268544]{1,0:T(8,128)(2,1)} %reduce.98) | data formatting | bytes 34373632
  742.3 9.3 reshape.1297
  751.6 9.3 multiply_convert_fusion.1
  761.0 9.5 multiply_convert_fusion.3
  906.4 9.5 copy.74
  915.9 11.0 reshape.1325
  947.9 9.5 copy.73
  957.4 11.0 reshape.1309
  971.6 25.2 %dynamic-update-slice.3 = f32[8590848]{0:T(1024)} dynamic-update-slice(f32[8590848]{0:T(1024)} %constant_dynamic-update-slice_fusion.3, f32[768000]{0:T(1024)S(1)} %copy-done.23, s32[]{} %constant.178) | dynamic-update-slice | bytes 6144004
  1001.4 26.6 %dynamic-update-slice.12 = f32[8590848]{0:T(1024)} dynamic-update-slice(f32[8590848]{0:T(1024)} %constant_dynamic-update-slice_fusion.2, f32[768000]{0:T(1024)} %reshape.1304, s32[]{} %constant.178) | dynamic-update-slice | bytes 6144004
  1029.4 60.7 %dynamic-update-slice.5 = f32[8590848]{0:T(1024)} dynamic-update-slice(f32[8590848]{0:T(1024)} %constant_dynamic-update-slice_fusion.1, f32[1769472]{0:T(1024)} %reshape.1322, s32[]{} %constant.180) | dynamic-update-slice | bytes 14155780
  1090.1 60.9 %dynamic-update-slice.14 = f32[8590848]{0:T(1024)} dynamic-update-slice(f32[8590848]{0:T(1024)} %constant_dynamic-update-slice_fusion, f32[1769472]{0:T(1024)} %reshape.1306, s32[]{} %constant.180) | dynamic-update-slice | bytes 14155780
  1151.0 20.2 dynamic-update-slice.6
  1171.2 21.2 dynamic-update-slice.15
  1192.4 80.4 %dynamic-update-slice.7 = f32[8590848]{0:T(1024)} dynamic-update-slice(f32[8590848]{0:T(1024)} %dynamic-update-slice.6, f32[2359296]{0:T(1024)} %bitcast.178, s32[]{} %constant.182) | dynamic-update-slice | bytes 18874372
  1272.8 80.5 %dynamic-update-slice.16 = f32[8590848]{0:T(1024)} dynamic-update-slice(f32[8590848]{0:T(1024)} %dynamic-update-slice.15, f32[2359296]{0:T(1024)} %bitcast.179, s32[]{} %constant.182) | dynamic-update-slice | bytes 18874372
  1353.3 80.2 %dynamic-update-slice.8 = f32[8590848]{0:T(1024)} dynamic-update-slice(f32[8590848]{0:T(1024)} %dynamic-update-slice.7, f32[2359296]{0:T(1024)} %reshape.1325, s32[]{} %constant.183) | dynamic-update-slice | bytes 18874372 | tf_op jit(solution)/shard_map/concatenate | solution.py:173
  1433.5 80.3 %dynamic-update-slice.17 = f32[8590848]{0:T(1024)} dynamic-update-slice(f32[8590848]{0:T(1024)} %dynamic-update-slice.16, f32[2359296]{0:T(1024)} %reshape.1309, s32[]{} %constant.183) | dynamic-update-slice | bytes 18874372 | tf_op jit(solution)/shard_map/concatenate | solution.py:173
  1513.8 34.3 %pad_add_fusion = f32[8593408]{0:T(1024)} fusion(f32[8590848]{0:T(1024)} %dynamic-update-slice.8, f32[8590848]{0:T(1024)} %dynamic-update-slice.17), kind=kLoop, calls=%fused_computation | loop fusion | flops 8593408 | bytes 103100416 | tf_op jit(solution)/shard_map/add | solution.py:206
  1550.1 12.7 multiply_reduce_fusion.4
  1562.8 731.6 %all-reduce.8.cloned.1.call-done = f32[8593408]{0:T(1024)} async-done(((f32[8593408]{0:T(1024)}), f32[8593408]{0:T(1024)}) %all-reduce.8.cloned.1.call-update) | async-done | bytes 34373648
  2299.6 93.4 %psum.15 = f32[1,1]{1,0:T(1,128)} all-reduce(f32[1,1]{1,0:T(1,128)} %bitcast.56), channel_id=1, replica_groups=mesh['rep'=4,'fsdp'=32] {'fsdp'}, use_global_device_ids=true, to_apply=%region_52.53 | all-reduce | flops 1 | bytes 8 | tf_op jit(solution)/shard_map/psum | solution.py:207
  (449 shorter events, 268.8 us)
Async XLA Ops:
  7.2 11.9 copy-start.122
  7.2 12.5 copy-start.50
  7.2 278.8 %all-gather.3.cloned.1.call-start = ((), (), s32[]{:S(2)}) async-start(), calls=%async_computation.1 | async-start | bytes 35447808 | tf_op jit(solution)/shard_map/all_gather | solution.py:199
  15.5 2278.9 %all-reduce.8.cloned.1.call-start = ((), (), s32[]{:S(2)}) async-start(), calls=%async_computation.2 | async-start | bytes 68747264
  700.1 16.2 copy-start.2
  730.3 85.0 %copy-start.75 = (f32[196]{0:T(256)}, f32[196]{0:T(256)S(1)}, u32[]{:S(2)}) copy-start(f32[196]{0:T(256)S(1)} %broadcast_multiply_fusion.9) | copy-start | bytes 2356
  731.1 29.9 %copy-start.92 = (f32[196]{0:T(256)}, f32[196]{0:T(256)S(1)}, u32[]{:S(2)}) copy-start(f32[196]{0:T(256)S(1)} %fusion.40) | copy-start | bytes 2356
  741.2 74.0 %copy-start.79 = (f32[196]{0:T(256)}, f32[196]{0:T(256)S(1)}, u32[]{:S(2)}) copy-start(f32[196]{0:T(256)S(1)} %broadcast_multiply_fusion.6) | copy-start | bytes 2356
  742.2 73.0 %copy-start.95 = (f32[196]{0:T(256)}, f32[196]{0:T(256)S(1)}, u32[]{:S(2)}) copy-start(f32[196]{0:T(256)S(1)} %fusion.43) | copy-start | bytes 2356
  742.3 9.3 copy-start.20
  751.6 18.9 slice-start
  761.0 9.6 copy-start.40
  761.0 9.6 slice-start.1
  773.2 36.3 %copy-start.67 = (f32[196]{0:T(256)}, f32[196]{0:T(256)S(1)}, u32[]{:S(2)}) copy-start(f32[196]{0:T(256)S(1)} %broadcast_multiply_fusion.8) | copy-start | bytes 2356
  773.4 36.0 %copy-start.77 = (f32[196]{0:T(256)}, f32[196]{0:T(256)S(1)}, u32[]{:S(2)}) copy-start(f32[196]{0:T(256)S(1)} %fusion.41) | copy-start | bytes 2356
  773.5 43.6 %copy-start.69 = (f32[196]{0:T(256)}, f32[196]{0:T(256)S(1)}, u32[]{:S(2)}) copy-start(f32[196]{0:T(256)S(1)} %broadcast_multiply_fusion.5) | copy-start | bytes 2356
  773.7 43.4 %copy-start.81 = (f32[196]{0:T(256)}, f32[196]{0:T(256)S(1)}, u32[]{:S(2)}) copy-start(f32[196]{0:T(256)S(1)} %fusion.44) | copy-start | bytes 2356
  800.6 16.5 copy-start.90
  802.0 15.1 copy-start.108
  915.9 11.0 copy-start.34
  957.4 14.2 copy-start.23
  1090.1 60.9 %copy-start.33 = (f32[589824]{0:T(1024)S(1)}, f32[589824]{0:T(1024)}, u32[]{:S(2)}) copy-start(f32[589824]{0:T(1024)} %reshape.1323) | copy-start | bytes 7077892
  1548.2 746.2 %copy-start.30 = (f32[268544]{0:T(1024)S(1)}, f32[268544]{0:T(1024)}, u32[]{:S(2)}) copy-start(f32[268544]{0:T(1024)} %param.10) | copy-start | bytes 3222532
  1548.2 856.2 %all-reduce.6.cloned.1.call-start = ((), (), s32[]{:S(2)}) async-start(), calls=%async_computation | async-start | bytes 2154496 | tf_op jit(solution)/shard_map/psum | solution.py:209
  (112 other events, 363.3 us)
Sparse Core Ops, SparseCore 0:
  15.6 270.3 all-gather.2
  1548.3 746.0 all-reduce.7
  2298.4 38.3 all-reduce.5
where the time goes:
time: 2460 us; the launch traced here: 2410 us
  waiting for transfers between devices  996 us (40%)
  local copies, waits for them, and re-layouts  768 us (31%)
  other arithmetic  422 us (17%)
  matrix products  114 us (5%)
  blocking collectives  93.4 us (4%)
    unnamed x4, waiting for transfers between devices  732 us
    unnamed x287, local copies, waits for them, and re-layouts  469 us
    all_gather x1, other arithmetic, body(): whole = lax.all_gather(lowered, 'fsdp', axis=0, tiled=True)  340 us
    all_gather x1, waiting for transfers between devices, body(): whole = lax.all_gather(lowered, 'fsdp', axis=0, tiled=True)  264 us
    concatenate x2, local copies, waits for them, and re-layouts, image_grads(): flat = jnp.concatenate([piece.reshape(-1) for piece in parts])  160 us
    psum x1, blocking collectives, body(): sums = [lax.psum(loss_here, 'fsdp')]  93.4 us
    reshape x16, local copies, waits for them, and re-layouts, image_grads(): flat = jnp.concatenate([piece.reshape(-1) for piece in parts])  57.9 us
  transfers between devices with their start and end apart: 3, of which 2 were waited for; matrix products, arithmetic and copies ran while one was open for 1% of the time, Pallas kernels for 0%

commit v1 on v0

v1 whole, which is shorter than its diff:
```python
from functools import partial

import jax
import jax.numpy as jnp
from jax import lax
from jax.experimental import pallas as pl
from jax.experimental.pallas import tpu as pltpu
from jax.sharding import PartitionSpec as P

SHARD = 2098
SLOT = 132
HALF = 66
QUART = 33
NSLOT = 32
SECTIONS = []
_t = 0
for _base, _c, _g, _rpg in ((0, 6, 61, 96), (5796, 8, 48, 125), (11796, 6, 1, 96), (11820, 18, 48, 288), (25644, 6, 48, 96), (30252, 24, 48, 384), (48684, 6, 192, 96)):
    SECTIONS.append((_base, _c, _g, _rpg, _t))
    _t += _c * _g
NTILE = _t
HI = 352
LO = 224
MARGIN = 512
FROWS = 3072
HEAD_ROWS = 16
MESH = pl.DeviceIdType.MESH


def coords():
    rep = lax.axis_index("rep")
    fs = lax.axis_index("fsdp")
    return lax.div(rep, 2), lax.rem(rep, 2), lax.div(fs, 8), lax.rem(lax.div(fs, 4), 2), lax.rem(fs, 4)


def device(xl, xh, core, z, y):
    return {"rep": xl * 2 + core, "fsdp": z * 8 + xh * 4 + y}


def gather_kernel(w_ref, patch_ref, meta_ref, t_out, patch_out, meta_out, flat, headrows, mainb, lob, hib, rmain, rlo, rhi, slot, local_sem, x_send, x_recv, g_send, g_recv):
    xl, b, z, a, y = coords()
    fs = z * 8 + a * 4 + y
    swap = a != b
    xo = lax.rem(xl + a + b, 2)
    up = lax.rem(fs + 1, NSLOT)
    down = lax.rem(fs + NSLOT - 1, NSLOT)

    def halo_to(s):
        return device(xo, b, lax.rem(lax.div(s, 4), 2), lax.div(s, 8), lax.rem(s, 4))

    def halo_from(s):
        sa = lax.rem(lax.div(s, 4), 2)
        return device(lax.rem(xl + sa + a, 2), sa, a, lax.div(s, 8), lax.rem(s, 4))

    partner = device(xo, b, a, z, y)
    mirror = device(xl, b, a, z, y)
    sibling = device(xl, a, 1 - b, z, y)

    def at_y(k):
        return device(xl, a, b, z, lax.rem(y + k, 4))

    def at_z(k):
        return device(xl, a, b, lax.rem(z + k, 4), y)

    load = pltpu.make_async_copy(w_ref, flat.at[pl.ds(MARGIN, SHARD)], local_sem.at[0])
    load.start()

    barrier = pltpu.get_barrier_semaphore()

    def greet(target):
        pl.semaphore_signal(barrier, inc=1, device_id=target, device_id_type=MESH)

    v = z * 8 + b * 4 + y
    for target in (halo_from(lax.rem(v + 1, NSLOT)), halo_from(lax.rem(v + NSLOT - 1, NSLOT)), at_y(1), at_y(3), at_z(1), at_z(3), sibling):
        greet(target)

    @pl.when(swap)
    def _():
        greet(partner)
        greet(mirror)

    def remote(src, dst, send, recv, k, target):
        return pltpu.make_async_remote_copy(src_ref=src, dst_ref=dst, send_sem=send.at[k], recv_sem=recv.at[k], device_id=target, device_id_type=MESH)

    pl.semaphore_wait(barrier, jnp.where(swap, 9, 7))

    load.wait()
    main = remote(mainb, rmain, x_send, x_recv, 0, partner)

    @pl.when(swap)
    def _():
        mainb[pl.ds(0, SHARD), :] = flat[pl.ds(MARGIN, SHARD), :].astype(jnp.bfloat16)
        main.start()

    hib[...] = flat[pl.ds(MARGIN + SHARD - HI, HI), :].astype(jnp.bfloat16)
    to_up = remote(hib, rlo, x_send, x_recv, 1, halo_to(up))
    to_up.start()
    lob[...] = flat[pl.ds(MARGIN, LO), :].astype(jnp.bfloat16)
    to_down = remote(lob, rhi, x_send, x_recv, 2, halo_to(down))
    to_down.start()

    patch_swap = remote(patch_ref, patch_out, x_send, x_recv, 3, mirror)
    meta_swap = remote(meta_ref, meta_out, x_send, x_recv, 4, mirror)
    patch_keep = pltpu.make_async_copy(patch_ref, patch_out, local_sem.at[1])
    meta_keep = pltpu.make_async_copy(meta_ref, meta_out, local_sem.at[2])

    @pl.when(swap)
    def _():
        patch_swap.start()
        meta_swap.start()
        main.wait_recv()
        flat[pl.ds(MARGIN, SHARD), :] = rmain[pl.ds(0, SHARD), :].astype(jnp.float32)

    @pl.when(jnp.logical_not(swap))
    def _():
        patch_keep.start()
        meta_keep.start()

    to_up.wait_recv()
    flat[pl.ds(MARGIN - HI, HI), :] = rlo[...].astype(jnp.float32)
    to_down.wait_recv()
    flat[pl.ds(MARGIN + SHARD, LO), :] = rhi[...].astype(jnp.float32)

    first = SLOT * v
    origin = SHARD * v - MARGIN
    for index, (base, c, groups, per, start) in enumerate(SECTIONS):
        lo = jnp.maximum(first, start)
        hi = jnp.minimum(first + SLOT, start + c * groups)
        if index == 1:
            lane = lax.broadcasted_iota(jnp.int32, (8, 128), 1)
            g0 = lax.div(jnp.maximum(lo, start) - start, 8)
            g1 = lax.div(jnp.maximum(hi, start) - start + 7, 8)

            def head_group(g, carry):
                row = base + per * g - origin
                for i in range(16):
                    q, s = divmod(1000 * i, 128)
                    one = flat[pl.ds(row + q, 8), :]
                    if s:
                        two = flat[pl.ds(row + q + 1, 8), :]
                        one = jnp.where(lane < 128 - s, pltpu.roll(one, 128 - s, 1), pltpu.roll(two, 128 - s, 1))
                    headrows[pl.ds(i * 8, 8), :] = one
                for j in range(8):
                    t = start + g * 8 + j - first

                    @pl.when(jnp.logical_and(t >= 0, t < SLOT))
                    def _():
                        slot[t] = headrows[pl.ds(j, 16, stride=8), :].astype(jnp.bfloat16)
                return carry

            lax.fori_loop(g0, g1, head_group, 0)
        else:

            def tile(t, carry):
                g = lax.div(t - start, c)
                j = lax.rem(t - start, c)
                row = base + 16 * c * g + j - origin
                slot[t - first] = flat[pl.ds(row, 16, stride=c), :].astype(jnp.bfloat16)
                return carry

            lax.fori_loop(lo, hi, tile, 0)
    pads = jnp.maximum(NTILE - first, 0)

    def blank(t, carry):
        slot[t] = jnp.zeros((16, 128), jnp.bfloat16)
        return carry

    lax.fori_loop(jnp.minimum(pads, SLOT), SLOT, blank, 0)

    def place(axis, k):
        return z * 8 + b * 4 + lax.rem(y + k, 4) if axis == 0 else (lax.rem(z + k, 4)) * 8 + b * 4 + y

    def place2(axis, k, j):
        if axis == 0:
            return (lax.rem(z + j, 4)) * 8 + b * 4 + lax.rem(y + k, 4)
        return (lax.rem(z + k, 4)) * 8 + b * 4 + lax.rem(y + j, 4)

    move = (at_y, at_z)
    keep = pltpu.make_async_copy(slot, t_out.at[v], local_sem.at[3])
    keep.start()
    sends = []
    GS = g_send
    GR = g_recv

    def gsend(k, src, dst, target):
        copy = remote(src, dst, GS, GR, k, target)
        copy.start()
        sends.append(copy)
        return copy

    def arrived(k, dst):
        remote(dst, dst, GS, GR, k, sibling).wait_recv()

    def part(slot_id, lo, n):
        return t_out.at[slot_id, pl.ds(lo, n)]

    def p1(h, k):
        return h * 20 + k

    def p2(h, m, k):
        return h * 20 + 4 + m * 4 + k

    def dd(h, j):
        return 40 + h * 16 + j

    own = lambda lo, n: slot.at[pl.ds(lo, n)]
    for h in range(2):
        A, B = h, 1 - h
        gsend(p1(h, 0), own(HALF * h, HALF), part(v, HALF * h, HALF), move[A](1))
        gsend(p1(h, 1), own(HALF * h, HALF), part(v, HALF * h, HALF), move[A](3))
    for h in range(2):
        A, B = h, 1 - h
        gsend(p2(h, 0, 0), own(HALF * h, HALF), part(v, HALF * h, HALF), move[B](1))
        gsend(p2(h, 0, 1), own(HALF * h, HALF), part(v, HALF * h, HALF), move[B](3))
        gsend(dd(h, 0), own(HALF * h, HALF), part(v, HALF * h, HALF), sibling)
    order = (0, 3, 1, 2)

    def spread(h, m):
        A, B = h, 1 - h
        s = place2(A, order[m], 0)
        gsend(p2(h, m, 0), part(s, HALF * h, HALF), part(s, HALF * h, HALF), move[B](1))
        gsend(p2(h, m, 1), part(s, HALF * h, HALF), part(s, HALF * h, HALF), move[B](3))
        gsend(dd(h, m), part(s, HALF * h, HALF), part(s, HALF * h, HALF), sibling)

    for h in range(2):
        A, B = h, 1 - h
        s = place2(A, 3, 0)
        arrived(p1(h, 0), part(s, HALF * h, HALF))
        gsend(p1(h, 2), part(s, HALF * h, QUART), part(s, HALF * h, QUART), move[A](1))
        s = place2(A, 1, 0)
        arrived(p1(h, 1), part(s, HALF * h, HALF))
        gsend(p1(h, 3), part(s, HALF * h + QUART, QUART), part(s, HALF * h + QUART, QUART), move[A](3))
        spread(h, 1)
        spread(h, 2)
    for h in range(2):
        A, B = h, 1 - h
        s = place2(A, 2, 0)
        arrived(p1(h, 2), part(s, HALF * h, QUART))
        arrived(p1(h, 3), part(s, HALF * h + QUART, QUART))
        spread(h, 3)
    for m in range(4):
        for h in range(2):
            A, B = h, 1 - h
            s = place2(A, order[m], 3)
            arrived(p2(h, m, 0), part(s, HALF * h, HALF))
            gsend(p2(h, m, 2), part(s, HALF * h, QUART), part(s, HALF * h, QUART), move[B](1))
            gsend(dd(h, 4 + m * 3), part(s, HALF * h, HALF), part(s, HALF * h, HALF), sibling)
            s = place2(A, order[m], 1)
            arrived(p2(h, m, 1), part(s, HALF * h, HALF))
            gsend(p2(h, m, 3), part(s, HALF * h + QUART, QUART), part(s, HALF * h + QUART, QUART), move[B](3))
            gsend(dd(h, 5 + m * 3), part(s, HALF * h, HALF), part(s, HALF * h, HALF), sibling)
    for m in range(4):
        for h in range(2):
            A, B = h, 1 - h
            s = place2(A, order[m], 2)
            arrived(p2(h, m, 2), part(s, HALF * h, QUART))
            arrived(p2(h, m, 3), part(s, HALF * h + QUART, QUART))
            gsend(dd(h, 6 + m * 3), part(s, HALF * h, HALF), part(s, HALF * h, HALF), sibling)
    for j in range(16):
        for h in range(2):
            arrived(dd(h, j), part(0, HALF * h, HALF))
    for copy in sends:
        copy.wait_send()
    keep.wait()
    to_up.wait_send()
    to_down.wait_send()

    @pl.when(swap)
    def _():
        main.wait_send()
        patch_swap.wait()
        meta_swap.wait()

    @pl.when(jnp.logical_not(swap))
    def _():
        patch_keep.wait()
        meta_keep.wait()


def gather(weights, patches, meta):
    hbm = pl.BlockSpec(memory_space=pl.ANY)
    return pl.pallas_call(
        gather_kernel,
        out_shape=(
            jax.ShapeDtypeStruct((NSLOT, SLOT, 16, 128), jnp.bfloat16),
            jax.ShapeDtypeStruct(patches.shape, patches.dtype),
            jax.ShapeDtypeStruct(meta.shape, meta.dtype),
        ),
        in_specs=[hbm] * 3,
        out_specs=(hbm,) * 3,
        scratch_shapes=[
            pltpu.VMEM((FROWS, 128), jnp.float32),
            pltpu.VMEM((128, 128), jnp.float32),
            pltpu.VMEM((2112, 128), jnp.bfloat16),
            pltpu.VMEM((LO, 128), jnp.bfloat16),
            pltpu.VMEM((HI, 128), jnp.bfloat16),
            pltpu.VMEM((2112, 128), jnp.bfloat16),
            pltpu.VMEM((HI, 128), jnp.bfloat16),
            pltpu.VMEM((LO, 128), jnp.bfloat16),
            pltpu.VMEM((SLOT, 16, 128), jnp.bfloat16),
            pltpu.SemaphoreType.DMA((4,)),
            pltpu.SemaphoreType.DMA((5,)),
            pltpu.SemaphoreType.DMA((5,)),
            pltpu.SemaphoreType.DMA((72,)),
            pltpu.SemaphoreType.DMA((72,)),
        ],
        compiler_params=pltpu.CompilerParams(collective_id=0, has_side_effects=True, vmem_limit_bytes=32 * 1024 * 1024),
        name="gather_weights",
    )(weights, patches, meta)


D = 768
HEADS = 12
HEAD_DIM = 64
FF = 3072
CLS = 1000
P_SIZE = 196
ROWS = 208
TOK = 2 * ROWS
NORM_EPS = 1e-06
SMOOTHING = 0.1
NTILES = 4224
T_E, T_HEAD, T_NORM, T_QKV, T_OUT, T_IN, T_FO = 0, 366, 750, 756, 1620, 1908, 3060
T_POS = 288
BLK = 256
STEP_ROWS = 32
F32 = jnp.float32
BF16 = jnp.bfloat16
ROOT_HALF = 0.7071067811865476
INV_ROOT_TWO_PI = 0.3989422804014327


def dot(x, w):
    return lax.dot_general(x, w, (((1,), (0,)), ((), ())), preferred_element_type=F32)


def dot_t(x, w):
    return lax.dot_general(x, w, (((1,), (1,)), ((), ())), preferred_element_type=F32)


def t_dot(x, w):
    return lax.dot_general(x, w, (((0,), (0,)), ((), ())), preferred_element_type=F32)


def stats(x):
    mean = jnp.sum(x, -1, keepdims=True) * (1.0 / D)
    centred = x - mean
    var = jnp.sum(centred * centred, -1, keepdims=True) * (1.0 / D)
    rstd = lax.rsqrt(var + NORM_EPS)
    return centred * rstd, rstd


def norm_back(d_hat, hat, rstd):
    m1 = jnp.sum(d_hat, -1, keepdims=True) * (1.0 / D)
    m2 = jnp.sum(d_hat * hat, -1, keepdims=True) * (1.0 / D)
    return rstd * (d_hat - m1 - hat * m2)


def compute_kernel(t_hbm, patch_ref, meta_ref, g_hbm, loss_ref, T, G, x, xt, h, a, at, mix, prob, o, h1, a2, hid, slope, h2, dh, dyb, du, dmix, sem, gsem):
    bounds = [(0, T_HEAD), (T_QKV, T_OUT), (T_NORM, T_QKV), (T_OUT, T_IN), (T_IN, T_FO), (T_FO, 4212), (T_HEAD, T_NORM)]
    loads = []
    for i, (lo, hi) in enumerate(bounds):
        copy = pltpu.make_async_copy(t_hbm.at[pl.ds(lo, hi - lo)], T.at[pl.ds(lo, hi - lo)], sem.at[i])
        copy.start()
        loads.append(copy)

    def section(ref, start, c, groups):
        return ref.at[pl.ds(start, groups * c)].reshape(groups, c, 16, 128)

    def cols(start, c, groups, j):
        part = section(T, start, c, groups)
        return jnp.concatenate([part[:, 2 * j + k].reshape(groups * 16, 128) for k in range(2)], axis=1)

    def put_cols(start, c, groups, j, value):
        low = value.astype(BF16)
        part = section(G, start, c, groups)
        for k in range(2):
            part[:, 2 * j + k] = low[:, k * 128 : (k + 1) * 128].reshape(groups, 16, 128)

    def row_of(start, k):
        return jnp.concatenate([T[start + j][k : k + 1, :] for j in range(6)], axis=1).astype(F32)

    def lanes(j):
        return pl.ds(pl.multiple_of(j * BLK, BLK), BLK)

    def rows(i):
        return pl.ds(pl.multiple_of(i * STEP_ROWS, STEP_ROWS), STEP_ROWS)

    steps = TOK // STEP_ROWS
    for i in range(2):
        x[pl.ds(i * ROWS, 192), :] = patch_ref[i, pl.ds(0, 192), :]
        x[pl.ds(i * ROWS + 192, 16), :] = jnp.concatenate([patch_ref[i, pl.ds(192, 4), :], jnp.zeros((12, D), BF16)], axis=0)

    real = lax.broadcasted_iota(jnp.int32, (ROWS, 128), 0) < P_SIZE
    loads[0].wait()
    for j in range(3):
        acc = dot(x[...], cols(T_E, 6, 48, j))
        p = cols(T_POS, 6, 13, j).astype(F32)
        p = jnp.where(lax.broadcasted_iota(jnp.int32, (ROWS, BLK), 0) < P_SIZE, p, 0.0)
        for i in range(2):
            h[pl.ds(i * ROWS, ROWS), pl.ds(j * BLK, BLK)] = acc[i * ROWS : (i + 1) * ROWS] + p

    loads[2].wait()
    gain1, shift1, gain2, shift2 = (row_of(T_NORM, k) for k in range(4))

    def norm_one(i, carry):
        hat, unused = stats(h[rows(i), :])
        a[rows(i), :] = (hat * gain1 + shift1).astype(BF16)
        return carry

    lax.fori_loop(0, steps, norm_one, 0)
    loads[1].wait()

    def mix_block(j, carry):
        mix[:, lanes(j)] = dot(a[...], cols(T_QKV, 18, 48, j)).astype(BF16)
        return carry

    lax.fori_loop(0, 9, mix_block, 0)

    first_half = lax.broadcasted_iota(jnp.int32, (ROWS, 128), 1) < HEAD_DIM
    key_ok = lax.broadcasted_iota(jnp.int32, (ROWS, ROWS), 1) < P_SIZE
    zero = jnp.zeros((ROWS, 128), BF16)

    def qkv_of(n):
        i = lax.div(n, 6)
        p = lax.rem(n, 6)
        r = pl.ds(pl.multiple_of(i * ROWS, ROWS), ROWS)
        ls = [pl.ds(pl.multiple_of(p * 128 + D * k, 128), 128) for k in range(3)]
        return r, ls

    def attend(n, carry):
        r, ls = qkv_of(n)
        q, k, v = (mix[r, l] for l in ls)
        q = q * jnp.asarray(0.125, BF16)
        outs = []
        for e in range(2):
            mask = first_half if e == 0 else jnp.logical_not(first_half)
            s = dot_t(jnp.where(mask, q, zero), k)
            s = jnp.where(key_ok, s, -jnp.inf)
            top = jnp.max(s, -1, keepdims=True)
            ex = jnp.exp(s - top)
            pr = (ex / jnp.sum(ex, -1, keepdims=True)).astype(BF16)
            prob[n * 2 + e] = pr
            outs.append(dot(pr, v))
        o[r, ls[0]] = jnp.where(first_half, outs[0], outs[1]).astype(BF16)
        return carry

    lax.fori_loop(0, 12, attend, 0)
    loads[3].wait()
    for j in range(3):
        h1[:, pl.ds(j * BLK, BLK)] = h[:, pl.ds(j * BLK, BLK)] + dot(o[...], cols(T_OUT, 6, 48, j))

    def norm_two(i, carry):
        hat, unused = stats(h1[rows(i), :])
        a2[rows(i), :] = (hat * gain2 + shift2).astype(BF16)
        return carry

    lax.fori_loop(0, steps, norm_two, 0)
    loads[4].wait()

    def up_block(j, carry):
        u = dot(a2[...], cols(T_IN, 24, 48, j))
        phi = 0.5 * (1.0 + lax.erf(u * ROOT_HALF))
        pdf = jnp.exp(-0.5 * u * u) * INV_ROOT_TWO_PI
        hid[:, lanes(j)] = (u * phi).astype(BF16)
        slope[:, lanes(j)] = (phi + u * pdf).astype(BF16)
        return carry

    lax.fori_loop(0, 12, up_block, 0)
    loads[5].wait()
    for j in range(3):
        h2[:, pl.ds(j * BLK, BLK)] = h1[:, pl.ds(j * BLK, BLK)] + dot(hid[...], cols(T_FO, 6, 192, j))

    gain_end, shift_end = (row_of(T_POS + 72, 4 + k) for k in range(2))
    means = []
    for i in range(2):

        def pool_step(n, carry):
            hat, unused = stats(h2[pl.ds(pl.multiple_of(i * ROWS + n * 16, 16), 16), :])
            ok = lax.broadcasted_iota(jnp.int32, (16, D), 0) + n * 16 < P_SIZE
            hat = jnp.where(ok, hat, 0.0)
            return carry + hat[:8] + hat[8:]

        total = lax.fori_loop(0, 13, pool_step, jnp.zeros((8, D), F32))
        means.append(jnp.sum(total, 0, keepdims=True) * (1.0 / P_SIZE))
    mean_hat = jnp.concatenate(means + [jnp.zeros((14, D), F32)], axis=0)
    two = lax.broadcasted_iota(jnp.int32, (16, D), 0) < 2
    pooled = jnp.where(two, mean_hat * gain_end + shift_end, 0.0).astype(BF16)
    loads[6].wait()
    logits = jnp.concatenate([dot(pooled, cols(T_HEAD, 8, 48, j)) for j in range(4)], axis=1)
    lane = lax.broadcasted_iota(jnp.int32, (16, 1024), 1)
    lane_f = lane.astype(F32)
    inside = lane < CLS
    logits = jnp.where(inside, logits, -1e30)
    top = jnp.max(logits, -1, keepdims=True)
    total = jnp.sum(jnp.where(inside, jnp.exp(logits - top), 0.0), -1, keepdims=True)
    logp = logits - top - jnp.log(total)
    meta = meta_ref[...]
    pad14 = jnp.zeros((14, 1), F32)
    label = jnp.concatenate([meta[0:2, 0:1], pad14], axis=0)
    scale = jnp.concatenate([meta[2:4, 0:1], pad14], axis=0)
    valid = jnp.concatenate([meta[4:6, 0:1], pad14], axis=0)
    target = jnp.where(lane_f == label, 1.0 - SMOOTHING, 0.0) + SMOOTHING / CLS
    values = -jnp.sum(jnp.where(inside, target * logp, 0.0), -1, keepdims=True)
    loss_ref[...] = jnp.broadcast_to(jnp.sum(values * valid, 0, keepdims=True), (8, 128))
    d_logits = jnp.where(inside, scale * (jnp.exp(logp) - target), 0.0).astype(BF16)
    d_pooled = jnp.zeros((16, D), F32)
    for j in range(4):
        w = cols(T_HEAD, 8, 48, j)
        d_pooled = d_pooled + dot_t(d_logits[:, j * BLK : (j + 1) * BLK], w)
        put_cols(T_HEAD, 8, 48, j, t_dot(pooled, d_logits[:, j * BLK : (j + 1) * BLK]))
    d_gain_end = jnp.sum(d_pooled * mean_hat, 0, keepdims=True)
    d_shift_end = jnp.sum(d_pooled, 0, keepdims=True)
    for i in range(2):
        d_hat = d_pooled[i : i + 1, :] * (1.0 / P_SIZE) * gain_end

        def end_step(n, carry):
            r = pl.ds(pl.multiple_of(i * ROWS + n * 16, 16), 16)
            hat, rstd = stats(h2[r, :])
            ok = lax.broadcasted_iota(jnp.int32, (16, D), 0) + n * 16 < P_SIZE
            d = jnp.where(ok, norm_back(jnp.broadcast_to(d_hat, (16, D)), hat, rstd), 0.0)
            dh[r, :] = d
            dyb[r, :] = d.astype(BF16)
            return carry

        lax.fori_loop(0, 13, end_step, 0)

    at[...] = a2[...].T
    da = h2
    da[...] = jnp.zeros((TOK, D), F32)

    def mlp_block(j, carry):
        dy = dyb[...]
        d_w = t_dot(hid[:, lanes(j)], dy).astype(BF16)
        part = section(G, T_FO + j * 96, 6, 16)
        for k in range(6):
            part[:, k] = d_w[:, k * 128 : (k + 1) * 128].reshape(16, 16, 128)
        part = section(T, T_FO + j * 96, 6, 16)
        w = jnp.concatenate([part[:, k].reshape(BLK, 128) for k in range(6)], axis=1)
        d_u = (dot_t(dy, w) * slope[:, lanes(j)].astype(F32)).astype(BF16)
        put_cols(T_IN, 24, 48, j, dot(at[...], d_u))
        da[...] += dot_t(d_u, cols(T_IN, 24, 48, j))
        return carry

    lax.fori_loop(0, 12, mlp_block, 0)

    def back_two(i, carry):
        dg, ds = carry
        hat, rstd = stats(h1[rows(i), :])
        d = da[rows(i), :]
        new = dh[rows(i), :] + norm_back(d * gain2, hat, rstd)
        dh[rows(i), :] = new
        dyb[rows(i), :] = new.astype(BF16)
        return dg + jnp.sum((d * hat).reshape(4, 8, D), 0), ds + jnp.sum(d.reshape(4, 8, D), 0)

    none = jnp.zeros((8, D), F32)
    d_gain2, d_shift2 = lax.fori_loop(0, steps, back_two, (none, none))

    at[...] = o[...].T
    da[...] = jnp.zeros((TOK, D), F32)
    for j in range(3):
        dz = dyb[:, pl.ds(j * BLK, BLK)]
        put_cols(T_OUT, 6, 48, j, dot(at[...], dz))
        da[...] += dot_t(dz, cols(T_OUT, 6, 48, j))
    o[...] = da[...].astype(BF16)

    def attend_back(n, carry):
        r, ls = qkv_of(n)
        q, k, v = (mix[r, l] for l in ls)
        q = q * jnp.asarray(0.125, BF16)
        k8 = k * jnp.asarray(0.125, BF16)
        do = o[r, ls[0]]
        dq, dk, dv = [], [], []
        for e in range(2):
            mask = first_half if e == 0 else jnp.logical_not(first_half)
            pr = prob[n * 2 + e]
            dv.append(t_dot(pr, do))
            dp = dot_t(jnp.where(mask, do, zero), v)
            prf = pr.astype(F32)
            row = jnp.sum(prf * dp, -1, keepdims=True)
            ds = (prf * (dp - row)).astype(BF16)
            dq.append(dot(ds, k8))
            dk.append(t_dot(ds, q))
        for l, pair in zip(ls, (dq, dk, dv)):
            dmix[r, l] = jnp.where(first_half, pair[0], pair[1]).astype(BF16)
        return carry

    lax.fori_loop(0, 12, attend_back, 0)

    at[...] = a[...].T
    da[...] = jnp.zeros((TOK, D), F32)

    def qkv_block(j, carry):
        d = dmix[:, lanes(j)]
        put_cols(T_QKV, 18, 48, j, dot(at[...], d))
        da[...] += dot_t(d, cols(T_QKV, 18, 48, j))
        return carry

    lax.fori_loop(0, 9, qkv_block, 0)

    def back_one(i, carry):
        dg, ds = carry
        hat, rstd = stats(h[rows(i), :])
        d = da[rows(i), :]
        new = dh[rows(i), :] + norm_back(d * gain1, hat, rstd)
        dh[rows(i), :] = new
        dyb[rows(i), :] = new.astype(BF16)
        return dg + jnp.sum((d * hat).reshape(4, 8, D), 0), ds + jnp.sum(d.reshape(4, 8, D), 0)

    d_gain1, d_shift1 = lax.fori_loop(0, steps, back_one, (none, none))
    d_norms = jnp.concatenate([jnp.sum(d, 0, keepdims=True) for d in (d_gain1, d_shift1, d_gain2, d_shift2)] + [jnp.zeros((12, D), F32)], axis=0).astype(BF16)
    for j in range(6):
        G[T_NORM + j] = d_norms[:, j * 128 : (j + 1) * 128]
    at[...] = x[...].T
    row_id = lax.broadcasted_iota(jnp.int32, (ROWS, BLK), 0)
    for j in range(3):
        put_cols(T_E, 6, 48, j, dot(at[...], dyb[:, pl.ds(j * BLK, BLK)]))
        c = pl.ds(j * BLK, BLK)
        s = slice(j * BLK, (j + 1) * BLK)
        d_pos = dh[pl.ds(0, ROWS), c] + dh[pl.ds(ROWS, ROWS), c]
        d_pos = jnp.where(row_id < P_SIZE, d_pos, 0.0)
        d_pos = jnp.where(row_id == P_SIZE, jnp.broadcast_to(d_gain_end[:, s], (ROWS, BLK)), d_pos)
        d_pos = jnp.where(row_id == P_SIZE + 1, jnp.broadcast_to(d_shift_end[:, s], (ROWS, BLK)), d_pos)
        put_cols(T_POS, 6, 13, j, d_pos)
    G[pl.ds(4212, 12)] = jnp.zeros((12, 16, 128), BF16)
    out = pltpu.make_async_copy(G, g_hbm, gsem)
    out.start()
    out.wait()


def compute(tiles, patches, meta):
    hbm = pl.BlockSpec(memory_space=pl.ANY)
    vmem = pl.BlockSpec(memory_space=pltpu.VMEM)
    V = pltpu.VMEM
    return pl.pallas_call(
        compute_kernel,
        out_shape=(jax.ShapeDtypeStruct((NTILES, 16, 128), BF16), jax.ShapeDtypeStruct((8, 128), F32)),
        in_specs=[hbm, vmem, vmem],
        out_specs=(hbm, vmem),
        scratch_shapes=[
            V((NTILES, 16, 128), BF16),
            V((NTILES, 16, 128), BF16),
            V((TOK, D), BF16),
            V((8, 128), BF16),
            V((TOK, D), F32),
            V((TOK, D), BF16),
            V((D, TOK), BF16),
            V((TOK, 3 * D), BF16),
            V((24, ROWS, ROWS), BF16),
            V((TOK, D), BF16),
            V((TOK, D), F32),
            V((TOK, D), BF16),
            V((TOK, FF), BF16),
            V((TOK, FF), BF16),
            V((TOK, D), F32),
            V((TOK, D), F32),
            V((TOK, D), BF16),
            V((8, 128), BF16),
            V((TOK, 3 * D), BF16),
            pltpu.SemaphoreType.DMA((8,)),
            pltpu.SemaphoreType.DMA,
        ],
        compiler_params=pltpu.CompilerParams(vmem_limit_bytes=62 * 1024 * 1024),
        name="grads",
    )(tiles, patches, meta)


EDGE = 24
FRONT = 768
BACK_ROWS = FRONT + SHARD + 640 + 6
PADDED = 2112
STEP = 10
BETA_ONE = 0.9
BETA_TWO = 0.95
ADAM_EPS = 1e-08
DECAY = 0.05
INNER_RATE = 0.01
OUTER_RATE = 0.7
OUTER_MU = 0.9
F32 = jnp.float32
BF16 = jnp.bfloat16
ORDER = (2, 1, 3, 0)


def reduce_kernel(
    g_ref, w_ref, first_ref, second_ref, mom_ref,
    avg_out, mom_out, new_out, first_out, second_out,
    L, R, RA, RB, window, flat, headrows, w, first, second, mom, upd, low, low2, pair, pair2, total, total2,
    load_sem, d_send, d_recv, a_send, a_recv, b_send, b_recv, x_send, x_recv,
):
    xl, b, z, a, y = coords()
    fs = z * 8 + a * 4 + y
    v = z * 8 + b * 4 + y
    swap = a != b

    def owner(s):
        return device(xl, lax.rem(lax.div(s, 4), 2), a, lax.div(s, 8), lax.rem(s, 4))

    def server(s):
        return device(xl, b, lax.rem(lax.div(s, 4), 2), lax.div(s, 8), lax.rem(s, 4))

    def around(s):
        return lax.rem(s + NSLOT, NSLOT)

    mirror = device(xl, b, a, z, y)
    sibling = device(xl, a, 1 - b, z, y)
    across = device(1 - xl, a, b, z, y)

    def at_z(k):
        return device(xl, a, b, lax.rem(z + k, 4), y)

    def at_y(k):
        return device(xl, a, b, z, lax.rem(y + k, 4))

    barrier = pltpu.get_barrier_semaphore()
    for target in (sibling, across, at_y(1), at_y(3), at_z(1), at_z(3), server(around(fs + 1)), server(around(fs - 1))):
        pl.semaphore_signal(barrier, inc=1, device_id=target, device_id_type=MESH)

    @pl.when(swap)
    def _():
        pl.semaphore_signal(barrier, inc=1, device_id=mirror, device_id_type=MESH)

    own = []
    for kz in range(4):
        for ky in range(4):
            s = lax.rem(z + ORDER[kz], 4) * 8 + b * 4 + lax.rem(y + ORDER[ky], 4)
            own.append(pltpu.make_async_copy(g_ref.at[s], L.at[kz, ky], load_sem.at[kz * 4 + ky]))
    extra = [pltpu.make_async_copy(src, dst, load_sem.at[16 + i]) for i, (src, dst) in enumerate(((w_ref, w), (first_ref, first), (second_ref, second), (mom_ref, mom)))]

    pl.semaphore_wait(barrier, jnp.where(swap, 9, 8))

    def remote(src, dst, send, recv, k, target):
        return pltpu.make_async_remote_copy(src_ref=src, dst_ref=dst, send_sem=send.at[k], recv_sem=recv.at[k], device_id=target, device_id_type=MESH)

    sends = []

    def go(*args):
        copy = remote(*args)
        copy.start()
        sends.append(copy)
        return copy

    sequence = [(0, 0), (0, 1), (1, 0), (0, 2), (0, 3), (2, 0), (3, 0), (1, 2), (1, 3), (2, 1), (3, 1), (1, 1), (2, 2), (2, 3), (3, 2), (3, 3)]
    for kz, ky in sequence:
        s = lax.rem(z + ORDER[kz], 4) * 8 + (1 - b) * 4 + lax.rem(y + ORDER[ky], 4)
        go(g_ref.at[s], R.at[kz, ky], d_send, d_recv, kz * 4 + ky, sibling)
        own[kz * 4 + ky].start()
    for copy in extra:
        copy.start()

    def add_into(dst, src, n):
        def one(i, carry):
            for k in range(3):
                t = i * 3 + k
                dst[t] = dst[t] + src[t]
            return carry

        lax.fori_loop(0, n // 3, one, 0)

    def arrive(dst, recv, k):
        remote(dst, dst, d_send, recv, k, sibling).wait_recv()

    done = set()

    def need(*slots):
        for kz, ky in slots:
            if (kz, ky) not in done:
                done.add((kz, ky))
                own[kz * 4 + ky].wait()
                arrive(R.at[kz, ky], d_recv, kz * 4 + ky)
                add_into(L.at[kz, ky], R.at[kz, ky], SLOT)

    move = (at_z, at_y)

    def block(h, ka, p):
        t = pl.ds(HALF * h, HALF)
        return L.at[ka, pl.ds(2 * p, 2), t] if h == 0 else L.at[pl.ds(2 * p, 2), ka, t]

    def cells(h, ka, p):
        return [(ka, 2 * p + i) if h == 0 else (2 * p + i, ka) for i in range(2)]

    def send_a(h, k, ka, p, step):
        need(*cells(h, ka, p))
        go(block(h, ka, p), RA.at[h, k], a_send, a_recv, h * 6 + k, move[h](step))

    def take_a(h, k, ka, p):
        need(*cells(h, ka, p))
        arrive(RA.at[h, k], a_recv, h * 6 + k)
        for i in range(2):
            add_into(block(h, ka, p).at[i], RA.at[h, k, i], HALF)

    for k, ka, p, step in ((0, 0, 0, 1), (1, 0, 1, 3), (2, 1, 1, 1), (3, 2, 0, 3)):
        for h in range(2):
            send_a(h, k, ka, p, step)
    for k, ka, p, step in ((0, 1, 0, 1), (1, 2, 1, 3)):
        for h in range(2):
            take_a(h, k, ka, p)
            send_a(h, k + 4, ka, p, step)

    def sum_three(h, p):
        ks = (3, 4) if p == 0 else (2, 5)
        need(*cells(h, 3, p))
        for k in ks:
            arrive(RA.at[h, k], a_recv, h * 6 + k)
        for i in range(2):
            dst, one, two = block(h, 3, p).at[i], RA.at[h, ks[0], i], RA.at[h, ks[1], i]

            def body(n, carry):
                for k in range(3):
                    t = n * 3 + k
                    dst[t] = (dst[t].astype(F32) + one[t].astype(F32) + two[t].astype(F32)).astype(BF16)
                return carry

            lax.fori_loop(0, HALF // 3, body, 0)

    def cell(h, kb, q):
        t = pl.ds(HALF * h + QUART * q, QUART)
        return L.at[3, kb, t] if h == 0 else L.at[kb, 3, t]

    def send_b(h, k, kb, q, step):
        go(cell(h, kb, q), RB.at[h, k], b_send, b_recv, h * 6 + k, move[1 - h](step))

    def take_b(h, k, kb, q):
        arrive(RB.at[h, k], b_recv, h * 6 + k)
        add_into(cell(h, kb, q), RB.at[h, k], QUART)

    for h in range(2):
        sum_three(h, 0)
        send_b(h, 0, 0, 0, 1)
        send_b(h, 1, 0, 1, 3)
        send_b(h, 2, 1, 1, 1)
    for h in range(2):
        sum_three(h, 1)
        send_b(h, 3, 2, 0, 3)
    for h in range(2):
        take_b(h, 0, 1, 0)
        send_b(h, 4, 1, 0, 1)
        take_b(h, 1, 2, 1)
        send_b(h, 5, 2, 1, 3)
    for h in range(2):
        for q, ks in ((0, (3, 4)), (1, (2, 5))):
            for k in ks:
                arrive(RB.at[h, k], b_recv, h * 6 + k)
            dst, one, two = cell(h, 3, q), RB.at[h, ks[0]], RB.at[h, ks[1]]

            def body(n, carry):
                for k in range(3):
                    t = n * 3 + k
                    dst[t] = (dst[t].astype(F32) + one[t].astype(F32) + two[t].astype(F32)).astype(BF16)
                return carry

            lax.fori_loop(0, QUART // 3, body, 0)

    mine = L.at[3, 3]
    main = remote(mine, window.at[pl.ds(EDGE, SLOT)], x_send, x_recv, 0, mirror)
    main_keep = pltpu.make_async_copy(mine, window.at[pl.ds(EDGE, SLOT)], load_sem.at[20])

    @pl.when(swap)
    def _():
        main.start()

    @pl.when(jnp.logical_not(swap))
    def _():
        main_keep.start()

    go(mine.at[pl.ds(0, EDGE)], window.at[pl.ds(EDGE + SLOT, EDGE)], x_send, x_recv, 1, owner(around(v - 1)))
    go(mine.at[pl.ds(SLOT - EDGE, EDGE)], window.at[pl.ds(0, EDGE)], x_send, x_recv, 2, owner(around(v + 1)))

    def clear(i, carry):
        flat[pl.ds(pl.multiple_of(i * 32, 32), 32), :] = jnp.zeros((32, 128), F32)
        return carry

    lax.fori_loop(0, BACK_ROWS // 32, clear, 0)
    for copy in extra:
        copy.wait()
    arrive(window.at[pl.ds(EDGE + SLOT, EDGE)], x_recv, 1)
    arrive(window.at[pl.ds(0, EDGE)], x_recv, 2)

    @pl.when(swap)
    def _():
        main.wait()

    @pl.when(jnp.logical_not(swap))
    def _():
        main_keep.wait()

    low_tile = SLOT * fs - EDGE
    high_tile = SLOT * fs + SLOT + EDGE
    origin = SHARD * fs - FRONT
    for index, (base, c, groups, per, start) in enumerate(SECTIONS):
        if index == 1:
            lane = lax.broadcasted_iota(jnp.int32, (8, 128), 1)
            g0 = lax.div(jnp.maximum(SHARD * fs - base, 0), per)
            g1 = lax.div(jnp.maximum(SHARD * (fs + 1) - base, 0) + per - 1, per)

            def head_group(g, carry):
                t = start + g * 8 - low_tile
                for j in range(8):
                    headrows[pl.ds(j, 16, stride=8), :] = window[t + j].astype(F32)
                row = base + per * g - origin
                for i in range(16):
                    q, s = divmod(1000 * i, 128)
                    value = headrows[pl.ds(i * 8, 8), :]
                    if s:
                        value = pltpu.roll(value, s, 1)
                        flat[pl.ds(row + q, 8), :] += jnp.where(lane >= s, value, 0.0)
                        flat[pl.ds(row + q + 1, 8), :] += jnp.where(lane < s, value, 0.0)
                    else:
                        flat[pl.ds(row + q, 8), :] += value
                return carry

            lax.fori_loop(jnp.minimum(g0, groups), jnp.minimum(g1, groups), head_group, 0)
        else:

            def tile(t, carry):
                g = lax.div(t - start, c)
                j = lax.rem(t - start, c)
                flat[pl.ds(base + 16 * c * g + j - origin, 16, stride=c), :] = window[t - low_tile].astype(F32)
                return carry

            lax.fori_loop(jnp.maximum(low_tile, start), jnp.minimum(high_tile, start + c * groups), tile, 0)

    fix_one = 1.0 / (1.0 - BETA_ONE**STEP)
    fix_two = 1.0 / (1.0 - BETA_TWO**STEP)

    def in_rows(fn, lo, hi, step=32):
        def body(i, carry):
            fn(pl.multiple_of(i * step, step), step)
            return carry

        n = (hi - lo) // step
        lax.fori_loop(lo // step, lo // step + n, body, 0)
        if lo + n * step < hi:
            fn(lo + n * step, hi - lo - n * step)

    def adam(r, n):
        grad = flat[pl.ds(FRONT + r, n), :]
        m = BETA_ONE * first[pl.ds(r, n), :] + (1.0 - BETA_ONE) * grad
        s = BETA_TWO * second[pl.ds(r, n), :] + (1.0 - BETA_TWO) * grad * grad
        first[pl.ds(r, n), :] = m
        second[pl.ds(r, n), :] = s
        u = (m * fix_one) / (jnp.sqrt(s * fix_two) + ADAM_EPS)
        upd[pl.ds(r, n), :] = u

    in_rows(adam, 0, SHARD)
    upd[pl.ds(SHARD, PADDED - SHARD), :] = jnp.zeros((PADDED - SHARD, 128), F32)
    outs = [pltpu.make_async_copy(src, dst, load_sem.at[16 + i]) for i, (src, dst) in enumerate(((first, first_out), (second, second_out)))]
    for copy in outs:
        copy.start()

    def lower(r, n):
        low[pl.ds(r, n), :] = upd[pl.ds(r, n), :].astype(BF16)

    in_rows(lower, 0, PADDED)
    go(low, low2, x_send, x_recv, 3, sibling)
    arrive(low2, x_recv, 3)
    half = PADDED // 2

    def pairs(r, n):
        at = pl.ds(pl.multiple_of(b * half + r, 16), n)
        pair[pl.ds(r, n), :] = low[at, :] + low2[at, :]

    in_rows(pairs, 0, half)
    go(pair, pair2, x_send, x_recv, 4, across)
    arrive(pair2, x_recv, 4)

    def fours(r, n):
        total[pl.ds(r, n), :] = pair[pl.ds(r, n), :].astype(F32) + pair2[pl.ds(r, n), :].astype(F32)

    in_rows(fours, 0, half)
    go(total, total2, x_send, x_recv, 5, sibling)

    def outer(source, shift):
        def rows_of(r, n):
            at = pl.ds(shift + r, n)
            t = source[pl.ds(r, n), :]
            old = w[at, :]
            averaged = INNER_RATE * (t * 0.25 + DECAY * old)
            momentum = OUTER_MU * mom[at, :] + averaged
            upd[at, :] = averaged
            mom[at, :] = momentum
            w[at, :] = old - OUTER_RATE * (averaged + OUTER_MU * momentum)

        return rows_of

    def both(here, there):
        in_rows(outer(here, 0), 0, half)
        in_rows(outer(there, half), 0, SHARD - half)

    arrive(total2, x_recv, 5)

    @pl.when(b == 0)
    def _():
        both(total, total2)

    @pl.when(b == 1)
    def _():
        both(total2, total)

    final = [(upd.at[pl.ds(0, SHARD)], avg_out), (mom, mom_out), (w, new_out)]
    final = [pltpu.make_async_copy(src, dst, load_sem.at[18 + i]) for i, (src, dst) in enumerate(final)]
    for copy in final:
        copy.start()
    for copy in sends:
        copy.wait_send()
    for copy in outs + final:
        copy.wait()


def reduce_update(grads, weights, first, second, momentum):
    hbm = pl.BlockSpec(memory_space=pl.ANY)
    V = pltpu.VMEM
    flat = jax.ShapeDtypeStruct((SHARD, 128), F32)
    dma = pltpu.SemaphoreType.DMA
    return pl.pallas_call(
        reduce_kernel,
        out_shape=(flat,) * 5,
        in_specs=[hbm] * 5,
        out_specs=(hbm,) * 5,
        scratch_shapes=[
            V((4, 4, SLOT, 16, 128), BF16),
            V((4, 4, SLOT, 16, 128), BF16),
            V((2, 6, 2, HALF, 16, 128), BF16),
            V((2, 6, QUART, 16, 128), BF16),
            V((EDGE + SLOT + EDGE, 16, 128), BF16),
            V((BACK_ROWS, 128), F32),
            V((128, 128), F32),
            V((SHARD, 128), F32),
            V((SHARD, 128), F32),
            V((SHARD, 128), F32),
            V((SHARD, 128), F32),
            V((PADDED, 128), F32),
            V((PADDED, 128), BF16),
            V((PADDED, 128), BF16),
            V((PADDED // 2, 128), BF16),
            V((PADDED // 2, 128), BF16),
            V((PADDED // 2, 128), F32),
            V((PADDED // 2, 128), F32),
            dma((21,)),
            dma((16,)),
            dma((16,)),
            dma((12,)),
            dma((12,)),
            dma((12,)),
            dma((12,)),
            dma((6,)),
            dma((6,)),
        ],
        compiler_params=pltpu.CompilerParams(collective_id=1, has_side_effects=True, vmem_limit_bytes=52 * 1024 * 1024),
        name="reduce_update",
    )(grads, weights, first, second, momentum)


def body(patches, labels, counts, weights, first_moments, second_moments, outer_momentum):
    rep = lax.axis_index("rep")
    rank = lax.axis_index("fsdp")
    total_count = jnp.sum(counts[0, 0]).astype(jnp.float32)
    valid = (rank < counts[0, 0]).astype(jnp.float32)
    fields = jnp.concatenate([labels[0, 0, :, 0].astype(jnp.float32), valid / total_count, valid, jnp.zeros((2,), jnp.float32)])
    meta = jnp.broadcast_to(fields[:, None], (8, 128))
    flat = weights.reshape(SHARD, 128)
    tiles, images, meta = gather(flat, patches.reshape(2, P_SIZE, D), meta)
    grads, loss = compute(tiles.reshape(NTILES, 16, 128), images, meta)
    group = 2 * lax.div(rep, 2) + lax.rem(lax.div(rank, 4), 2)
    losses = lax.psum(jnp.where(jnp.arange(4) == group, loss[0, 0], 0.0), ("rep", "fsdp"))
    averaged, momentum, new_weights, first, second = reduce_update(
        grads.reshape(NSLOT, SLOT, 16, 128),
        flat,
        first_moments.reshape(SHARD, 128),
        second_moments.reshape(SHARD, 128),
        outer_momentum.reshape(SHARD, 128),
    )
    return (
        averaged.reshape(-1),
        momentum.reshape(-1),
        new_weights.reshape(-1),
        first.reshape(1, -1),
        second.reshape(1, -1),
        lax.dynamic_slice(losses, (rep,), (1,)).reshape(1, 1),
    )


def solution(mesh):
    placed = (
        P("rep", None, None, "fsdp", None, None),
        P("rep", None, None, "fsdp"),
        P("rep", None, None),
        P("fsdp"),
        P("rep", "fsdp"),
        P("rep", "fsdp"),
        P("fsdp"),
    )
    return jax.shard_map(
        body,
        mesh=mesh,
        in_specs=placed,
        out_specs=(
            P("fsdp"),
            P("fsdp"),
            P("fsdp"),
            P("rep", "fsdp"),
            P("rep", "fsdp"),
            P("rep", None),
        ),
        check_vma=False,
    )
```

time: 2460 us -> 365 us (0.15)
  the two profiles are of different devices: /device:TPU:0 before, /device:TPU:24 now
where the time goes in v1:
time: 365 us; the launch traced here: 362 us
  Pallas kernels  251 us (69%)
  blocking collectives  64.4 us (18%)
  other arithmetic  23.6 us (6%)
  local copies, waits for them, and re-layouts  21.7 us (6%)
    pallas_call x1, Pallas kernels, compute(): pl.pallas_call(compute_kernel, out_shape=(jax.ShapeDtypeStruct((NTILES, 1...  91.3 us
    pallas_call x1, Pallas kernels, reduce_update(): pl.pallas_call(reduce_kernel, out_shape=(flat,) * 5, in_specs=[hbm] * 5,...  86.1 us
    pallas_call x1, Pallas kernels, gather(): pl.pallas_call(gather_kernel, out_shape=(jax.ShapeDtypeStruct((NSLOT, SLO...  73.7 us
    psum x1, blocking collectives, body(): lax.psum(jnp.where(jnp.arange(4) == group, loss[0, 0], 0.0), ('rep', 'fsd...  64.4 us
    unnamed x2, other arithmetic  22.2 us
    unnamed x24, local copies, waits for them, and re-layouts  12.9 us

profile of v1, /device:TPU:24, one launch (start us, length us, event | category | flops | bytes accessed | tf_op | source)
XLA Modules:
  0.0 362.3 jit_solution(16409401647970234227)
XLA Ops:
  0.6 0.0 copy-start.1
  0.7 1.2 copy.19
  1.9 0.6 reduce_sum.9
  3.3 0.1 pad_maximum_fusion
  3.4 0.1 broadcast_in_dim.14.meta_ref
  3.4 73.7 %gather_weights.1 = (bf16[32,132,16,128]{3,2,1,0:T(8,128)(2,1)S(1)}, bf16[2,196,768]{2,1,0:T(8,128)(2,1)S(1)}, f32[8,128]{1,0:T(8,128)S(1)}) custom-call(f32[2098,128]{1,0:T(8,128)S(1)} %bitcast.30, bf16[2,196,768]{2,1,0:T(8,128)(2,1)S(1)} %bitcast.31, f32[8,128]{1,0:T(8,128)S(1)} %broadcast_in_dim.14.meta_ref), custom_call_target="tpu_custom_call" | custom-call | tf_op jit(solution)/shard_map/gather_weights/pallas_call | solution.py:281
  77.2 5.9 %copy-done = bf16[32,132,16,128]{3,2,1,0:T(8,128)(2,1)} copy-done((bf16[32,132,16,128]{3,2,1,0:T(8,128)(2,1)}, bf16[32,132,16,128]{3,2,1,0:T(8,128)(2,1)S(1)}, u32[]{:S(2)}) %copy-start) | copy-done | bytes 17301528
  83.1 0.8 copy-done.2
  83.9 0.6 copy-done.3
  84.5 91.3 %grads.1 = (bf16[4224,16,128]{2,1,0:T(8,128)(2,1)}, f32[8,128]{1,0:T(8,128)}) custom-call(bf16[4224,16,128]{2,1,0:T(8,128)(2,1)} %bitcast.28, bf16[2,196,768]{2,1,0:T(8,128)(2,1)} %copy-done.2, f32[8,128]{1,0:T(8,128)} %copy-done.3), custom_call_target="tpu_custom_call" | custom-call | tf_op jit(solution)/shard_map/grads/pallas_call | solution.py:634
  175.8 0.0 copy-start.7
  175.8 11.2 %reduce.1 = f32[268544]{0:T(1024)} reduce(f32[1,268544]{1,0:T(1,128)S(1)} %copy-done.6, f32[]{:T(128)} %constant.33), dimensions={0}, to_apply=%param.11.reduce_sub_computation | reduce | bytes 2148356 | tf_op args[4]
  187.0 11.0 %reduce.2 = f32[268544]{0:T(1024)} reduce(f32[1,268544]{1,0:T(1,128)S(1)} %copy-done.7, f32[]{:T(128)} %constant.33), dimensions={0}, to_apply=%param.12.reduce_sub_computation | reduce | bytes 2148356 | tf_op args[5]
  198.0 86.1 %reduce_update.1 = (f32[2098,128]{1,0:T(8,128)S(1)}, f32[2098,128]{1,0:T(8,128)}, f32[2098,128]{1,0:T(8,128)}, f32[2098,128]{1,0:T(8,128)}, f32[2098,128]{1,0:T(8,128)}) custom-call(bf16[32,132,16,128]{3,2,1,0:T(8,128)(2,1)} %bitcast.33, f32[2098,128]{1,0:T(8,128)} %bitcast.29, f32[2098,128]{1,0:T(8,128)} %bitcast.34, f32[2098,128]{1,0:T(8,128)} %bitcast.35, ...), custom_call_target="tpu_custom_call" | custom-call | tf_op jit(solution)/shard_map/reduce_update/pallas_call | solution.py:1014
  284.1 7.0 %copy_bitcast_fusion = (f32[1,268544]{1,0:T(1,128)}, f32[1,268544]{1,0:T(1,128)}) fusion(f32[1,1,2098,128]{3,2,1,0:T(8,128)} %bitcast.40, f32[1,1,2098,128]{3,2,1,0:T(8,128)} %bitcast.39), kind=kLoop, calls=%fused_computation | loop fusion | bytes 4296704 | tf_op jit(solution)/shard_map/reshape | solution.py:1077
  291.1 1.2 slice.3
  292.3 0.6 compare_select_fusion
  292.9 64.4 %psum.7 = f32[4]{0:T(128)S(1)} all-reduce(f32[4]{0:T(128)S(1)} %compare_select_fusion), channel_id=1, replica_groups=mesh['rep'=4,'fsdp'=32] {'rep','fsdp'}, use_global_device_ids=true, to_apply=%region_1.2 | all-reduce | flops 4 | bytes 32 | tf_op jit(solution)/shard_map/psum | solution.py:1064
  357.4 0.6 dynamic_slice.3
  358.0 1.0 copy.23
  359.0 0.6 copy-done.5
  359.6 1.0 copy.24
  360.7 0.6 copy-done.4
  361.2 1.0 copy.25
  (17 shorter events, 0.0 us)
Async XLA Ops:
  0.6 2.8 copy-start.1
  0.6 1.2 copy-start.8
  0.7 2.6 copy-start.9
  77.2 5.9 %copy-start = (bf16[32,132,16,128]{3,2,1,0:T(8,128)(2,1)}, bf16[32,132,16,128]{3,2,1,0:T(8,128)(2,1)S(1)}, u32[]{:S(2)}) copy-start(bf16[32,132,16,128]{3,2,1,0:T(8,128)(2,1)S(1)} %get-tuple-element.16) | copy-start | bytes 51904516
  83.1 0.8 copy-start.2
  83.9 0.6 copy-start.3
  84.5 91.3 %copy-start.6 = (f32[1,268544]{1,0:T(1,128)S(1)}, f32[1,268544]{1,0:T(1,128)}, u32[]{:S(2)}) copy-start(f32[1,268544]{1,0:T(1,128)} %param.11) | copy-start | bytes 3222532
  175.8 11.2 %copy-start.7 = (f32[1,268544]{1,0:T(1,128)S(1)}, f32[1,268544]{1,0:T(1,128)}, u32[]{:S(2)}) copy-start(f32[1,268544]{1,0:T(1,128)} %param.12) | copy-start | bytes 3222532
  358.0 1.6 copy-start.5
  359.6 1.6 copy-start.4

commit v2 on v1

--- a/solution.py
+++ b/solution.py
@@ -175,7 +175,7 @@
         return (lax.rem(z + k, 4)) * 8 + b * 4 + lax.rem(y + j, 4)
 
     move = (at_y, at_z)
-    keep = pltpu.make_async_copy(slot, t_out.at[v], local_sem.at[3])
+    keep = pltpu.make_async_copy(slot, t_out.at[pl.ds(v * SLOT, SLOT)], local_sem.at[3])
     keep.start()
     sends = []
     GS = g_send
@@ -191,7 +191,7 @@
         remote(dst, dst, GS, GR, k, sibling).wait_recv()
 
     def part(slot_id, lo, n):
-        return t_out.at[slot_id, pl.ds(lo, n)]
+        return t_out.at[pl.ds(slot_id * SLOT + lo, n)]
 
     def p1(h, k):
         return h * 20 + k
@@ -276,38 +276,6 @@
         meta_keep.wait()
 
 
-def gather(weights, patches, meta):
-    hbm = pl.BlockSpec(memory_space=pl.ANY)
-    return pl.pallas_call(
-        gather_kernel,
-        out_shape=(
-            jax.ShapeDtypeStruct((NSLOT, SLOT, 16, 128), jnp.bfloat16),
-            jax.ShapeDtypeStruct(patches.shape, patches.dtype),
-            jax.ShapeDtypeStruct(meta.shape, meta.dtype),
-        ),
-        in_specs=[hbm] * 3,
-        out_specs=(hbm,) * 3,
-        scratch_shapes=[
-            pltpu.VMEM((FROWS, 128), jnp.float32),
-            pltpu.VMEM((128, 128), jnp.float32),
-            pltpu.VMEM((2112, 128), jnp.bfloat16),
-            pltpu.VMEM((LO, 128), jnp.bfloat16),
-            pltpu.VMEM((HI, 128), jnp.bfloat16),
-            pltpu.VMEM((2112, 128), jnp.bfloat16),
-            pltpu.VMEM((HI, 128), jnp.bfloat16),
-            pltpu.VMEM((LO, 128), jnp.bfloat16),
-            pltpu.VMEM((SLOT, 16, 128), jnp.bfloat16),
-            pltpu.SemaphoreType.DMA((4,)),
-            pltpu.SemaphoreType.DMA((5,)),
-            pltpu.SemaphoreType.DMA((5,)),
-            pltpu.SemaphoreType.DMA((72,)),
-            pltpu.SemaphoreType.DMA((72,)),
-        ],
-        compiler_params=pltpu.CompilerParams(collective_id=0, has_side_effects=True, vmem_limit_bytes=32 * 1024 * 1024),
-        name="gather_weights",
-    )(weights, patches, meta)
-
-
 D = 768
 HEADS = 12
 HEAD_DIM = 64
@@ -355,13 +323,8 @@
     return rstd * (d_hat - m1 - hat * m2)
 
 
-def compute_kernel(t_hbm, patch_ref, meta_ref, g_hbm, loss_ref, T, G, x, xt, h, a, at, mix, prob, o, h1, a2, hid, slope, h2, dh, dyb, du, dmix, sem, gsem):
-    bounds = [(0, T_HEAD), (T_QKV, T_OUT), (T_NORM, T_QKV), (T_OUT, T_IN), (T_IN, T_FO), (T_FO, 4212), (T_HEAD, T_NORM)]
-    loads = []
-    for i, (lo, hi) in enumerate(bounds):
-        copy = pltpu.make_async_copy(t_hbm.at[pl.ds(lo, hi - lo)], T.at[pl.ds(lo, hi - lo)], sem.at[i])
-        copy.start()
-        loads.append(copy)
+def compute_kernel(patch_ref, meta_ref, loss_ref, T, x, h, a, at, mix, prob, o, h1, a2, hid, slope, h2, dh, dyb, dmix):
+    G = T
 
     def section(ref, start, c, groups):
         return ref.at[pl.ds(start, groups * c)].reshape(groups, c, 16, 128)
@@ -391,7 +354,6 @@
         x[pl.ds(i * ROWS + 192, 16), :] = jnp.concatenate([patch_ref[i, pl.ds(192, 4), :], jnp.zeros((12, D), BF16)], axis=0)
 
     real = lax.broadcasted_iota(jnp.int32, (ROWS, 128), 0) < P_SIZE
-    loads[0].wait()
     for j in range(3):
         acc = dot(x[...], cols(T_E, 6, 48, j))
         p = cols(T_POS, 6, 13, j).astype(F32)
@@ -399,7 +361,6 @@
         for i in range(2):
             h[pl.ds(i * ROWS, ROWS), pl.ds(j * BLK, BLK)] = acc[i * ROWS : (i + 1) * ROWS] + p
 
-    loads[2].wait()
     gain1, shift1, gain2, shift2 = (row_of(T_NORM, k) for k in range(4))
 
     def norm_one(i, carry):
@@ -408,7 +369,6 @@
         return carry
 
     lax.fori_loop(0, steps, norm_one, 0)
-    loads[1].wait()
 
     def mix_block(j, carry):
         mix[:, lanes(j)] = dot(a[...], cols(T_QKV, 18, 48, j)).astype(BF16)
@@ -445,7 +405,6 @@
         return carry
 
     lax.fori_loop(0, 12, attend, 0)
-    loads[3].wait()
     for j in range(3):
         h1[:, pl.ds(j * BLK, BLK)] = h[:, pl.ds(j * BLK, BLK)] + dot(o[...], cols(T_OUT, 6, 48, j))
 
@@ -455,7 +414,6 @@
         return carry
 
     lax.fori_loop(0, steps, norm_two, 0)
-    loads[4].wait()
 
     def up_block(j, carry):
         u = dot(a2[...], cols(T_IN, 24, 48, j))
@@ -466,7 +424,6 @@
         return carry
 
     lax.fori_loop(0, 12, up_block, 0)
-    loads[5].wait()
     for j in range(3):
         h2[:, pl.ds(j * BLK, BLK)] = h1[:, pl.ds(j * BLK, BLK)] + dot(hid[...], cols(T_FO, 6, 192, j))
 
@@ -485,7 +442,6 @@
     mean_hat = jnp.concatenate(means + [jnp.zeros((14, D), F32)], axis=0)
     two = lax.broadcasted_iota(jnp.int32, (16, D), 0) < 2
     pooled = jnp.where(two, mean_hat * gain_end + shift_end, 0.0).astype(BF16)
-    loads[6].wait()
     logits = jnp.concatenate([dot(pooled, cols(T_HEAD, 8, 48, j)) for j in range(4)], axis=1)
     lane = lax.broadcasted_iota(jnp.int32, (16, 1024), 1)
     lane_f = lane.astype(F32)
@@ -531,14 +487,13 @@
     def mlp_block(j, carry):
         dy = dyb[...]
         d_w = t_dot(hid[:, lanes(j)], dy).astype(BF16)
-        part = section(G, T_FO + j * 96, 6, 16)
+        part = section(T, T_FO + j * 96, 6, 16)
+        w = jnp.concatenate([part[:, k].reshape(BLK, 128) for k in range(6)], axis=1)
         for k in range(6):
             part[:, k] = d_w[:, k * 128 : (k + 1) * 128].reshape(16, 16, 128)
-        part = section(T, T_FO + j * 96, 6, 16)
-        w = jnp.concatenate([part[:, k].reshape(BLK, 128) for k in range(6)], axis=1)
         d_u = (dot_t(dy, w) * slope[:, lanes(j)].astype(F32)).astype(BF16)
+        da[...] += dot_t(d_u, cols(T_IN, 24, 48, j))
         put_cols(T_IN, 24, 48, j, dot(at[...], d_u))
-        da[...] += dot_t(d_u, cols(T_IN, 24, 48, j))
         return carry
 
     lax.fori_loop(0, 12, mlp_block, 0)
@@ -559,8 +514,8 @@
     da[...] = jnp.zeros((TOK, D), F32)
     for j in range(3):
         dz = dyb[:, pl.ds(j * BLK, BLK)]
+        da[...] += dot_t(dz, cols(T_OUT, 6, 48, j))
         put_cols(T_OUT, 6, 48, j, dot(at[...], dz))
-        da[...] += dot_t(dz, cols(T_OUT, 6, 48, j))
     o[...] = da[...].astype(BF16)
 
     def attend_back(n, carry):
@@ -591,8 +546,8 @@
 
     def qkv_block(j, carry):
         d = dmix[:, lanes(j)]
+        da[...] += dot_t(d, cols(T_QKV, 18, 48, j))
         put_cols(T_QKV, 18, 48, j, dot(at[...], d))
-        da[...] += dot_t(d, cols(T_QKV, 18, 48, j))
         return carry
 
     lax.fori_loop(0, 9, qkv_block, 0)
@@ -622,25 +577,47 @@
         d_pos = jnp.where(row_id == P_SIZE + 1, jnp.broadcast_to(d_shift_end[:, s], (ROWS, BLK)), d_pos)
         put_cols(T_POS, 6, 13, j, d_pos)
     G[pl.ds(4212, 12)] = jnp.zeros((12, 16, 128), BF16)
-    out = pltpu.make_async_copy(G, g_hbm, gsem)
+
+
+def front_kernel(w_ref, patch_ref, meta_ref, g_hbm, loss_ref, patch_in, meta_in, *rest):
+    gather_part, compute_part, gsem = rest[:14], rest[14:-1], rest[-1]
+    T = compute_part[0]
+    gather_kernel(w_ref, patch_ref, meta_ref, T, patch_in, meta_in, *gather_part)
+    compute_kernel(patch_in, meta_in, loss_ref, *compute_part)
+    out = pltpu.make_async_copy(T, g_hbm, gsem)
     out.start()
     out.wait()
 
 
-def compute(tiles, patches, meta):
+def front(weights, patches, meta):
     hbm = pl.BlockSpec(memory_space=pl.ANY)
     vmem = pl.BlockSpec(memory_space=pltpu.VMEM)
     V = pltpu.VMEM
+    dma = pltpu.SemaphoreType.DMA
     return pl.pallas_call(
-        compute_kernel,
+        front_kernel,
         out_shape=(jax.ShapeDtypeStruct((NTILES, 16, 128), BF16), jax.ShapeDtypeStruct((8, 128), F32)),
-        in_specs=[hbm, vmem, vmem],
+        in_specs=[hbm] * 3,
         out_specs=(hbm, vmem),
         scratch_shapes=[
-            V((NTILES, 16, 128), BF16),
+            V(patches.shape, BF16),
+            V((8, 128), F32),
+            V((FROWS, 128), F32),
+            V((128, 128), F32),
+            V((2112, 128), BF16),
+            V((LO, 128), BF16),
+            V((HI, 128), BF16),
+            V((2112, 128), BF16),
+            V((HI, 128), BF16),
+            V((LO, 128), BF16),
+            V((SLOT, 16, 128), BF16),
+            dma((4,)),
+            dma((5,)),
+            dma((5,)),
+            dma((72,)),
+            dma((72,)),
             V((NTILES, 16, 128), BF16),
             V((TOK, D), BF16),
-            V((8, 128), BF16),
             V((TOK, D), F32),
             V((TOK, D), BF16),
             V((D, TOK), BF16),
@@ -654,14 +631,12 @@
             V((TOK, D), F32),
             V((TOK, D), F32),
             V((TOK, D), BF16),
-            V((8, 128), BF16),
             V((TOK, 3 * D), BF16),
-            pltpu.SemaphoreType.DMA((8,)),
-            pltpu.SemaphoreType.DMA,
+            dma,
         ],
-        compiler_params=pltpu.CompilerParams(vmem_limit_bytes=62 * 1024 * 1024),
-        name="grads",
-    )(tiles, patches, meta)
+        compiler_params=pltpu.CompilerParams(collective_id=0, has_side_effects=True, vmem_limit_bytes=60 * 1024 * 1024),
+        name="front",
+    )(weights, patches, meta)
 
 
 EDGE = 24
@@ -682,10 +657,10 @@
 
 
 def reduce_kernel(
-    g_ref, w_ref, first_ref, second_ref, mom_ref,
-    avg_out, mom_out, new_out, first_out, second_out,
+    g_ref, loss_ref, w_ref, first_ref, second_ref, mom_ref,
+    avg_out, mom_out, new_out, first_out, second_out, loss_out,
     L, R, RA, RB, window, flat, headrows, w, first, second, mom, upd, low, low2, pair, pair2, total, total2,
-    load_sem, d_send, d_recv, a_send, a_recv, b_send, b_recv, x_send, x_recv,
+    load_sem, d_send, d_recv, a_send, a_recv, b_send, b_recv, x_send, x_recv, LS, l_send, l_recv,
 ):
     xl, b, z, a, y = coords()
     fs = z * 8 + a * 4 + y
@@ -747,6 +722,13 @@
     for copy in extra:
         copy.start()
 
+    LS[0] = loss_ref[...]
+
+    def loss_send(src, dst, target):
+        go(LS.at[src], LS.at[dst], l_send, l_recv, dst - 1, target)
+
+    loss_send(0, 1, sibling)
+
     def add_into(dst, src, n):
         def one(i, carry):
             for k in range(3):
@@ -791,6 +773,10 @@
     for k, ka, p, step in ((0, 0, 0, 1), (1, 0, 1, 3), (2, 1, 1, 1), (3, 2, 0, 3)):
         for h in range(2):
             send_a(h, k, ka, p, step)
+    arrive(LS.at[1], l_recv, 0)
+    LS[8] = loss_ref[...] + LS[1]
+    loss_send(8, 2, at_y(1))
+    loss_send(8, 3, at_y(3))
     for k, ka, p, step in ((0, 1, 0, 1), (1, 2, 1, 3)):
         for h in range(2):
             take_a(h, k, ka, p)
@@ -823,6 +809,9 @@
         arrive(RB.at[h, k], b_recv, h * 6 + k)
         add_into(cell(h, kb, q), RB.at[h, k], QUART)
 
+    arrive(LS.at[2], l_recv, 1)
+    loss_send(2, 4, at_y(1))
+    arrive(LS.at[3], l_recv, 2)
     for h in range(2):
         sum_three(h, 0)
         send_b(h, 0, 0, 0, 1)
@@ -831,6 +820,10 @@
     for h in range(2):
         sum_three(h, 1)
         send_b(h, 3, 2, 0, 3)
+    arrive(LS.at[4], l_recv, 3)
+    LS[9] = (LS[8] + LS[4]) + (LS[2] + LS[3])
+    loss_send(9, 5, at_z(1))
+    loss_send(9, 6, at_z(3))
     for h in range(2):
         take_b(h, 0, 1, 0)
         send_b(h, 4, 1, 0, 1)
@@ -850,6 +843,9 @@
 
             lax.fori_loop(0, QUART // 3, body, 0)
 
+    arrive(LS.at[5], l_recv, 4)
+    loss_send(5, 7, at_z(1))
+    arrive(LS.at[6], l_recv, 5)
     mine = L.at[3, 3]
     main = remote(mine, window.at[pl.ds(EDGE, SLOT)], x_send, x_recv, 0, mirror)
     main_keep = pltpu.make_async_copy(mine, window.at[pl.ds(EDGE, SLOT)], load_sem.at[20])
@@ -919,6 +915,14 @@
 
             lax.fori_loop(jnp.maximum(low_tile, start), jnp.minimum(high_tile, start + c * groups), tile, 0)
 
+    arrive(LS.at[7], l_recv, 6)
+    LS[10] = (LS[9] + LS[7]) + (LS[5] + LS[6])
+    loss_swap = remote(LS.at[10], LS.at[11], l_send, l_recv, 10, mirror)
+
+    @pl.when(swap)
+    def _():
+        loss_swap.start()
+
     fix_one = 1.0 / (1.0 - BETA_ONE**STEP)
     fix_two = 1.0 / (1.0 - BETA_TWO**STEP)
 
@@ -1000,22 +1004,32 @@
     final = [pltpu.make_async_copy(src, dst, load_sem.at[18 + i]) for i, (src, dst) in enumerate(final)]
     for copy in final:
         copy.start()
+    @pl.when(swap)
+    def _():
+        loss_swap.wait()
+        loss_out[...] = LS[11]
+
+    @pl.when(jnp.logical_not(swap))
+    def _():
+        loss_out[...] = LS[10]
+
     for copy in sends:
         copy.wait_send()
     for copy in outs + final:
         copy.wait()
 
 
-def reduce_update(grads, weights, first, second, momentum):
+def reduce_update(grads, loss, weights, first, second, momentum):
     hbm = pl.BlockSpec(memory_space=pl.ANY)
     V = pltpu.VMEM
+    vmem = pl.BlockSpec(memory_space=pltpu.VMEM)
     flat = jax.ShapeDtypeStruct((SHARD, 128), F32)
     dma = pltpu.SemaphoreType.DMA
     return pl.pallas_call(
         reduce_kernel,
-        out_shape=(flat,) * 5,
-        in_specs=[hbm] * 5,
-        out_specs=(hbm,) * 5,
+        out_shape=(flat,) * 5 + (jax.ShapeDtypeStruct((8, 128), F32),),
+        in_specs=[hbm, vmem] + [hbm] * 4,
+        out_specs=(hbm,) * 5 + (vmem,),
         scratch_shapes=[
             V((4, 4, SLOT, 16, 128), BF16),
             V((4, 4, SLOT, 16, 128), BF16),
@@ -1044,38 +1058,90 @@
             dma((12,)),
             dma((6,)),
             dma((6,)),
+            V((12, 8, 128), F32),
+            dma((11,)),
+            dma((11,)),
         ],
         compiler_params=pltpu.CompilerParams(collective_id=1, has_side_effects=True, vmem_limit_bytes=52 * 1024 * 1024),
         name="reduce_update",
-    )(grads, weights, first, second, momentum)
+    )(grads, loss, weights, first, second, momentum)
+
+
+def rows_kernel(one, two, out_one, out_two, sem):
+    copies = [pltpu.make_async_copy(src.reshape(SHARD, 128), dst, sem.at[i]) for i, (src, dst) in enumerate(((one, out_one), (two, out_two)))]
+    for copy in copies:
+        copy.start()
+    for copy in copies:
+        copy.wait()
+
+
+def as_rows(one, two):
+    hbm = pl.BlockSpec(memory_space=pl.ANY)
+    shape = jax.ShapeDtypeStruct((SHARD, 128), F32)
+    return pl.pallas_call(
+        rows_kernel,
+        out_shape=(shape,) * 2,
+        in_specs=[hbm] * 2,
+        out_specs=(hbm,) * 2,
+        scratch_shapes=[pltpu.SemaphoreType.DMA((2,))],
+        name="as_rows",
+    )(one, two)
+
+
+def flat_kernel(*refs):
+    count = len(refs) // 2
+    sem = refs[-1]
+    copies = []
+    for i in range(count):
+        src, dst = refs[i], refs[count + i]
+        if len(dst.shape) == 2 and dst.shape[0] == 1:
+            dst = dst.reshape(SHARD, 128)
+        copies.append(pltpu.make_async_copy(src, dst, sem.at[i]))
+    for copy in copies:
+        copy.start()
+    for copy in copies:
+        copy.wait()
+
+
+def finish(averaged, momentum, new_weights, first, second):
+    hbm = pl.BlockSpec(memory_space=pl.ANY)
+    shape = jax.ShapeDtypeStruct((SHARD, 128), F32)
+    row = jax.ShapeDtypeStruct((1, SHARD * 128), F32)
+    return pl.pallas_call(
+        flat_kernel,
+        out_shape=(shape,) * 3 + (row,) * 2,
+        in_specs=[hbm] * 5,
+        out_specs=(hbm,) * 5,
+        scratch_shapes=[pltpu.SemaphoreType.DMA((5,))],
+        name="finish",
+    )(averaged, momentum, new_weights, first, second)
 
 
 def body(patches, labels, counts, weights, first_moments, second_moments, outer_momentum):
-    rep = lax.axis_index("rep")
     rank = lax.axis_index("fsdp")
     total_count = jnp.sum(counts[0, 0]).astype(jnp.float32)
     valid = (rank < counts[0, 0]).astype(jnp.float32)
     fields = jnp.concatenate([labels[0, 0, :, 0].astype(jnp.float32), valid / total_count, valid, jnp.zeros((2,), jnp.float32)])
     meta = jnp.broadcast_to(fields[:, None], (8, 128))
     flat = weights.reshape(SHARD, 128)
-    tiles, images, meta = gather(flat, patches.reshape(2, P_SIZE, D), meta)
-    grads, loss = compute(tiles.reshape(NTILES, 16, 128), images, meta)
-    group = 2 * lax.div(rep, 2) + lax.rem(lax.div(rank, 4), 2)
-    losses = lax.psum(jnp.where(jnp.arange(4) == group, loss[0, 0], 0.0), ("rep", "fsdp"))
-    averaged, momentum, new_weights, first, second = reduce_update(
+    first, second = as_rows(first_moments, second_moments)
+    grads, loss = front(flat, patches.reshape(2, P_SIZE, D), meta)
+    averaged, momentum, new_weights, first, second, losses = reduce_update(
         grads.reshape(NSLOT, SLOT, 16, 128),
+        loss,
         flat,
-        first_moments.reshape(SHARD, 128),
-        second_moments.reshape(SHARD, 128),
+        first,
+        second,
         outer_momentum.reshape(SHARD, 128),
     )
+    averaged, momentum, new_weights, first, second = finish(averaged, momentum, new_weights, first, second)
     return (
         averaged.reshape(-1),
         momentum.reshape(-1),
         new_weights.reshape(-1),
-        first.reshape(1, -1),
-        second.reshape(1, -1),
-        lax.dynamic_slice(losses, (rep,), (1,)).reshape(1, 1),
+        first,
+        second,
+        losses[:1, :1],
     )
 
 

time: 365 us -> 490 us (1.34)
  Pallas kernels: 251 us -> 477 us
  blocking collectives: 64.4 us -> 0 us
  other arithmetic: 23.6 us -> 3.35 us
  local copies, waits for them, and re-layouts: 21.7 us -> 4.77 us
    pallas_call x3 -> x4, Pallas kernels: 251 us -> 477 us  [the longest x1 164 us: finish(): pl.pallas_call(flat_kernel, out_shape=(shape,) * 3 + (row,) * 2, in_specs...]
    psum x1 -> x0, blocking collectives: 64.4 us -> none  [body(): lax.psum(jnp.where(jnp.arange(4) == group, loss[0, 0], 0.0), ('rep', 'fsd...]
    unnamed x2 -> x0, other arithmetic: 22.2 us -> none
    unnamed x24 -> x5, local copies, waits for them, and re-layouts: 12.9 us -> 3.6 us
    reshape x1 -> x0, local copies, waits for them, and re-layouts: 6.99 us -> none  [body(): second.reshape(1, -1)]
where the time goes in v2:
time: 490 us; the launch traced here: 487 us
  Pallas kernels  477 us (97%)
    pallas_call x1, Pallas kernels, finish(): pl.pallas_call(flat_kernel, out_shape=(shape,) * 3 + (row,) * 2, in_specs...  164 us
    pallas_call x1, Pallas kernels, front(): pl.pallas_call(front_kernel, out_shape=(jax.ShapeDtypeStruct((NTILES, 16,...  162 us
    pallas_call x1, Pallas kernels, reduce_update(): pl.pallas_call(reduce_kernel, out_shape=(flat,) * 5 + (jax.ShapeDtypeStru...  85.7 us
    pallas_call x1, Pallas kernels, as_rows(): pl.pallas_call(rows_kernel, out_shape=(shape,) * 2, in_specs=[hbm] * 2, o...  66.2 us

profile of v2, /device:TPU:24, one launch (start us, length us, event | category | flops | bytes accessed | tf_op | source)
XLA Modules:
  0.0 486.8 jit_solution(14451072555568215271)
XLA Ops:
  0.6 1.3 reduce_sum.9
  2.6 0.7 fusion
  3.3 0.7 fusion.1
  3.9 0.7 convert_bitcast_fusion
  4.6 0.1 pad_maximum_fusion
  4.7 0.7 broadcast_in_dim.2.meta_ref
  5.3 2.0 copy.15
  7.3 66.2 %as_rows.1 = (f32[2098,128]{1,0:T(8,128)}, f32[2098,128]{1,0:T(8,128)}) custom-call(f32[1,268544]{1,0:T(1,128)} %one.1, f32[1,268544]{1,0:T(1,128)} %two.1), custom_call_target="tpu_custom_call" | custom-call | tf_op jit(solution)/shard_map/as_rows/pallas_call | solution.py:1081
  73.5 161.6 %front.1 = (bf16[4224,16,128]{2,1,0:T(8,128)(2,1)}, f32[8,128]{1,0:T(8,128)}) custom-call(f32[2098,128]{1,0:T(8,128)} %bitcast.16, bf16[2,196,768]{2,1,0:T(8,128)(2,1)} %bitcast.18, f32[8,128]{1,0:T(8,128)} %broadcast_in_dim.2.meta_ref), custom_call_target="tpu_custom_call" | custom-call | tf_op jit(solution)/shard_map/front/pallas_call | solution.py:597
  235.1 0.0 copy-start.1
  235.1 0.7 copy-done.1
  235.8 85.7 %reduce_update.1 = (f32[2098,128]{1,0:T(8,128)S(1)}, f32[2098,128]{1,0:T(8,128)}, f32[2098,128]{1,0:T(8,128)}, f32[2098,128]{1,0:T(8,128)}, f32[2098,128]{1,0:T(8,128)}, /*index=5*/f32[8,128]{1,0:T(8,128)S(1)}) custom-call(bf16[32,132,16,128]{3,2,1,0:T(8,128)(2,1)} %bitcast.15, f32[8,128]{1,0:T(8,128)S(1)} %copy-done.1, f32[2098,128]{1,0:T(8,128)} %bitcast.17, ...), custom_call_target="tpu_custom_call" | custom-call | tf_op jit(solution)/shard_map/reduce_update/pallas_call | solution.py:1028
  321.5 0.0 copy-start
  321.5 1.0 copy-done
  322.5 0.5 slice.3
  323.0 163.8 %finish.1 = (f32[2098,128]{1,0:T(8,128)}, f32[2098,128]{1,0:T(8,128)}, f32[2098,128]{1,0:T(8,128)}, f32[1,268544]{1,0:T(1,128)}, f32[1,268544]{1,0:T(1,128)}) custom-call(f32[2098,128]{1,0:T(8,128)} %copy-done, f32[2098,128]{1,0:T(8,128)} %get-tuple-element.26.refs_1_, f32[2098,128]{1,0:T(8,128)} %get-tuple-element.27.refs_2_, ...), custom_call_target="tpu_custom_call" | custom-call | tf_op jit(solution)/shard_map/finish/pallas_call | solution.py:1110
  (1 shorter events, 0.0 us)
Async XLA Ops:
  235.1 0.7 copy-start.1
  321.5 1.0 copy-start

commit v3 on v2

v3 whole, which is shorter than its diff:
```python
from functools import partial

import jax
import jax.numpy as jnp
from jax import lax
from jax.experimental import pallas as pl
from jax.experimental.pallas import tpu as pltpu
from jax.sharding import PartitionSpec as P

SHARD = 2098
SLOT = 132
HALF = 66
QUART = 33
NSLOT = 32
ROUNDS = 22
UNIT = 6
STAGES = ((0, 4), (4, 10), (10, 16), (16, 22))
SECTIONS = []
_t = 0
for _base, _c, _g, _rpg in ((0, 6, 61, 96), (5796, 8, 48, 125), (11796, 6, 1, 96), (11820, 18, 48, 288), (25644, 6, 48, 96), (30252, 24, 48, 384), (48684, 6, 192, 96)):
    SECTIONS.append((_base, _c, _g, _rpg, _t))
    _t += _c * _g
NTILE = _t
HI = 352
LO = 224
MARGIN = 512
FROWS = 3072
HEAD_ROWS = 16
MESH = pl.DeviceIdType.MESH


def coords():
    rep = lax.axis_index("rep")
    fs = lax.axis_index("fsdp")
    return lax.div(rep, 2), lax.rem(rep, 2), lax.div(fs, 8), lax.rem(lax.div(fs, 4), 2), lax.rem(fs, 4)


def device(xl, xh, core, z, y):
    return {"rep": xl * 2 + core, "fsdp": z * 8 + xh * 4 + y}


def flat_device(xl, core, s):
    return device(xl, lax.rem(lax.div(s, 4), 2), core, lax.div(s, 8), lax.rem(s, 4))


class Links:

    def __init__(self, T, R, RA, RB, g_send, g_recv, r_send, r_recv):
        self.xl, self.b, self.z, self.a, self.y = coords()
        self.T5 = T.reshape(ROUNDS, 4, 2, 4, UNIT, 16, 128)
        self.R, self.RA, self.RB = R, RA, RB
        self.g_send, self.g_recv, self.r_send, self.r_recv = g_send, g_recv, r_send, r_recv
        self.pending = []
        self.sibling = device(self.xl, self.a, 1 - self.b, self.z, self.y)

    def at_y(self, k):
        return device(self.xl, self.a, self.b, self.z, lax.rem(self.y + k, 4))

    def at_z(self, k):
        return device(self.xl, self.a, self.b, lax.rem(self.z + k, 4), self.y)

    def go(self, src, dst, send, recv, target):
        copy = pltpu.make_async_remote_copy(src_ref=src, dst_ref=dst, send_sem=send, recv_sem=recv, device_id=target, device_id_type=MESH)
        copy.start()
        self.pending.append(copy)

    def landed(self, dst, send, recv):
        pltpu.make_async_remote_copy(src_ref=dst, dst_ref=dst, send_sem=send, recv_sem=recv, device_id=self.sibling, device_id_type=MESH).wait_recv()

    def sent(self):
        for copy in self.pending:
            copy.wait_send()
        self.pending = []

    def span(self, i, h):
        lo, hi = STAGES[i]
        n = (hi - lo) // 2
        return pl.ds(lo + h * n, n)

    def first_axis(self, h, k):
        return (self.at_y if h == 0 else self.at_z)(k)

    def second_axis(self, h, k):
        return (self.at_z if h == 0 else self.at_y)(k)

    def one(self, i, h, k, q=None):
        rd = self.span(i, h)
        t = pl.ds(0, UNIT) if q is None else pl.ds(3 * q, 3)
        if h == 0:
            return self.T5.at[rd, self.z, self.b, lax.rem(self.y + k, 4), t]
        return self.T5.at[rd, lax.rem(self.z + k, 4), self.b, self.y, t]

    def row(self, i, h, k, core=None, p=None):
        rd = self.span(i, h)
        core = self.b if core is None else core
        t = pl.ds(0, 4) if p is None else pl.ds(2 * p, 2)
        if h == 0:
            return self.T5.at[rd, lax.rem(self.z + k, 4), core, t]
        return self.T5.at[rd, t, core, lax.rem(self.y + k, 4)]

    def gsem(self, i, h, k):
        n = (i * 2 + h) * 12 + k
        return self.g_send.at[n], self.g_recv.at[n]

    def gather_go(self, i, h, k, view, target):
        self.go(view, view, *self.gsem(i, h, k), target)

    def gather_wait(self, i, h, k, view):
        self.landed(view, *self.gsem(i, h, k))

    def gather_step(self, i, step):
        for h in range(2):
            if step == 0:
                self.gather_go(i, h, 0, self.one(i, h, 0), self.first_axis(h, 1))
                self.gather_go(i, h, 1, self.one(i, h, 0), self.first_axis(h, 3))
            elif step == 1:
                self.gather_wait(i, h, 0, self.one(i, h, 3))
                self.gather_go(i, h, 2, self.one(i, h, 3, 0), self.first_axis(h, 1))
                self.gather_wait(i, h, 1, self.one(i, h, 1))
                self.gather_go(i, h, 3, self.one(i, h, 1, 1), self.first_axis(h, 3))
            elif step == 2:
                self.gather_wait(i, h, 2, self.one(i, h, 2, 0))
                self.gather_wait(i, h, 3, self.one(i, h, 2, 1))
                self.gather_go(i, h, 4, self.row(i, h, 0), self.second_axis(h, 1))
                self.gather_go(i, h, 5, self.row(i, h, 0), self.second_axis(h, 3))
                self.gather_go(i, h, 8, self.row(i, h, 0), self.sibling)
            elif step == 3:
                self.gather_wait(i, h, 4, self.row(i, h, 3))
                self.gather_go(i, h, 6, self.row(i, h, 3, p=0), self.second_axis(h, 1))
                self.gather_go(i, h, 9, self.row(i, h, 3), self.sibling)
                self.gather_wait(i, h, 5, self.row(i, h, 1))
                self.gather_go(i, h, 7, self.row(i, h, 1, p=1), self.second_axis(h, 3))
                self.gather_go(i, h, 10, self.row(i, h, 1), self.sibling)
            elif step == 4:
                self.gather_wait(i, h, 6, self.row(i, h, 2, p=0))
                self.gather_wait(i, h, 7, self.row(i, h, 2, p=1))
                self.gather_go(i, h, 11, self.row(i, h, 2), self.sibling)
            else:
                for k, offset in ((8, 0), (9, 3), (10, 1), (11, 2)):
                    self.gather_wait(i, h, k, self.row(i, h, offset, core=1 - self.b))

    def rsem(self, i, h, k):
        n = (i * 2 + h) * 13 + k
        return self.r_send.at[n], self.r_recv.at[n]

    def cell(self, i, h, k, q):
        rd = self.span(i, h)
        t = pl.ds(3 * q, 3)
        if h == 0:
            return self.T5.at[rd, self.z, self.b, lax.rem(self.y + k, 4), t]
        return self.T5.at[rd, lax.rem(self.z + k, 4), self.b, self.y, t]

    def add(self, dst, *sources, inner=()):
        n = dst.shape[0]

        def one(r, carry):
            for k in range(inner) if inner else (None,):
                at = (r,) if k is None else (r, k)
                if len(sources) == 1:
                    dst[at] = dst[at] + sources[0][at]
                else:
                    total = dst[at].astype(jnp.float32)
                    for source in sources:
                        total = total + source[at].astype(jnp.float32)
                    dst[at] = total.astype(jnp.bfloat16)
            return carry

        lax.fori_loop(0, n, one, 0)

    def reduce_step(self, i, h, step):
        rd = self.span(i, h)
        T5 = self.T5

        def send_a(k, ka, p, shift):
            self.go(self.row(i, h, ka, p=p), self.RA.at[k, rd], *self.rsem(i, h, 1 + k), self.second_axis(h, shift))

        def wait_a(k):
            self.landed(self.RA.at[k, rd], *self.rsem(i, h, 1 + k))

        def send_b(k, kb, q, shift):
            self.go(self.cell(i, h, kb, q), self.RB.at[k, rd], *self.rsem(i, h, 7 + k), self.first_axis(h, shift))

        def wait_b(k):
            self.landed(self.RB.at[k, rd], *self.rsem(i, h, 7 + k))

        if step == 0:
            self.go(T5.at[rd, :, 1 - self.b], self.R.at[rd], *self.rsem(i, h, 0), self.sibling)
        elif step == 1:
            self.landed(self.R.at[rd], *self.rsem(i, h, 0))
            mine, theirs = T5.at[rd, :, self.b], self.R.at[rd]
            n = mine.shape[0]

            def both(r, carry):
                q = lax.div(r, 4)
                w = lax.rem(r, 4)
                for k in range(4):
                    mine[q, w, k] = mine[q, w, k] + theirs[q, w, k]
                return carry

            lax.fori_loop(0, 4 * n, both, 0)
            send_a(0, 2, 0, 1)
            send_a(1, 2, 1, 3)
            send_a(2, 1, 1, 1)
            send_a(3, 3, 0, 3)
        elif step == 2:
            wait_a(0)
            self.add(self.row(i, h, 1, p=0), self.RA.at[0, rd], inner=2)
            send_a(4, 1, 0, 1)
            wait_a(1)
            self.add(self.row(i, h, 3, p=1), self.RA.at[1, rd], inner=2)
            send_a(5, 3, 1, 3)
        elif step == 3:
            for k in (2, 3, 4, 5):
                wait_a(k)
            self.add(self.row(i, h, 0, p=0), self.RA.at[3, rd], self.RA.at[4, rd], inner=2)
            self.add(self.row(i, h, 0, p=1), self.RA.at[2, rd], self.RA.at[5, rd], inner=2)
            send_b(0, 2, 0, 1)
            send_b(1, 2, 1, 3)
            send_b(2, 1, 1, 1)
            send_b(3, 3, 0, 3)
        elif step == 4:
            wait_b(0)
            self.add(self.cell(i, h, 1, 0), self.RB.at[0, rd])
            send_b(4, 1, 0, 1)
            wait_b(1)
            self.add(self.cell(i, h, 3, 1), self.RB.at[1, rd])
            send_b(5, 3, 1, 3)
        else:
            for k in (2, 3, 4, 5):
                wait_b(k)
            self.add(self.cell(i, h, 0, 0), self.RB.at[3, rd], self.RB.at[4, rd])
            self.add(self.cell(i, h, 0, 1), self.RB.at[2, rd], self.RB.at[5, rd])


def start_gather(links, w_ref, patch_ref, meta_ref, T, patch_in, meta_in, flat, headrows, lob, hib, rlo, rhi, slot, local_sem, x_send, x_recv, u_send, u_recv):
    xl, b, z, a, y = links.xl, links.b, links.z, links.a, links.y
    fs = z * 8 + a * 4 + y
    swap = a != b
    xo = lax.rem(xl + a + b, 2)
    holder = z * 8 + b * 4 + y
    up = flat_device(xl, b, lax.rem(fs + 1, NSLOT))
    down = flat_device(xl, b, lax.rem(fs + NSLOT - 1, NSLOT))
    mirror = device(xl, b, a, z, y)
    load = pltpu.make_async_copy(w_ref, flat.at[pl.ds(MARGIN, SHARD)], local_sem.at[0])
    load.start()
    barrier = pltpu.get_barrier_semaphore()

    def greet(target):
        pl.semaphore_signal(barrier, inc=1, device_id=target, device_id_type=MESH)

    for target in (up, down, links.at_y(1), links.at_y(3), links.at_z(1), links.at_z(3), links.sibling):
        greet(target)

    @pl.when(swap)
    def _():
        greet(mirror)

    own_index = lax.rem(fs * 11, NSLOT)
    keeps = jnp.logical_and(a == b, own_index < ROUNDS)

    def greet_source(j, carry):
        s = lax.div(32 * j + holder, ROUNDS)
        sa = lax.rem(lax.div(s, 4), 2)

        @pl.when(jnp.logical_not(jnp.logical_and(keeps, s == fs)))
        def _():
            greet(device(lax.rem(xl + sa + a, 2), sa, a, lax.div(s, 8), lax.rem(s, 4)))

        return carry

    lax.fori_loop(0, ROUNDS, greet_source, 0)
    pl.semaphore_wait(barrier, 7 + ROUNDS + jnp.where(swap, 1, 0) - jnp.where(keeps, 1, 0))
    load.wait()

    def remote(src, dst, k, target):
        return pltpu.make_async_remote_copy(src_ref=src, dst_ref=dst, send_sem=x_send.at[k], recv_sem=x_recv.at[k], device_id=target, device_id_type=MESH)

    hib[...] = flat[pl.ds(MARGIN + SHARD - HI, HI), :].astype(jnp.bfloat16)
    to_up = remote(hib, rlo, 0, up)
    to_up.start()
    lob[...] = flat[pl.ds(MARGIN, LO), :].astype(jnp.bfloat16)
    to_down = remote(lob, rhi, 1, down)
    to_down.start()
    patch_swap = remote(patch_ref, patch_in, 2, mirror)
    meta_swap = remote(meta_ref, meta_in, 3, mirror)
    patch_keep = pltpu.make_async_copy(patch_ref, patch_in, local_sem.at[1])
    meta_keep = pltpu.make_async_copy(meta_ref, meta_in, local_sem.at[2])
    to_up.wait_recv()
    flat[pl.ds(MARGIN - HI, HI), :] = rlo[...].astype(jnp.float32)
    to_down.wait_recv()
    flat[pl.ds(MARGIN + SHARD, LO), :] = rhi[...].astype(jnp.float32)

    first = SLOT * fs
    origin = SHARD * fs - MARGIN
    for index, (base, c, groups, per, start) in enumerate(SECTIONS):
        lo = jnp.maximum(first, start)
        hi = jnp.minimum(first + SLOT, start + c * groups)
        if index == 1:
            lane = lax.broadcasted_iota(jnp.int32, (8, 128), 1)
            g0 = lax.div(jnp.maximum(lo, start) - start, 8)
            g1 = lax.div(jnp.maximum(hi, start) - start + 7, 8)

            def head_group(g, carry):
                row = base + per * g - origin
                for i in range(16):
                    q, s = divmod(1000 * i, 128)
                    one = flat[pl.ds(row + q, 8), :]
                    if s:
                        two = flat[pl.ds(row + q + 1, 8), :]
                        one = jnp.where(lane < 128 - s, pltpu.roll(one, 128 - s, 1), pltpu.roll(two, 128 - s, 1))
                    headrows[pl.ds(i * 8, 8), :] = one
                for j in range(8):
                    t = start + g * 8 + j - first

                    @pl.when(jnp.logical_and(t >= 0, t < SLOT))
                    def _():
                        slot[t] = headrows[pl.ds(j, 16, stride=8), :].astype(jnp.bfloat16)
                return carry

            lax.fori_loop(g0, g1, head_group, 0)
        else:

            def tile(t, carry):
                g = lax.div(t - start, c)
                j = lax.rem(t - start, c)
                row = base + 16 * c * g + j - origin
                slot[t - first] = flat[pl.ds(row, 16, stride=c), :].astype(jnp.bfloat16)
                return carry

            lax.fori_loop(lo, hi, tile, 0)
    pads = jnp.maximum(NTILE - first, 0)

    def blank(t, carry):
        slot[t] = jnp.zeros((16, 128), jnp.bfloat16)
        return carry

    lax.fori_loop(jnp.minimum(pads, SLOT), SLOT, blank, 0)


    def unit_copy(i):
        k = ROUNDS * fs + i
        d = lax.rem(k, 32)
        src = slot.at[pl.ds(UNIT * i, UNIT)]
        dst = T.at[pl.ds(UNIT * k, UNIT)]
        target = device(xo, b, lax.rem(lax.div(d, 4), 2), lax.div(d, 8), lax.rem(d, 4))
        mine = jnp.logical_and(keeps, i == own_index)
        away = pltpu.make_async_remote_copy(src_ref=src, dst_ref=dst, send_sem=u_send.at[i], recv_sem=u_recv.at[lax.div(k, 32)], device_id=target, device_id_type=MESH)
        here = pltpu.make_async_copy(src, dst, local_sem.at[3])
        return mine, away, here

    def send_unit(i, carry):
        mine, away, here = unit_copy(i)

        @pl.when(mine)
        def _():
            here.start()

        @pl.when(jnp.logical_not(mine))
        def _():
            away.start()

        return carry

    lax.fori_loop(0, ROUNDS, send_unit, 0)

    @pl.when(swap)
    def _():
        patch_swap.start()
        meta_swap.start()

    @pl.when(jnp.logical_not(swap))
    def _():
        patch_keep.start()
        meta_keep.start()

    def units_here(i):
        def wait(j, carry):
            place = T.at[pl.ds(UNIT * (32 * j + holder), UNIT)]
            mine = jnp.logical_and(keeps, lax.div(32 * j + holder, ROUNDS) == fs)

            @pl.when(mine)
            def _():
                pltpu.make_async_copy(place, place, local_sem.at[3]).wait()

            @pl.when(jnp.logical_not(mine))
            def _():
                pltpu.make_async_remote_copy(src_ref=place, dst_ref=place, send_sem=u_send.at[0], recv_sem=u_recv.at[j], device_id=links.sibling, device_id_type=MESH).wait_recv()

            return carry

        lax.fori_loop(*STAGES[i], wait, 0)

    def finish_start():
        def wait(i, carry):
            mine, away, here = unit_copy(i)

            @pl.when(jnp.logical_not(mine))
            def _():
                away.wait_send()

            return carry

        lax.fori_loop(0, ROUNDS, wait, 0)
        to_up.wait_send()
        to_down.wait_send()

        @pl.when(swap)
        def _():
            patch_swap.wait()
            meta_swap.wait()

        @pl.when(jnp.logical_not(swap))
        def _():
            patch_keep.wait()
            meta_keep.wait()

    return units_here, finish_start


D = 768
HEADS = 12
HEAD_DIM = 64
FF = 3072
CLS = 1000
P_SIZE = 196
ROWS = 208
TOK = 2 * ROWS
NORM_EPS = 1e-06
SMOOTHING = 0.1
NTILES = 4224
T_E, T_HEAD, T_NORM, T_QKV, T_OUT, T_IN, T_FO = 0, 366, 750, 756, 1620, 1908, 3060
T_POS = 288
BLK = 256
STEP_ROWS = 32
F32 = jnp.float32
BF16 = jnp.bfloat16
ROOT_HALF = 0.7071067811865476
INV_ROOT_TWO_PI = 0.3989422804014327


def dot(x, w):
    return lax.dot_general(x, w, (((1,), (0,)), ((), ())), preferred_element_type=F32)


def dot_t(x, w):
    return lax.dot_general(x, w, (((1,), (1,)), ((), ())), preferred_element_type=F32)


def t_dot(x, w):
    return lax.dot_general(x, w, (((0,), (0,)), ((), ())), preferred_element_type=F32)


def stats(x):
    mean = jnp.sum(x, -1, keepdims=True) * (1.0 / D)
    centred = x - mean
    var = jnp.sum(centred * centred, -1, keepdims=True) * (1.0 / D)
    rstd = lax.rsqrt(var + NORM_EPS)
    return centred * rstd, rstd


def norm_back(d_hat, hat, rstd):
    m1 = jnp.sum(d_hat, -1, keepdims=True) * (1.0 / D)
    m2 = jnp.sum(d_hat * hat, -1, keepdims=True) * (1.0 / D)
    return rstd * (d_hat - m1 - hat * m2)


def compute(step, patch_ref, meta_ref, loss_ref, T, x, h, a, at, mix, prob, o, h1, a2, hid, slope, h2, dh, dyb):
    G = T
    dmix = mix

    def section(ref, start, c, groups):
        return ref.at[pl.ds(start, groups * c)].reshape(groups, c, 16, 128)

    def cols(start, c, groups, j):
        part = section(T, start, c, groups)
        return jnp.concatenate([part[:, 2 * j + k].reshape(groups * 16, 128) for k in range(2)], axis=1)

    def put_cols(start, c, groups, j, value):
        low = value.astype(BF16)
        part = section(G, start, c, groups)
        for k in range(2):
            part[:, 2 * j + k] = low[:, k * 128 : (k + 1) * 128].reshape(groups, 16, 128)

    def row_of(start, k):
        return jnp.concatenate([T[start + j][k : k + 1, :] for j in range(6)], axis=1).astype(F32)

    def lanes(j):
        return pl.ds(pl.multiple_of(j * BLK, BLK), BLK)

    def rows(i):
        return pl.ds(pl.multiple_of(i * STEP_ROWS, STEP_ROWS), STEP_ROWS)

    steps = TOK // STEP_ROWS
    step("start")
    for i in range(2):
        x[pl.ds(i * ROWS, 192), :] = patch_ref[i, pl.ds(0, 192), :]
        x[pl.ds(i * ROWS + 192, 16), :] = jnp.concatenate([patch_ref[i, pl.ds(192, 4), :], jnp.zeros((12, D), BF16)], axis=0)

    real = lax.broadcasted_iota(jnp.int32, (ROWS, 128), 0) < P_SIZE
    for j in range(3):
        acc = dot(x[...], cols(T_E, 6, 48, j))
        p = cols(T_POS, 6, 13, j).astype(F32)
        p = jnp.where(lax.broadcasted_iota(jnp.int32, (ROWS, BLK), 0) < P_SIZE, p, 0.0)
        for i in range(2):
            h[pl.ds(i * ROWS, ROWS), pl.ds(j * BLK, BLK)] = acc[i * ROWS : (i + 1) * ROWS] + p

    step("embedded")
    gain1, shift1, gain2, shift2 = (row_of(T_NORM, k) for k in range(4))

    def norm_one(i, carry):
        hat, unused = stats(h[rows(i), :])
        a[rows(i), :] = (hat * gain1 + shift1).astype(BF16)
        return carry

    lax.fori_loop(0, steps, norm_one, 0)

    step("qkv")
    def mix_block(j, carry):
        mix[:, lanes(j)] = dot(a[...], cols(T_QKV, 18, 48, j)).astype(BF16)
        return carry

    lax.fori_loop(0, 9, mix_block, 0)

    first_half = lax.broadcasted_iota(jnp.int32, (ROWS, 128), 1) < HEAD_DIM
    key_ok = lax.broadcasted_iota(jnp.int32, (ROWS, ROWS), 1) < P_SIZE
    zero = jnp.zeros((ROWS, 128), BF16)

    def qkv_of(n):
        i = lax.div(n, 6)
        p = lax.rem(n, 6)
        r = pl.ds(pl.multiple_of(i * ROWS, ROWS), ROWS)
        ls = [pl.ds(pl.multiple_of(p * 128 + D * k, 128), 128) for k in range(3)]
        return r, ls

    def attend(n, carry):
        r, ls = qkv_of(n)
        q, k, v = (mix[r, l] for l in ls)
        q = q * jnp.asarray(0.125, BF16)
        outs = []
        for e in range(2):
            mask = first_half if e == 0 else jnp.logical_not(first_half)
            s = dot_t(jnp.where(mask, q, zero), k)
            s = jnp.where(key_ok, s, -jnp.inf)
            top = jnp.max(s, -1, keepdims=True)
            ex = jnp.exp(s - top)
            pr = (ex / jnp.sum(ex, -1, keepdims=True)).astype(BF16)
            prob[n * 2 + e] = pr
            outs.append(dot(pr, v))
        o[r, ls[0]] = jnp.where(first_half, outs[0], outs[1]).astype(BF16)
        return carry

    for part in range(4):
        step("attend%d" % part)
        lax.fori_loop(3 * part, 3 * part + 3, attend, 0)
    step("attended")
    for j in range(3):
        h1[:, pl.ds(j * BLK, BLK)] = h[:, pl.ds(j * BLK, BLK)] + dot(o[...], cols(T_OUT, 6, 48, j))

    def norm_two(i, carry):
        hat, unused = stats(h1[rows(i), :])
        a2[rows(i), :] = (hat * gain2 + shift2).astype(BF16)
        return carry

    lax.fori_loop(0, steps, norm_two, 0)

    step("up")
    def up_block(j, carry):
        u = dot(a2[...], cols(T_IN, 24, 48, j))
        phi = 0.5 * (1.0 + lax.erf(u * ROOT_HALF))
        pdf = jnp.exp(-0.5 * u * u) * INV_ROOT_TWO_PI
        hid[:, lanes(j)] = (u * phi).astype(BF16)
        slope[:, lanes(j)] = (phi + u * pdf).astype(BF16)
        return carry

    lax.fori_loop(0, 12, up_block, 0)
    step("down")
    for j in range(3):
        h2[:, pl.ds(j * BLK, BLK)] = h1[:, pl.ds(j * BLK, BLK)] + dot(hid[...], cols(T_FO, 6, 192, j))

    step("pool")
    gain_end, shift_end = (row_of(T_POS + 72, 4 + k) for k in range(2))
    means = []
    for i in range(2):

        def pool_step(n, carry):
            hat, unused = stats(h2[pl.ds(pl.multiple_of(i * ROWS + n * 16, 16), 16), :])
            ok = lax.broadcasted_iota(jnp.int32, (16, D), 0) + n * 16 < P_SIZE
            hat = jnp.where(ok, hat, 0.0)
            return carry + hat[:8] + hat[8:]

        total = lax.fori_loop(0, 13, pool_step, jnp.zeros((8, D), F32))
        means.append(jnp.sum(total, 0, keepdims=True) * (1.0 / P_SIZE))
    mean_hat = jnp.concatenate(means + [jnp.zeros((14, D), F32)], axis=0)
    two = lax.broadcasted_iota(jnp.int32, (16, D), 0) < 2
    pooled = jnp.where(two, mean_hat * gain_end + shift_end, 0.0).astype(BF16)
    logits = jnp.concatenate([dot(pooled, cols(T_HEAD, 8, 48, j)) for j in range(4)], axis=1)
    lane = lax.broadcasted_iota(jnp.int32, (16, 1024), 1)
    lane_f = lane.astype(F32)
    inside = lane < CLS
    logits = jnp.where(inside, logits, -1e30)
    top = jnp.max(logits, -1, keepdims=True)
    total = jnp.sum(jnp.where(inside, jnp.exp(logits - top), 0.0), -1, keepdims=True)
    logp = logits - top - jnp.log(total)
    meta = meta_ref[...]
    pad14 = jnp.zeros((14, 1), F32)
    label = jnp.concatenate([meta[0:2, 0:1], pad14], axis=0)
    scale = jnp.concatenate([meta[2:4, 0:1], pad14], axis=0)
    valid = jnp.concatenate([meta[4:6, 0:1], pad14], axis=0)
    target = jnp.where(lane_f == label, 1.0 - SMOOTHING, 0.0) + SMOOTHING / CLS
    values = -jnp.sum(jnp.where(inside, target * logp, 0.0), -1, keepdims=True)
    loss_ref[...] = jnp.broadcast_to(jnp.sum(values * valid, 0, keepdims=True), (8, 128))
    d_logits = jnp.where(inside, scale * (jnp.exp(logp) - target), 0.0).astype(BF16)
    d_pooled = jnp.zeros((16, D), F32)
    for j in range(4):
        w = cols(T_HEAD, 8, 48, j)
        d_pooled = d_pooled + dot_t(d_logits[:, j * BLK : (j + 1) * BLK], w)
        put_cols(T_HEAD, 8, 48, j, t_dot(pooled, d_logits[:, j * BLK : (j + 1) * BLK]))
    d_gain_end = jnp.sum(d_pooled * mean_hat, 0, keepdims=True)
    d_shift_end = jnp.sum(d_pooled, 0, keepdims=True)
    for i in range(2):
        d_hat = d_pooled[i : i + 1, :] * (1.0 / P_SIZE) * gain_end

        def end_step(n, carry):
            r = pl.ds(pl.multiple_of(i * ROWS + n * 16, 16), 16)
            hat, rstd = stats(h2[r, :])
            ok = lax.broadcasted_iota(jnp.int32, (16, D), 0) + n * 16 < P_SIZE
            d = jnp.where(ok, norm_back(jnp.broadcast_to(d_hat, (16, D)), hat, rstd), 0.0)
            dh[r, :] = d
            dyb[r, :] = d.astype(BF16)
            return carry

        lax.fori_loop(0, 13, end_step, 0)

    step("backward")
    at[...] = a2[...].T
    da = h2

    def down_block(j, carry):
        dy = dyb[...]
        d_w = t_dot(hid[:, lanes(j)], dy).astype(BF16)
        part = section(T, T_FO + j * 96, 6, 16)
        w = jnp.concatenate([part[:, k].reshape(BLK, 128) for k in range(6)], axis=1)
        hid[:, lanes(j)] = (dot_t(dy, w) * slope[:, lanes(j)].astype(F32)).astype(BF16)
        for k in range(6):
            part[:, k] = d_w[:, k * 128 : (k + 1) * 128].reshape(16, 16, 128)
        return carry

    G[pl.ds(4212, 12)] = jnp.zeros((12, 16, 128), BF16)
    lax.fori_loop(0, 8, down_block, 0)
    step("fc_out0")
    lax.fori_loop(8, 12, down_block, 0)
    step("fc_out1")
    da[...] = jnp.zeros((TOK, D), F32)

    def up_back(j, carry):
        d_u = hid[:, lanes(j)]
        da[...] += dot_t(d_u, cols(T_IN, 24, 48, j))
        put_cols(T_IN, 24, 48, j, dot(at[...], d_u))
        return carry

    for part in range(4):
        lax.fori_loop(3 * part, 3 * part + 3, up_back, 0)
        step("fc_in%d" % part)

    def back_two(i, carry):
        dg, ds = carry
        hat, rstd = stats(h1[rows(i), :])
        d = da[rows(i), :]
        new = dh[rows(i), :] + norm_back(d * gain2, hat, rstd)
        dh[rows(i), :] = new
        dyb[rows(i), :] = new.astype(BF16)
        return dg + jnp.sum((d * hat).reshape(4, 8, D), 0), ds + jnp.sum(d.reshape(4, 8, D), 0)

    none = jnp.zeros((8, D), F32)
    d_gain2, d_shift2 = lax.fori_loop(0, steps, back_two, (none, none))

    step("normed2")
    at[...] = o[...].T
    da[...] = jnp.zeros((TOK, D), F32)
    for j in range(3):
        dz = dyb[:, pl.ds(j * BLK, BLK)]
        da[...] += dot_t(dz, cols(T_OUT, 6, 48, j))
        put_cols(T_OUT, 6, 48, j, dot(at[...], dz))
    o[...] = da[...].astype(BF16)

    step("out")
    def attend_back(n, carry):
        r, ls = qkv_of(n)
        q, k, v = (mix[r, l] for l in ls)
        q = q * jnp.asarray(0.125, BF16)
        k8 = k * jnp.asarray(0.125, BF16)
        do = o[r, ls[0]]
        dq, dk, dv = [], [], []
        for e in range(2):
            mask = first_half if e == 0 else jnp.logical_not(first_half)
            pr = prob[n * 2 + e]
            dv.append(t_dot(pr, do))
            dp = dot_t(jnp.where(mask, do, zero), v)
            prf = pr.astype(F32)
            row = jnp.sum(prf * dp, -1, keepdims=True)
            ds = (prf * (dp - row)).astype(BF16)
            dq.append(dot(ds, k8))
            dk.append(t_dot(ds, q))
        for l, pair in zip(ls, (dq, dk, dv)):
            dmix[r, l] = jnp.where(first_half, pair[0], pair[1]).astype(BF16)
        return carry

    for part in range(4):
        lax.fori_loop(3 * part, 3 * part + 3, attend_back, 0)
        step("back%d" % part)

    at[...] = a[...].T
    da[...] = jnp.zeros((TOK, D), F32)

    def qkv_block(j, carry):
        d = dmix[:, lanes(j)]
        da[...] += dot_t(d, cols(T_QKV, 18, 48, j))
        put_cols(T_QKV, 18, 48, j, dot(at[...], d))
        return carry

    lax.fori_loop(0, 9, qkv_block, 0)

    step("qkv_back")
    def back_one(i, carry):
        dg, ds = carry
        hat, rstd = stats(h[rows(i), :])
        d = da[rows(i), :]
        new = dh[rows(i), :] + norm_back(d * gain1, hat, rstd)
        dh[rows(i), :] = new
        dyb[rows(i), :] = new.astype(BF16)
        return dg + jnp.sum((d * hat).reshape(4, 8, D), 0), ds + jnp.sum(d.reshape(4, 8, D), 0)

    d_gain1, d_shift1 = lax.fori_loop(0, steps, back_one, (none, none))
    d_norms = jnp.concatenate([jnp.sum(d, 0, keepdims=True) for d in (d_gain1, d_shift1, d_gain2, d_shift2)] + [jnp.zeros((12, D), F32)], axis=0).astype(BF16)
    for j in range(6):
        G[T_NORM + j] = d_norms[:, j * 128 : (j + 1) * 128]
    step("norms")
    at[...] = x[...].T
    row_id = lax.broadcasted_iota(jnp.int32, (ROWS, BLK), 0)
    for j in range(3):
        put_cols(T_E, 6, 48, j, dot(at[...], dyb[:, pl.ds(j * BLK, BLK)]))
        c = pl.ds(j * BLK, BLK)
        s = slice(j * BLK, (j + 1) * BLK)
        d_pos = dh[pl.ds(0, ROWS), c] + dh[pl.ds(ROWS, ROWS), c]
        d_pos = jnp.where(row_id < P_SIZE, d_pos, 0.0)
        d_pos = jnp.where(row_id == P_SIZE, jnp.broadcast_to(d_gain_end[:, s], (ROWS, BLK)), d_pos)
        d_pos = jnp.where(row_id == P_SIZE + 1, jnp.broadcast_to(d_shift_end[:, s], (ROWS, BLK)), d_pos)
        put_cols(T_POS, 6, 13, j, d_pos)
    step("embed")


FORWARD = {
    "start": ((0, 0), (1, 0), (0, 1), (0, 2), (1, 1), (2, 0), (0, 3), (1, 2), (0, 4), (2, 1), (3, 0), (0, 5)),
    "embedded": ((1, 3), (2, 2), (3, 1)),
    "qkv": ((1, 4), (1, 5), (3, 2)),
    "attend0": ((2, 3),),
    "attend1": ((3, 3), (2, 4)),
    "attend2": ((3, 4),),
    "up": ((2, 5),),
    "down": ((3, 5),),
}
BACKWARD = {
    "fc_out0": ((3, 0, 0),),
    "fc_out1": ((3, 1, 0), (3, 0, 1)),
    "fc_in0": ((3, 1, 1),),
    "fc_in1": ((3, 0, 2),),
    "fc_in2": ((3, 1, 2), (3, 0, 3)),
    "fc_in3": ((2, 0, 0), (2, 1, 0), (3, 1, 3)),
    "normed2": ((3, 0, 4), (3, 1, 4), (2, 0, 1)),
    "out": ((2, 1, 1), (3, 0, 5)),
    "back0": ((2, 0, 2), (2, 1, 2), (3, 1, 5)),
    "back1": ((2, 0, 3), (2, 1, 3)),
    "back2": ((2, 0, 4), (2, 1, 4)),
    "back3": ((2, 0, 5), (2, 1, 5)),
    "qkv_back": ((1, 0, 0), (1, 1, 0)),
    "norms": ((0, 1, 0), (1, 0, 1), (1, 1, 1)),
    "embed": ((0, 0, 0), (0, 1, 1), (1, 0, 2), (1, 1, 2), (0, 0, 1), (1, 0, 3), (1, 1, 3), (0, 1, 2), (0, 0, 2), (1, 0, 4), (1, 1, 4), (0, 1, 3), (0, 0, 3), (1, 0, 5), (1, 1, 5), (0, 1, 4), (0, 0, 4), (0, 1, 5), (0, 0, 5)),
}


def grads_kernel(w_ref, patch_ref, meta_ref, red_ref, loss_out, T, R, RA, RB, g_send, g_recv, r_send, r_recv, LS, l_send, l_recv, patch_in, meta_in, loss, *rest):
    gather_refs, compute_refs, out_sem = rest[:12], rest[12:-1], rest[-1]
    links = Links(T, R, RA, RB, g_send, g_recv, r_send, r_recv)
    xl, b, z, a, y = links.xl, links.b, links.z, links.a, links.y
    swap = a != b
    mirror = device(xl, b, a, z, y)
    units_here, finish_start = start_gather(links, w_ref, patch_ref, meta_ref, T, patch_in, meta_in, *gather_refs)

    def loss_send(src, dst, target):
        links.go(LS.at[src], LS.at[dst], l_send.at[dst], l_recv.at[dst], target)

    def loss_wait(*slots):
        for k in slots:
            links.landed(LS.at[k], l_send.at[k], l_recv.at[k])

    def loss_step(n):
        if n == 0:
            LS[0] = loss[...]
            loss_send(0, 1, links.sibling)
        elif n == 1:
            loss_wait(1)
            LS[8] = LS[0] + LS[1]
            loss_send(8, 2, links.at_y(1))
            loss_send(8, 3, links.at_y(3))
        elif n == 2:
            loss_wait(2, 3)
            loss_send(2, 4, links.at_y(1))
        elif n == 3:
            loss_wait(4)
            LS[9] = (LS[8] + LS[4]) + (LS[2] + LS[3])
            loss_send(9, 5, links.at_z(1))
            loss_send(9, 6, links.at_z(3))
        elif n == 4:
            loss_wait(5, 6)
            loss_send(5, 7, links.at_z(1))
        elif n == 5:
            loss_wait(7)
            LS[10] = (LS[9] + LS[7]) + (LS[5] + LS[6])

            @pl.when(swap)
            def _():
                loss_swap.start()

        else:

            @pl.when(swap)
            def _():
                loss_swap.wait()
                loss_out[...] = LS[11]

            @pl.when(jnp.logical_not(swap))
            def _():
                loss_out[...] = LS[10]

    loss_swap = pltpu.make_async_remote_copy(src_ref=LS.at[10], dst_ref=LS.at[11], send_sem=l_send.at[11], recv_sem=l_recv.at[11], device_id=mirror, device_id_type=MESH)
    losses = {"fc_out0": 0, "fc_in0": 1, "fc_in2": 2, "normed2": 3, "back0": 4, "back2": 5, "qkv_back": 6}

    def step(name):
        if name == "pool":
            links.sent()
        for item in FORWARD.get(name, ()):
            if item[1] == 0:
                units_here(item[0])
            links.gather_step(*item)
        if name == "start":
            finish_start()
        for item in BACKWARD.get(name, ()):
            links.reduce_step(*item)
        if name in losses:
            loss_step(losses[name])

    compute(step, patch_in, meta_in, loss, T, *compute_refs)
    mine = T.reshape(ROUNDS, 32, UNIT, 16, 128).at[:, z * 8 + b * 4 + y]
    out = pltpu.make_async_copy(mine, red_ref, out_sem)
    out.start()
    links.sent()
    out.wait()


def grads(weights, patches, meta):
    hbm = pl.BlockSpec(memory_space=pl.ANY)
    vmem = pl.BlockSpec(memory_space=pltpu.VMEM)
    V = pltpu.VMEM
    dma = pltpu.SemaphoreType.DMA
    return pl.pallas_call(
        grads_kernel,
        out_shape=(jax.ShapeDtypeStruct((ROUNDS, UNIT, 16, 128), BF16), jax.ShapeDtypeStruct((8, 128), F32)),
        in_specs=[hbm] * 3,
        out_specs=(hbm, vmem),
        scratch_shapes=[
            V((NTILES, 16, 128), BF16),
            V((ROUNDS, 4, 4, UNIT, 16, 128), BF16),
            V((6, ROUNDS, 2, UNIT, 16, 128), BF16),
            V((6, ROUNDS, 3, 16, 128), BF16),
            dma((96,)),
            dma((96,)),
            dma((104,)),
            dma((104,)),
            V((12, 8, 128), F32),
            dma((12,)),
            dma((12,)),
            V(patches.shape, BF16),
            V((8, 128), F32),
            V((8, 128), F32),
            V((FROWS, 128), F32),
            V((128, 128), F32),
            V((LO, 128), BF16),
            V((HI, 128), BF16),
            V((HI, 128), BF16),
            V((LO, 128), BF16),
            V((SLOT, 16, 128), BF16),
            dma((4,)),
            dma((4,)),
            dma((4,)),
            dma((ROUNDS,)),
            dma((ROUNDS,)),
            V((TOK, D), BF16),
            V((TOK, D), F32),
            V((TOK, D), BF16),
            V((D, TOK), BF16),
            V((TOK, 3 * D), BF16),
            V((24, ROWS, ROWS), BF16),
            V((TOK, D), BF16),
            V((TOK, D), F32),
            V((TOK, D), BF16),
            V((TOK, FF), BF16),
            V((TOK, FF), BF16),
            V((TOK, D), F32),
            V((TOK, D), F32),
            V((TOK, D), BF16),
            dma,
        ],
        compiler_params=pltpu.CompilerParams(collective_id=0, has_side_effects=True, vmem_limit_bytes=60 * 1024 * 1024),
        name="grads",
    )(weights, patches, meta)


EDGE = 24
FRONT = 768
BACK_ROWS = FRONT + SHARD + 640 + 6
PADDED = 2112
STEP = 10
EDGE_UNITS = 4
WINDOW = ROUNDS + 2 * EDGE_UNITS
BETA_ONE = 0.9
BETA_TWO = 0.95
ADAM_EPS = 1e-08
DECAY = 0.05
INNER_RATE = 0.01
OUTER_RATE = 0.7
OUTER_MU = 0.9


def update_kernel(
    red_ref, w_ref, first_ref, second_ref, mom_ref,
    avg_out, mom_out, new_out, first_out, second_out,
    red, window, flat, headrows, w, first, second, mom, upd, low, low2, pair, pair2, total, total2,
    load_sem, x_send, x_recv, o_send, e_send, w_recv,
):
    xl, b, z, a, y = coords()
    fs = z * 8 + a * 4 + y
    holder = z * 8 + b * 4 + y
    sibling = device(xl, a, 1 - b, z, y)
    across = device(1 - xl, a, b, z, y)
    extra = [pltpu.make_async_copy(src, dst, load_sem.at[i]) for i, (src, dst) in enumerate(((w_ref, w), (first_ref, first), (second_ref, second), (mom_ref, mom)))]
    load = pltpu.make_async_copy(red_ref, red, load_sem.at[4])
    load.start()
    for copy in extra:
        copy.start()

    barrier = pltpu.get_barrier_semaphore()

    def greet(target):
        pl.semaphore_signal(barrier, inc=1, device_id=target, device_id_type=MESH)

    greet(sibling)
    greet(across)
    first_unit = ROUNDS * fs - EDGE_UNITS

    def window_unit(p):
        k = first_unit + p
        d = lax.rem(k + 32, 32)
        inside = jnp.logical_and(k >= 0, k < 32 * ROUNDS)
        mine = jnp.logical_and(a == b, d == holder)
        return inside, mine, device(xl, b, lax.rem(lax.div(d, 4), 2), lax.div(d, 8), lax.rem(d, 4))

    def greet_holder(p, carry):
        inside, mine, source = window_unit(p)

        @pl.when(jnp.logical_and(inside, jnp.logical_not(mine)))
        def _():
            greet(source)

        return carry

    lax.fori_loop(0, WINDOW, greet_holder, 0)

    def held_unit(j):
        k = 32 * j + holder
        q = lax.div(k, ROUNDS)
        r = lax.rem(k, ROUNDS)
        shift = jnp.where(r < EDGE_UNITS, -1, jnp.where(r >= ROUNDS - EDGE_UNITS, 1, 0))
        near = jnp.logical_and(shift != 0, jnp.logical_and(q + shift >= 0, q + shift < NSLOT))
        return k, q, jnp.where(near, q + shift, q), near

    def to_owner(j, k, s, send):
        p = k - (ROUNDS * s - EDGE_UNITS)
        src = red.at[j]
        dst = window.at[pl.ds(UNIT * p, UNIT)]
        sa = lax.rem(lax.div(s, 4), 2)
        mine = jnp.logical_and(a == b, s == fs)
        target = device(xl, sa, a, lax.div(s, 8), lax.rem(s, 4))
        away = pltpu.make_async_remote_copy(src_ref=src, dst_ref=dst, send_sem=send.at[j], recv_sem=w_recv.at[p], device_id=target, device_id_type=MESH)
        here = pltpu.make_async_copy(src, dst, load_sem.at[10])
        return mine, away, here

    def count(j, n):
        k, q, s, near = held_unit(j)
        first_away = jnp.logical_not(jnp.logical_and(a == b, q == fs))
        second_away = jnp.logical_and(near, jnp.logical_not(jnp.logical_and(a == b, s == fs)))
        return n + jnp.where(first_away, 1, 0) + jnp.where(second_away, 1, 0)

    outgoing = lax.fori_loop(0, ROUNDS, count, 2)
    pl.semaphore_wait(barrier, outgoing)
    load.wait()

    def give(j, carry):
        k, q, s, near = held_unit(j)
        mine, away, here = to_owner(j, k, q, o_send)

        @pl.when(mine)
        def _():
            here.start()

        @pl.when(jnp.logical_not(mine))
        def _():
            away.start()

        mine2, away2, here2 = to_owner(j, k, s, e_send)

        @pl.when(jnp.logical_and(near, mine2))
        def _():
            here2.start()

        @pl.when(jnp.logical_and(near, jnp.logical_not(mine2)))
        def _():
            away2.start()

        return carry

    lax.fori_loop(0, ROUNDS, give, 0)

    def given(j, carry):
        k, q, s, near = held_unit(j)
        mine, away, here = to_owner(j, k, q, o_send)

        @pl.when(jnp.logical_not(mine))
        def _():
            away.wait_send()

        mine2, away2, here2 = to_owner(j, k, s, e_send)

        @pl.when(jnp.logical_and(near, jnp.logical_not(mine2)))
        def _():
            away2.wait_send()

        return carry

    def clear(i, carry):
        flat[pl.ds(pl.multiple_of(i * 32, 32), 32), :] = jnp.zeros((32, 128), F32)
        return carry

    lax.fori_loop(0, BACK_ROWS // 32, clear, 0)

    def got(p, carry):
        inside, mine, source = window_unit(p)
        place = window.at[pl.ds(UNIT * p, UNIT)]

        @pl.when(jnp.logical_and(inside, mine))
        def _():
            pltpu.make_async_copy(place, place, load_sem.at[10]).wait()

        @pl.when(jnp.logical_and(inside, jnp.logical_not(mine)))
        def _():
            pltpu.make_async_remote_copy(src_ref=place, dst_ref=place, send_sem=x_send.at[0], recv_sem=w_recv.at[p], device_id=sibling, device_id_type=MESH).wait_recv()

        return carry

    lax.fori_loop(0, WINDOW, got, 0)
    for copy in extra:
        copy.wait()
    sends = []

    def go(src, dst, send, recv, k, target):
        copy = pltpu.make_async_remote_copy(src_ref=src, dst_ref=dst, send_sem=send.at[k], recv_sem=recv.at[k], device_id=target, device_id_type=MESH)
        copy.start()
        sends.append(copy)

    def arrive(dst, recv, k):
        pltpu.make_async_remote_copy(src_ref=dst, dst_ref=dst, send_sem=x_send.at[k], recv_sem=recv.at[k], device_id=sibling, device_id_type=MESH).wait_recv()

    low_tile = SLOT * fs - EDGE
    high_tile = SLOT * fs + SLOT + EDGE
    origin = SHARD * fs - FRONT
    for index, (base, c, groups, per, start) in enumerate(SECTIONS):
        if index == 1:
            lane = lax.broadcasted_iota(jnp.int32, (8, 128), 1)
            g0 = lax.div(jnp.maximum(SHARD * fs - base, 0), per)
            g1 = lax.div(jnp.maximum(SHARD * (fs + 1) - base, 0) + per - 1, per)

            def head_group(g, carry):
                t = start + g * 8 - low_tile
                for j in range(8):
                    headrows[pl.ds(j, 16, stride=8), :] = window[t + j].astype(F32)
                row = base + per * g - origin
                for i in range(16):
                    q, s = divmod(1000 * i, 128)
                    value = headrows[pl.ds(i * 8, 8), :]
                    if s:
                        value = pltpu.roll(value, s, 1)
                        flat[pl.ds(row + q, 8), :] += jnp.where(lane >= s, value, 0.0)
                        flat[pl.ds(row + q + 1, 8), :] += jnp.where(lane < s, value, 0.0)
                    else:
                        flat[pl.ds(row + q, 8), :] += value
                return carry

            lax.fori_loop(jnp.minimum(g0, groups), jnp.minimum(g1, groups), head_group, 0)
        else:

            def tile(t, carry):
                g = lax.div(t - start, c)
                j = lax.rem(t - start, c)
                flat[pl.ds(base + 16 * c * g + j - origin, 16, stride=c), :] = window[t - low_tile].astype(F32)
                return carry

            lax.fori_loop(jnp.maximum(low_tile, start), jnp.minimum(high_tile, start + c * groups), tile, 0)

    fix_one = 1.0 / (1.0 - BETA_ONE**STEP)
    fix_two = 1.0 / (1.0 - BETA_TWO**STEP)

    def in_rows(fn, lo, hi, step=32):
        def body(i, carry):
            fn(pl.multiple_of(i * step, step), step)
            return carry

        n = (hi - lo) // step
        lax.fori_loop(lo // step, lo // step + n, body, 0)
        if lo + n * step < hi:
            fn(lo + n * step, hi - lo - n * step)

    def adam(r, n):
        grad = flat[pl.ds(FRONT + r, n), :]
        m = BETA_ONE * first[pl.ds(r, n), :] + (1.0 - BETA_ONE) * grad
        s = BETA_TWO * second[pl.ds(r, n), :] + (1.0 - BETA_TWO) * grad * grad
        first[pl.ds(r, n), :] = m
        second[pl.ds(r, n), :] = s
        u = (m * fix_one) / (jnp.sqrt(s * fix_two) + ADAM_EPS)
        upd[pl.ds(r, n), :] = u

    in_rows(adam, 0, SHARD)
    upd[pl.ds(SHARD, PADDED - SHARD), :] = jnp.zeros((PADDED - SHARD, 128), F32)
    outs = [pltpu.make_async_copy(src, dst, load_sem.at[5 + i]) for i, (src, dst) in enumerate(((first, first_out), (second, second_out)))]
    for copy in outs:
        copy.start()

    def lower(r, n):
        low[pl.ds(r, n), :] = upd[pl.ds(r, n), :].astype(BF16)

    in_rows(lower, 0, PADDED)
    go(low, low2, x_send, x_recv, 0, sibling)
    arrive(low2, x_recv, 0)
    half = PADDED // 2

    def pairs(r, n):
        at = pl.ds(pl.multiple_of(b * half + r, 16), n)
        pair[pl.ds(r, n), :] = low[at, :] + low2[at, :]

    in_rows(pairs, 0, half)
    go(pair, pair2, x_send, x_recv, 1, across)
    arrive(pair2, x_recv, 1)

    def fours(r, n):
        total[pl.ds(r, n), :] = pair[pl.ds(r, n), :].astype(F32) + pair2[pl.ds(r, n), :].astype(F32)

    in_rows(fours, 0, half)
    go(total, total2, x_send, x_recv, 2, sibling)

    def outer(source, shift):
        def rows_of(r, n):
            at = pl.ds(shift + r, n)
            t = source[pl.ds(r, n), :]
            old = w[at, :]
            averaged = INNER_RATE * (t * 0.25 + DECAY * old)
            momentum = OUTER_MU * mom[at, :] + averaged
            upd[at, :] = averaged
            mom[at, :] = momentum
            w[at, :] = old - OUTER_RATE * (averaged + OUTER_MU * momentum)

        return rows_of

    def both(here, there):
        in_rows(outer(here, 0), 0, half)
        in_rows(outer(there, half), 0, SHARD - half)

    arrive(total2, x_recv, 2)

    @pl.when(b == 0)
    def _():
        both(total, total2)

    @pl.when(b == 1)
    def _():
        both(total2, total)

    final = [(upd.at[pl.ds(0, SHARD)], avg_out), (mom, mom_out), (w, new_out)]
    final = [pltpu.make_async_copy(src, dst, load_sem.at[7 + i]) for i, (src, dst) in enumerate(final)]
    for copy in final:
        copy.start()
    for copy in sends:
        copy.wait_send()
    lax.fori_loop(0, ROUNDS, given, 0)
    for copy in outs + final:
        copy.wait()


def update(red, weights, first, second, momentum):
    hbm = pl.BlockSpec(memory_space=pl.ANY)
    V = pltpu.VMEM
    flat = jax.ShapeDtypeStruct((SHARD, 128), F32)
    dma = pltpu.SemaphoreType.DMA
    return pl.pallas_call(
        update_kernel,
        out_shape=(flat,) * 5,
        in_specs=[hbm] * 5,
        out_specs=(hbm,) * 5,
        scratch_shapes=[
            V((ROUNDS, UNIT, 16, 128), BF16),
            V((EDGE + SLOT + EDGE, 16, 128), BF16),
            V((BACK_ROWS, 128), F32),
            V((128, 128), F32),
            V((SHARD, 128), F32),
            V((SHARD, 128), F32),
            V((SHARD, 128), F32),
            V((SHARD, 128), F32),
            V((PADDED, 128), F32),
            V((PADDED, 128), BF16),
            V((PADDED, 128), BF16),
            V((PADDED // 2, 128), BF16),
            V((PADDED // 2, 128), BF16),
            V((PADDED // 2, 128), F32),
            V((PADDED // 2, 128), F32),
            dma((11,)),
            dma((3,)),
            dma((3,)),
            dma((ROUNDS,)),
            dma((ROUNDS,)),
            dma((WINDOW,)),
        ],
        compiler_params=pltpu.CompilerParams(collective_id=1, has_side_effects=True, vmem_limit_bytes=60 * 1024 * 1024),
        name="update",
    )(red, weights, first, second, momentum)


def move_kernel(*refs):
    one, two, out_one, out_two, buf_one, buf_two, sem = refs

    def rows(ref):
        return ref.reshape(SHARD, 128) if ref.shape[0] == 1 else ref

    ins = [pltpu.make_async_copy(rows(src), dst, sem.at[i]) for i, (src, dst) in enumerate(((one, buf_one), (two, buf_two)))]
    outs = [pltpu.make_async_copy(src, rows(dst), sem.at[2 + i]) for i, (src, dst) in enumerate(((buf_one, out_one), (buf_two, out_two)))]
    for copy in ins:
        copy.start()
    for i in range(2):
        ins[i].wait()
        outs[i].start()
    for copy in outs:
        copy.wait()


def move(one, two, shape, name):
    hbm = pl.BlockSpec(memory_space=pl.ANY)
    shape = jax.ShapeDtypeStruct(shape, F32)
    rows = pltpu.VMEM((SHARD, 128), F32)
    return pl.pallas_call(
        move_kernel,
        out_shape=(shape,) * 2,
        in_specs=[hbm] * 2,
        out_specs=(hbm,) * 2,
        scratch_shapes=[rows, rows, pltpu.SemaphoreType.DMA((4,))],
        compiler_params=pltpu.CompilerParams(vmem_limit_bytes=60 * 1024 * 1024),
        name=name,
    )(one, two)


def body(patches, labels, counts, weights, first_moments, second_moments, outer_momentum):
    rank = lax.axis_index("fsdp")
    total_count = jnp.sum(counts[0, 0]).astype(jnp.float32)
    valid = (rank < counts[0, 0]).astype(jnp.float32)
    fields = jnp.concatenate([labels[0, 0, :, 0].astype(jnp.float32), valid / total_count, valid, jnp.zeros((2,), jnp.float32)])
    meta = jnp.broadcast_to(fields[:, None], (8, 128))
    flat = weights.reshape(SHARD, 128)
    first, second = move(first_moments, second_moments, (SHARD, 128), "as_rows")
    reduced, losses = grads(flat, patches.reshape(2, P_SIZE, D), meta)
    averaged, momentum, new_weights, first, second = update(reduced, flat, first, second, outer_momentum.reshape(SHARD, 128))
    first, second = move(first, second, (1, SHARD * 128), "as_flat")
    return (
        averaged.reshape(-1),
        momentum.reshape(-1),
        new_weights.reshape(-1),
        first,
        second,
        losses[:1, :1],
    )


def solution(mesh):
    placed = (
        P("rep", None, None, "fsdp", None, None),
        P("rep", None, None, "fsdp"),
        P("rep", None, None),
        P("fsdp"),
        P("rep", "fsdp"),
        P("rep", "fsdp"),
        P("fsdp"),
    )
    return jax.shard_map(
        body,
        mesh=mesh,
        in_specs=placed,
        out_specs=(
            P("fsdp"),
            P("fsdp"),
            P("fsdp"),
            P("rep", "fsdp"),
            P("rep", "fsdp"),
            P("rep", None),
        ),
        check_vma=False,
    )
```

time: 490 us -> 261 us (0.53)
  Pallas kernels: 477 us -> 247 us
    pallas_call x4, Pallas kernels: 477 us -> 247 us  [the longest x1 205 us: grads(): pl.pallas_call(grads_kernel, out_shape=(jax.ShapeDtypeStruct((ROUNDS, UNI...]
where the time goes in v3:
time: 261 us; the launch traced here: 260 us
  Pallas kernels  247 us (95%)
  local copies, waits for them, and re-layouts  8.09 us (3%)
  other arithmetic  3.35 us (1%)
    pallas_call x1, Pallas kernels, grads(): pl.pallas_call(grads_kernel, out_shape=(jax.ShapeDtypeStruct((ROUNDS, UNI...  205 us
    pallas_call x1, Pallas kernels, update(): pl.pallas_call(update_kernel, out_shape=(flat,) * 5, in_specs=[hbm] * 5,...  37.3 us
    unnamed x10, local copies, waits for them, and re-layouts  6.25 us
    pallas_call x2, Pallas kernels, move(): pl.pallas_call(move_kernel, out_shape=(shape,) * 2, in_specs=[hbm] * 2, o...  5.29 us

profile of v3, /device:TPU:24, one launch (start us, length us, event | category | flops | bytes accessed | tf_op | source)
XLA Modules:
  0.0 260.2 jit_solution(13706066832031832251)
XLA Ops:
  0.6 1.3 reduce_sum.9
  2.6 0.7 fusion
  3.3 0.7 fusion.1
  3.9 0.7 convert_bitcast_fusion
  4.6 0.1 pad_maximum_fusion
  4.7 0.7 broadcast_in_dim.2.meta_ref
  5.3 2.0 copy.15
  7.3 204.7 %grads.1 = (bf16[22,6,16,128]{3,2,1,0:T(8,128)(2,1)}, f32[8,128]{1,0:T(8,128)}) custom-call(f32[2098,128]{1,0:T(8,128)} %bitcast.14, bf16[2,196,768]{2,1,0:T(8,128)(2,1)} %bitcast.16, f32[8,128]{1,0:T(8,128)} %broadcast_in_dim.2.meta_ref), custom_call_target="tpu_custom_call" | custom-call | tf_op jit(solution)/shard_map/grads/pallas_call | solution.py:865
  212.0 1.2 slice.3
  213.2 2.6 as_rows.1
  215.8 37.3 %update.1 = (f32[2098,128]{1,0:T(8,128)}, f32[2098,128]{1,0:T(8,128)}, f32[2098,128]{1,0:T(8,128)}, f32[2098,128]{1,0:T(8,128)}, f32[2098,128]{1,0:T(8,128)}) custom-call(bf16[22,6,16,128]{3,2,1,0:T(8,128)(2,1)} %get-tuple-element.17.red_ref, f32[2098,128]{1,0:T(8,128)} %bitcast.15, f32[2098,128]{1,0:T(8,128)} %get-tuple-element.18.first_ref, ...), custom_call_target="tpu_custom_call" | custom-call | tf_op jit(solution)/shard_map/update/pallas_call | solution.py:1211
  253.2 0.0 copy-start.2
  253.2 2.7 %as_flat.1 = (f32[1,268544]{1,0:T(1,128)}, f32[1,268544]{1,0:T(1,128)}) custom-call(f32[2098,128]{1,0:T(8,128)} %get-tuple-element.23.refs_0_, f32[2098,128]{1,0:T(8,128)} %get-tuple-element.24.refs_1_), custom_call_target="tpu_custom_call" | custom-call | tf_op jit(solution)/shard_map/as_flat/pallas_call | solution.py:1265
  255.9 0.0 copy-done.2
  255.9 0.0 copy-start.1
  255.9 1.1 copy.19
  256.9 0.6 copy-done.1
  257.5 0.0 copy-start
  257.5 1.0 copy.20
  258.6 0.6 copy-done
  259.1 1.0 copy.21
  (1 shorter events, 0.0 us)
Async XLA Ops:
  253.2 2.7 %copy-start.2 = (f32[2098,128]{1,0:T(8,128)S(1)}, f32[2098,128]{1,0:T(8,128)}, u32[]{:S(2)}) copy-start(f32[2098,128]{1,0:T(8,128)} %get-tuple-element.20) | copy-start | bytes 3222532
  255.9 1.6 copy-start.1
  257.5 1.6 copy-start

commit v4 on v3

--- a/solution.py
+++ b/solution.py
@@ -232,7 +232,7 @@
             self.add(self.cell(i, h, 0, 1), self.RB.at[2, rd], self.RB.at[5, rd])
 
 
-def start_gather(links, w_ref, patch_ref, meta_ref, T, patch_in, meta_in, flat, headrows, lob, hib, rlo, rhi, slot, local_sem, x_send, x_recv, u_send, u_recv):
+def start_gather(links, w_ref, patch_ref, labels_ref, counts_ref, T, patch_in, meta_in, meta_ref, flat, headrows, lob, hib, rlo, rhi, slot, local_sem, x_send, x_recv, u_send, u_recv):
     xl, b, z, a, y = links.xl, links.b, links.z, links.a, links.y
     fs = z * 8 + a * 4 + y
     swap = a != b
@@ -244,6 +244,13 @@
     load = pltpu.make_async_copy(w_ref, flat.at[pl.ds(MARGIN, SHARD)], local_sem.at[0])
     load.start()
     barrier = pltpu.get_barrier_semaphore()
+    total = (counts_ref[0] + counts_ref[1]).astype(jnp.float32)
+    for m in range(2):
+        valid = jnp.full((1, 128), jnp.where(fs < counts_ref[m], 1.0, 0.0), jnp.float32)
+        meta_ref[m : m + 1, :] = jnp.full((1, 128), labels_ref[m].astype(jnp.float32), jnp.float32)
+        meta_ref[2 + m : 3 + m, :] = valid / jnp.full((1, 128), total, jnp.float32)
+        meta_ref[4 + m : 5 + m, :] = valid
+    meta_ref[6:8, :] = jnp.zeros((2, 128), jnp.float32)
 
     def greet(target):
         pl.semaphore_signal(barrier, inc=1, device_id=target, device_id_type=MESH)
@@ -285,83 +292,101 @@
     meta_swap = remote(meta_ref, meta_in, 3, mirror)
     patch_keep = pltpu.make_async_copy(patch_ref, patch_in, local_sem.at[1])
     meta_keep = pltpu.make_async_copy(meta_ref, meta_in, local_sem.at[2])
-    to_up.wait_recv()
-    flat[pl.ds(MARGIN - HI, HI), :] = rlo[...].astype(jnp.float32)
-    to_down.wait_recv()
-    flat[pl.ds(MARGIN + SHARD, LO), :] = rhi[...].astype(jnp.float32)
-
-    first = SLOT * fs
+    first = ROUNDS * fs
     origin = SHARD * fs - MARGIN
-    for index, (base, c, groups, per, start) in enumerate(SECTIONS):
-        lo = jnp.maximum(first, start)
-        hi = jnp.minimum(first + SLOT, start + c * groups)
-        if index == 1:
-            lane = lax.broadcasted_iota(jnp.int32, (8, 128), 1)
-            g0 = lax.div(jnp.maximum(lo, start) - start, 8)
-            g1 = lax.div(jnp.maximum(hi, start) - start + 7, 8)
-
-            def head_group(g, carry):
-                row = base + per * g - origin
-                for i in range(16):
-                    q, s = divmod(1000 * i, 128)
-                    one = flat[pl.ds(row + q, 8), :]
-                    if s:
-                        two = flat[pl.ds(row + q + 1, 8), :]
-                        one = jnp.where(lane < 128 - s, pltpu.roll(one, 128 - s, 1), pltpu.roll(two, 128 - s, 1))
-                    headrows[pl.ds(i * 8, 8), :] = one
-                for j in range(8):
-                    t = start + g * 8 + j - first
-
-                    @pl.when(jnp.logical_and(t >= 0, t < SLOT))
-                    def _():
-                        slot[t] = headrows[pl.ds(j, 16, stride=8), :].astype(jnp.bfloat16)
-                return carry
-
-            lax.fori_loop(g0, g1, head_group, 0)
-        else:
-
-            def tile(t, carry):
-                g = lax.div(t - start, c)
-                j = lax.rem(t - start, c)
-                row = base + 16 * c * g + j - origin
-                slot[t - first] = flat[pl.ds(row, 16, stride=c), :].astype(jnp.bfloat16)
-                return carry
-
-            lax.fori_loop(lo, hi, tile, 0)
-    pads = jnp.maximum(NTILE - first, 0)
-
-    def blank(t, carry):
-        slot[t] = jnp.zeros((16, 128), jnp.bfloat16)
-        return carry
-
-    lax.fori_loop(jnp.minimum(pads, SLOT), SLOT, blank, 0)
-
 
     def unit_copy(i):
-        k = ROUNDS * fs + i
+        k = first + i
         d = lax.rem(k, 32)
         src = slot.at[pl.ds(UNIT * i, UNIT)]
         dst = T.at[pl.ds(UNIT * k, UNIT)]
         target = device(xo, b, lax.rem(lax.div(d, 4), 2), lax.div(d, 8), lax.rem(d, 4))
         mine = jnp.logical_and(keeps, i == own_index)
         away = pltpu.make_async_remote_copy(src_ref=src, dst_ref=dst, send_sem=u_send.at[i], recv_sem=u_recv.at[lax.div(k, 32)], device_id=target, device_id_type=MESH)
-        here = pltpu.make_async_copy(src, dst, local_sem.at[3])
-        return mine, away, here
-
-    def send_unit(i, carry):
-        mine, away, here = unit_copy(i)
+        return mine, away, (src, dst)
+
+    def send_unit(i):
+        mine, away, (src, dst) = unit_copy(i)
 
         @pl.when(mine)
         def _():
-            here.start()
+            pltpu.make_async_copy(src, dst, local_sem.at[3]).start()
 
         @pl.when(jnp.logical_not(mine))
         def _():
             away.start()
 
-        return carry
-
-    lax.fori_loop(0, ROUNDS, send_unit, 0)
+    lane = lax.broadcasted_iota(jnp.int32, (8, 128), 1)
+
+    def head_group(g, base, per, start):
+        row = base + per * g - origin
+        for i in range(16):
+            q, s = divmod(1000 * i, 128)
+            one = flat[pl.ds(row + q, 8), :]
+            if s:
+                two = flat[pl.ds(row + q + 1, 8), :]
+                one = jnp.where(lane < 128 - s, pltpu.roll(one, 128 - s, 1), pltpu.roll(two, 128 - s, 1))
+            headrows[pl.ds(i * 8, 8), :] = one
+        for j in range(8):
+            t = start + g * 8 + j - UNIT * first
+
+            @pl.when(jnp.logical_and(t >= 0, t < SLOT))
+            def _():
+                slot[t] = headrows[pl.ds(j, 16, stride=8), :].astype(jnp.bfloat16)
+
+    def inside(row, rows):
+        return jnp.logical_and(row >= MARGIN, row + rows <= MARGIN + SHARD)
+
+    def convert(near):
+        for index, (base, c, groups, per, start) in enumerate(SECTIONS):
+            lo = jnp.maximum(UNIT * first, start)
+            hi = jnp.minimum(UNIT * first + SLOT, start + c * groups)
+            if index == 1:
+
+                def group(g, carry):
+                    @pl.when(inside(base + per * g - origin, per + 1) == near)
+                    def _():
+                        head_group(g, base, per, start)
+
+                    return carry
+
+                lax.fori_loop(lax.div(jnp.maximum(lo, start) - start, 8), lax.div(jnp.maximum(hi, start) - start + 7, 8), group, 0)
+                if not near:
+
+                    def deal(u, carry):
+                        send_unit(u - first)
+                        return carry
+
+                    lax.fori_loop(lax.div(lo, UNIT), lax.div(hi, UNIT), deal, 0)
+            else:
+
+                def unit(u, carry):
+                    t = UNIT * u - start
+                    g = lax.div(t, c)
+                    row = base + 16 * c * g + lax.rem(t, c) - origin
+
+                    @pl.when(inside(row, 15 * c + UNIT) == near)
+                    def _():
+                        for k in range(UNIT):
+                            slot[UNIT * (u - first) + k] = flat[pl.ds(row + k, 16, stride=c), :].astype(jnp.bfloat16)
+                        send_unit(u - first)
+
+                    return carry
+
+                lax.fori_loop(lax.div(lo, UNIT), lax.div(hi, UNIT), unit, 0)
+
+    convert(True)
+    to_up.wait_recv()
+    flat[pl.ds(MARGIN - HI, HI), :] = rlo[...].astype(jnp.float32)
+    to_down.wait_recv()
+    flat[pl.ds(MARGIN + SHARD, LO), :] = rhi[...].astype(jnp.float32)
+    convert(False)
+
+    @pl.when(fs == NSLOT - 1)
+    def _():
+        slot[pl.ds(SLOT - 12, 12)] = jnp.zeros((12, 16, 128), jnp.bfloat16)
+        send_unit(ROUNDS - 2)
+        send_unit(ROUNDS - 1)
 
     @pl.when(swap)
     def _():
@@ -392,7 +417,7 @@
 
     def finish_start():
         def wait(i, carry):
-            mine, away, here = unit_copy(i)
+            mine, away, unused = unit_copy(i)
 
             @pl.when(jnp.logical_not(mine))
             def _():
@@ -431,7 +456,7 @@
 T_E, T_HEAD, T_NORM, T_QKV, T_OUT, T_IN, T_FO = 0, 366, 750, 756, 1620, 1908, 3060
 T_POS = 288
 BLK = 256
-STEP_ROWS = 32
+BLOCKS = ((0, 96), (96, 112), (208, 96), (304, 112))
 F32 = jnp.float32
 BF16 = jnp.bfloat16
 ROOT_HALF = 0.7071067811865476
@@ -450,12 +475,19 @@
     return lax.dot_general(x, w, (((0,), (0,)), ((), ())), preferred_element_type=F32)
 
 
-def stats(x):
+def stats(x, keep, r, k):
     mean = jnp.sum(x, -1, keepdims=True) * (1.0 / D)
     centred = x - mean
     var = jnp.sum(centred * centred, -1, keepdims=True) * (1.0 / D)
     rstd = lax.rsqrt(var + NORM_EPS)
-    return centred * rstd, rstd
+    keep[r, k : k + 1] = mean
+    keep[r, k + 1 : k + 2] = rstd
+    return centred * rstd
+
+
+def kept(x, keep, r, k):
+    rstd = keep[r, k + 1 : k + 2]
+    return (x - keep[r, k : k + 1]) * rstd, rstd
 
 
 def norm_back(d_hat, hat, rstd):
@@ -464,7 +496,7 @@
     return rstd * (d_hat - m1 - hat * m2)
 
 
-def compute(step, patch_ref, meta_ref, loss_ref, T, x, h, a, at, mix, prob, o, h1, a2, hid, slope, h2, dh, dyb):
+def compute(step, patch_ref, meta_ref, loss_ref, T, x, h, a, at, mix, prob, o, h1, a2, hid, slope, h2, dh, dyb, keep):
     G = T
     dmix = mix
 
@@ -487,10 +519,6 @@
     def lanes(j):
         return pl.ds(pl.multiple_of(j * BLK, BLK), BLK)
 
-    def rows(i):
-        return pl.ds(pl.multiple_of(i * STEP_ROWS, STEP_ROWS), STEP_ROWS)
-
-    steps = TOK // STEP_ROWS
     step("start")
     for i in range(2):
         x[pl.ds(i * ROWS, 192), :] = patch_ref[i, pl.ds(0, 192), :]
@@ -507,72 +535,75 @@
     step("embedded")
     gain1, shift1, gain2, shift2 = (row_of(T_NORM, k) for k in range(4))
 
-    def norm_one(i, carry):
-        hat, unused = stats(h[rows(i), :])
-        a[rows(i), :] = (hat * gain1 + shift1).astype(BF16)
+    for at_row, n in BLOCKS:
+        r = pl.ds(at_row, n)
+        a[r, :] = (stats(h[r, :], keep, r, 0) * gain1 + shift1).astype(BF16)
+
+    step("qkv")
+    def wide_cols(start, c, groups, j):
+        return jnp.concatenate([cols(start, c, groups, 3 * j + k) for k in range(3)], axis=1)
+
+    def wide_lanes(j):
+        return pl.ds(pl.multiple_of(j * D, D), D)
+
+    def mix_block(j, carry):
+        mix[:, wide_lanes(j)] = dot(a[...], wide_cols(T_QKV, 18, 48, j)).astype(BF16)
         return carry
 
-    lax.fori_loop(0, steps, norm_one, 0)
-
-    step("qkv")
-    def mix_block(j, carry):
-        mix[:, lanes(j)] = dot(a[...], cols(T_QKV, 18, 48, j)).astype(BF16)
+    lax.fori_loop(0, 3, mix_block, 0)
+
+    first_half = lax.broadcasted_iota(jnp.int32, (ROWS, 128), 1) < HEAD_DIM
+    key_ok = lax.broadcasted_iota(jnp.int32, (ROWS, ROWS), 0) < P_SIZE
+    first_rows = lax.broadcasted_iota(jnp.int32, (128, ROWS), 0) < HEAD_DIM
+    halves = (first_half, jnp.logical_not(first_half))
+    zero = jnp.zeros((ROWS, 128), BF16)
+
+    def split(block):
+        return jnp.concatenate([jnp.where(first_half, block, zero), jnp.where(first_half, zero, block)], axis=0)
+
+    def heads_of(p, i):
+        r = pl.ds(i * ROWS, ROWS)
+        return r, [pl.ds(pl.multiple_of(p * 128 + D * k, 128), 128) for k in range(3)]
+
+    def attend(p, carry):
+        for i in range(2):
+            r, ls = heads_of(p, i)
+            q, k, v = (mix[r, l] for l in ls)
+            q = q * jnp.asarray(0.125, BF16)
+            vt = v.T
+            outs = []
+            for e in range(2):
+                s = dot_t(jnp.where(halves[e], k, zero), q)
+                s = jnp.where(key_ok, s, -jnp.inf)
+                ex = jnp.exp(s - jnp.max(s, 0, keepdims=True))
+                pr = (ex * (1.0 / jnp.sum(ex, 0, keepdims=True))).astype(BF16)
+                prob[p * 2 + i, e] = pr
+                outs.append(dot(vt, pr))
+            o[r, ls[0]] = jnp.where(first_rows, outs[0], outs[1]).astype(BF16).T
         return carry
 
-    lax.fori_loop(0, 9, mix_block, 0)
-
-    first_half = lax.broadcasted_iota(jnp.int32, (ROWS, 128), 1) < HEAD_DIM
-    key_ok = lax.broadcasted_iota(jnp.int32, (ROWS, ROWS), 1) < P_SIZE
-    zero = jnp.zeros((ROWS, 128), BF16)
-
-    def qkv_of(n):
-        i = lax.div(n, 6)
-        p = lax.rem(n, 6)
-        r = pl.ds(pl.multiple_of(i * ROWS, ROWS), ROWS)
-        ls = [pl.ds(pl.multiple_of(p * 128 + D * k, 128), 128) for k in range(3)]
-        return r, ls
-
-    def attend(n, carry):
-        r, ls = qkv_of(n)
-        q, k, v = (mix[r, l] for l in ls)
-        q = q * jnp.asarray(0.125, BF16)
-        outs = []
-        for e in range(2):
-            mask = first_half if e == 0 else jnp.logical_not(first_half)
-            s = dot_t(jnp.where(mask, q, zero), k)
-            s = jnp.where(key_ok, s, -jnp.inf)
-            top = jnp.max(s, -1, keepdims=True)
-            ex = jnp.exp(s - top)
-            pr = (ex / jnp.sum(ex, -1, keepdims=True)).astype(BF16)
-            prob[n * 2 + e] = pr
-            outs.append(dot(pr, v))
-        o[r, ls[0]] = jnp.where(first_half, outs[0], outs[1]).astype(BF16)
-        return carry
-
+    parts = ((0, 2), (2, 3), (3, 5), (5, 6))
     for part in range(4):
         step("attend%d" % part)
-        lax.fori_loop(3 * part, 3 * part + 3, attend, 0)
+        lax.fori_loop(*parts[part], attend, 0)
     step("attended")
     for j in range(3):
         h1[:, pl.ds(j * BLK, BLK)] = h[:, pl.ds(j * BLK, BLK)] + dot(o[...], cols(T_OUT, 6, 48, j))
 
-    def norm_two(i, carry):
-        hat, unused = stats(h1[rows(i), :])
-        a2[rows(i), :] = (hat * gain2 + shift2).astype(BF16)
-        return carry
-
-    lax.fori_loop(0, steps, norm_two, 0)
+    for at_row, n in BLOCKS:
+        r = pl.ds(at_row, n)
+        a2[r, :] = (stats(h1[r, :], keep, r, 2) * gain2 + shift2).astype(BF16)
 
     step("up")
     def up_block(j, carry):
-        u = dot(a2[...], cols(T_IN, 24, 48, j))
+        u = dot(a2[...], wide_cols(T_IN, 24, 48, j))
         phi = 0.5 * (1.0 + lax.erf(u * ROOT_HALF))
         pdf = jnp.exp(-0.5 * u * u) * INV_ROOT_TWO_PI
-        hid[:, lanes(j)] = (u * phi).astype(BF16)
-        slope[:, lanes(j)] = (phi + u * pdf).astype(BF16)
+        hid[:, wide_lanes(j)] = (u * phi).astype(BF16)
+        slope[:, wide_lanes(j)] = (phi + u * pdf).astype(BF16)
         return carry
 
-    lax.fori_loop(0, 12, up_block, 0)
+    lax.fori_loop(0, 4, up_block, 0)
     step("down")
     for j in range(3):
         h2[:, pl.ds(j * BLK, BLK)] = h1[:, pl.ds(j * BLK, BLK)] + dot(hid[...], cols(T_FO, 6, 192, j))
@@ -580,15 +611,15 @@
     step("pool")
     gain_end, shift_end = (row_of(T_POS + 72, 4 + k) for k in range(2))
     means = []
+    last_rows = lax.broadcasted_iota(jnp.int32, (112, D), 0) < P_SIZE - 96
     for i in range(2):
-
-        def pool_step(n, carry):
-            hat, unused = stats(h2[pl.ds(pl.multiple_of(i * ROWS + n * 16, 16), 16), :])
-            ok = lax.broadcasted_iota(jnp.int32, (16, D), 0) + n * 16 < P_SIZE
-            hat = jnp.where(ok, hat, 0.0)
-            return carry + hat[:8] + hat[8:]
-
-        total = lax.fori_loop(0, 13, pool_step, jnp.zeros((8, D), F32))
+        total = jnp.zeros((8, D), F32)
+        for at_row, n in BLOCKS[2 * i : 2 * i + 2]:
+            r = pl.ds(at_row, n)
+            hat = stats(h2[r, :], keep, r, 4)
+            if n == 112:
+                hat = jnp.where(last_rows, hat, 0.0)
+            total = total + jnp.sum(hat.reshape(n // 8, 8, D), 0)
         means.append(jnp.sum(total, 0, keepdims=True) * (1.0 / P_SIZE))
     mean_hat = jnp.concatenate(means + [jnp.zeros((14, D), F32)], axis=0)
     two = lax.broadcasted_iota(jnp.int32, (16, D), 0) < 2
@@ -620,117 +651,112 @@
     for i in range(2):
         d_hat = d_pooled[i : i + 1, :] * (1.0 / P_SIZE) * gain_end
 
-        def end_step(n, carry):
-            r = pl.ds(pl.multiple_of(i * ROWS + n * 16, 16), 16)
-            hat, rstd = stats(h2[r, :])
-            ok = lax.broadcasted_iota(jnp.int32, (16, D), 0) + n * 16 < P_SIZE
-            d = jnp.where(ok, norm_back(jnp.broadcast_to(d_hat, (16, D)), hat, rstd), 0.0)
+        m1 = jnp.sum(d_hat, -1, keepdims=True) * (1.0 / D)
+        for at_row, n in BLOCKS[2 * i : 2 * i + 2]:
+            r = pl.ds(at_row, n)
+            hat, rstd = kept(h2[r, :], keep, r, 4)
+            m2 = jnp.sum(d_hat * hat, -1, keepdims=True) * (1.0 / D)
+            d = rstd * ((d_hat - m1) - hat * m2)
+            if n == 112:
+                d = jnp.where(last_rows, d, 0.0)
             dh[r, :] = d
             dyb[r, :] = d.astype(BF16)
-            return carry
-
-        lax.fori_loop(0, 13, end_step, 0)
 
     step("backward")
     at[...] = a2[...].T
     da = h2
 
+    wide = D // 16
+
     def down_block(j, carry):
+        part = section(T, T_FO + j * wide * 6, 6, wide)
+        w = jnp.concatenate([part[:, k].reshape(D, 128) for k in range(6)], axis=1)
         dy = dyb[...]
-        d_w = t_dot(hid[:, lanes(j)], dy).astype(BF16)
-        part = section(T, T_FO + j * 96, 6, 16)
-        w = jnp.concatenate([part[:, k].reshape(BLK, 128) for k in range(6)], axis=1)
-        hid[:, lanes(j)] = (dot_t(dy, w) * slope[:, lanes(j)].astype(F32)).astype(BF16)
+        d_w = t_dot(hid[:, wide_lanes(j)], dy).astype(BF16)
+        hid[:, wide_lanes(j)] = (dot_t(dy, w) * slope[:, wide_lanes(j)].astype(F32)).astype(BF16)
         for k in range(6):
-            part[:, k] = d_w[:, k * 128 : (k + 1) * 128].reshape(16, 16, 128)
+            part[:, k] = d_w[:, k * 128 : (k + 1) * 128].reshape(wide, 16, 128)
         return carry
 
     G[pl.ds(4212, 12)] = jnp.zeros((12, 16, 128), BF16)
-    lax.fori_loop(0, 8, down_block, 0)
+    lax.fori_loop(0, 3, down_block, 0)
     step("fc_out0")
-    lax.fori_loop(8, 12, down_block, 0)
+    lax.fori_loop(3, 4, down_block, 0)
     step("fc_out1")
-    da[...] = jnp.zeros((TOK, D), F32)
-
-    def up_back(j, carry):
-        d_u = hid[:, lanes(j)]
-        da[...] += dot_t(d_u, cols(T_IN, 24, 48, j))
-        put_cols(T_IN, 24, 48, j, dot(at[...], d_u))
-        return carry
-
-    for part in range(4):
-        lax.fori_loop(3 * part, 3 * part + 3, up_back, 0)
-        step("fc_in%d" % part)
-
-    def back_two(i, carry):
-        dg, ds = carry
-        hat, rstd = stats(h1[rows(i), :])
-        d = da[rows(i), :]
-        new = dh[rows(i), :] + norm_back(d * gain2, hat, rstd)
-        dh[rows(i), :] = new
-        dyb[rows(i), :] = new.astype(BF16)
-        return dg + jnp.sum((d * hat).reshape(4, 8, D), 0), ds + jnp.sum(d.reshape(4, 8, D), 0)
-
-    none = jnp.zeros((8, D), F32)
-    d_gain2, d_shift2 = lax.fori_loop(0, steps, back_two, (none, none))
+    def row_block(start, c, j):
+        part = section(T, start + j * 16 * c, c, 16)
+        return jnp.concatenate([part[:, k].reshape(BLK, 128) for k in range(c)], axis=1)
+
+    def put_rows(start, c, j, first, value):
+        part = section(G, start + j * 16 * c, c, 16)
+        low = value.astype(BF16)
+        for k in range(value.shape[1] // 128):
+            part[:, first + k] = low[:, k * 128 : (k + 1) * 128].reshape(16, 16, 128)
+
+    for j in range(3):
+        da[:, pl.ds(j * BLK, BLK)] = dot_t(hid[...], row_block(T_IN, 24, j))
+    step("fc_in0")
+    for j in range(3):
+        for k in range(4):
+            put_rows(T_IN, 24, j, 6 * k, dot(at[pl.ds(j * BLK, BLK), :], hid[:, pl.ds(k * D, D)]))
+        step("fc_in%d" % (j + 1))
+
+    def norm_grads(inputs, column, gain):
+        dg, ds = jnp.zeros((8, D), F32), jnp.zeros((8, D), F32)
+        for at_row, n in BLOCKS:
+            r = pl.ds(at_row, n)
+            hat, rstd = kept(inputs[r, :], keep, r, column)
+            d = da[r, :]
+            new = dh[r, :] + norm_back(d * gain, hat, rstd)
+            dh[r, :] = new
+            dyb[r, :] = new.astype(BF16)
+            dg = dg + jnp.sum((d * hat).reshape(n // 8, 8, D), 0)
+            ds = ds + jnp.sum(d.reshape(n // 8, 8, D), 0)
+        return dg, ds
+
+    d_gain2, d_shift2 = norm_grads(h1, 2, gain2)
 
     step("normed2")
     at[...] = o[...].T
-    da[...] = jnp.zeros((TOK, D), F32)
     for j in range(3):
-        dz = dyb[:, pl.ds(j * BLK, BLK)]
-        da[...] += dot_t(dz, cols(T_OUT, 6, 48, j))
-        put_cols(T_OUT, 6, 48, j, dot(at[...], dz))
-    o[...] = da[...].astype(BF16)
+        o[:, pl.ds(j * BLK, BLK)] = dot_t(dyb[...], row_block(T_OUT, 6, j)).astype(BF16)
+    for j in range(3):
+        put_rows(T_OUT, 6, j, 0, dot(at[pl.ds(j * BLK, BLK), :], dyb[...]))
 
     step("out")
-    def attend_back(n, carry):
-        r, ls = qkv_of(n)
-        q, k, v = (mix[r, l] for l in ls)
-        q = q * jnp.asarray(0.125, BF16)
-        k8 = k * jnp.asarray(0.125, BF16)
-        do = o[r, ls[0]]
-        dq, dk, dv = [], [], []
-        for e in range(2):
-            mask = first_half if e == 0 else jnp.logical_not(first_half)
-            pr = prob[n * 2 + e]
-            dv.append(t_dot(pr, do))
-            dp = dot_t(jnp.where(mask, do, zero), v)
+    def attend_back(p, carry):
+        for i in range(2):
+            r, ls = heads_of(p, i)
+            q, k, v = (mix[r, l] for l in ls)
+            q = q * jnp.asarray(0.125, BF16)
+            k8 = k * jnp.asarray(0.125, BF16)
+            kt = k8.T
+            do = o[r, ls[0]]
+            pr = prob[p * 2 + i]
+            dv = dot(pr.reshape(TOK, ROWS), do)
+            dp = dot_t(split(v), do).reshape(2, ROWS, ROWS)
             prf = pr.astype(F32)
-            row = jnp.sum(prf * dp, -1, keepdims=True)
+            row = jnp.sum(prf * dp, 1, keepdims=True)
             ds = (prf * (dp - row)).astype(BF16)
-            dq.append(dot(ds, k8))
-            dk.append(t_dot(ds, q))
-        for l, pair in zip(ls, (dq, dk, dv)):
-            dmix[r, l] = jnp.where(first_half, pair[0], pair[1]).astype(BF16)
+            dq = [dot(kt[HEAD_DIM * e : HEAD_DIM * (e + 1)], ds[e]) for e in range(2)]
+            dk = dot(ds.reshape(TOK, ROWS), q)
+            dmix[r, ls[0]] = jnp.concatenate(dq, axis=0).astype(BF16).T
+            dmix[r, ls[1]] = jnp.where(first_half, dk[:ROWS], dk[ROWS:]).astype(BF16)
+            dmix[r, ls[2]] = jnp.where(first_half, dv[:ROWS], dv[ROWS:]).astype(BF16)
         return carry
 
     for part in range(4):
-        lax.fori_loop(3 * part, 3 * part + 3, attend_back, 0)
+        lax.fori_loop(*parts[part], attend_back, 0)
         step("back%d" % part)
 
     at[...] = a[...].T
-    da[...] = jnp.zeros((TOK, D), F32)
-
-    def qkv_block(j, carry):
-        d = dmix[:, lanes(j)]
-        da[...] += dot_t(d, cols(T_QKV, 18, 48, j))
-        put_cols(T_QKV, 18, 48, j, dot(at[...], d))
-        return carry
-
-    lax.fori_loop(0, 9, qkv_block, 0)
-
+    for j in range(3):
+        da[:, pl.ds(j * BLK, BLK)] = dot_t(dmix[...], row_block(T_QKV, 18, j))
+    for j in range(3):
+        for k in range(3):
+            put_rows(T_QKV, 18, j, 6 * k, dot(at[pl.ds(j * BLK, BLK), :], dmix[:, pl.ds(k * D, D)]))
     step("qkv_back")
-    def back_one(i, carry):
-        dg, ds = carry
-        hat, rstd = stats(h[rows(i), :])
-        d = da[rows(i), :]
-        new = dh[rows(i), :] + norm_back(d * gain1, hat, rstd)
-        dh[rows(i), :] = new
-        dyb[rows(i), :] = new.astype(BF16)
-        return dg + jnp.sum((d * hat).reshape(4, 8, D), 0), ds + jnp.sum(d.reshape(4, 8, D), 0)
-
-    d_gain1, d_shift1 = lax.fori_loop(0, steps, back_one, (none, none))
+    d_gain1, d_shift1 = norm_grads(h, 0, gain1)
     d_norms = jnp.concatenate([jnp.sum(d, 0, keepdims=True) for d in (d_gain1, d_shift1, d_gain2, d_shift2)] + [jnp.zeros((12, D), F32)], axis=0).astype(BF16)
     for j in range(6):
         G[T_NORM + j] = d_norms[:, j * 128 : (j + 1) * 128]
@@ -764,27 +790,27 @@
     "fc_out1": ((3, 1, 0), (3, 0, 1)),
     "fc_in0": ((3, 1, 1),),
     "fc_in1": ((3, 0, 2),),
-    "fc_in2": ((3, 1, 2), (3, 0, 3)),
-    "fc_in3": ((2, 0, 0), (2, 1, 0), (3, 1, 3)),
-    "normed2": ((3, 0, 4), (3, 1, 4), (2, 0, 1)),
-    "out": ((2, 1, 1), (3, 0, 5)),
-    "back0": ((2, 0, 2), (2, 1, 2), (3, 1, 5)),
-    "back1": ((2, 0, 3), (2, 1, 3)),
-    "back2": ((2, 0, 4), (2, 1, 4)),
-    "back3": ((2, 0, 5), (2, 1, 5)),
-    "qkv_back": ((1, 0, 0), (1, 1, 0)),
+    "fc_in2": ((2, 0, 0), (3, 1, 2)),
+    "fc_in3": ((2, 1, 0), (2, 0, 1), (3, 0, 3)),
+    "normed2": ((2, 1, 1), (3, 1, 3)),
+    "out": ((3, 0, 4), (2, 0, 2), (3, 1, 4)),
+    "back0": ((2, 1, 2), (3, 0, 5)),
+    "back1": ((2, 0, 3), (3, 1, 5)),
+    "back2": ((2, 1, 3),),
+    "back3": ((2, 0, 4), (2, 1, 4)),
+    "qkv_back": ((1, 0, 0), (1, 1, 0), (2, 0, 5), (2, 1, 5)),
     "norms": ((0, 1, 0), (1, 0, 1), (1, 1, 1)),
-    "embed": ((0, 0, 0), (0, 1, 1), (1, 0, 2), (1, 1, 2), (0, 0, 1), (1, 0, 3), (1, 1, 3), (0, 1, 2), (0, 0, 2), (1, 0, 4), (1, 1, 4), (0, 1, 3), (0, 0, 3), (1, 0, 5), (1, 1, 5), (0, 1, 4), (0, 0, 4), (0, 1, 5), (0, 0, 5)),
+    "embed": ((0, 0, 0), (0, 1, 1), (0, 0, 1), (1, 0, 2), (1, 1, 2), (0, 1, 2), (0, 0, 2), (1, 0, 3), (1, 1, 3), (0, 1, 3), (0, 0, 3), (1, 0, 4), (1, 1, 4), (0, 1, 4), (0, 0, 4), (1, 0, 5), (1, 1, 5), (0, 1, 5), (0, 0, 5)),
 }
 
 
-def grads_kernel(w_ref, patch_ref, meta_ref, red_ref, loss_out, T, R, RA, RB, g_send, g_recv, r_send, r_recv, LS, l_send, l_recv, patch_in, meta_in, loss, *rest):
+def grads_kernel(w_ref, patch_ref, labels_ref, counts_ref, red_ref, loss_out, T, R, RA, RB, g_send, g_recv, r_send, r_recv, LS, l_send, l_recv, patch_in, meta_in, meta, loss, *rest):
     gather_refs, compute_refs, out_sem = rest[:12], rest[12:-1], rest[-1]
     links = Links(T, R, RA, RB, g_send, g_recv, r_send, r_recv)
     xl, b, z, a, y = links.xl, links.b, links.z, links.a, links.y
     swap = a != b
     mirror = device(xl, b, a, z, y)
-    units_here, finish_start = start_gather(links, w_ref, patch_ref, meta_ref, T, patch_in, meta_in, *gather_refs)
+    units_here, finish_start = start_gather(links, w_ref, patch_ref, labels_ref, counts_ref, T, patch_in, meta_in, meta, *gather_refs)
 
     def loss_send(src, dst, target):
         links.go(LS.at[src], LS.at[dst], l_send.at[dst], l_recv.at[dst], target)
@@ -857,7 +883,7 @@
     out.wait()
 
 
-def grads(weights, patches, meta):
+def grads(weights, patches, labels, counts):
     hbm = pl.BlockSpec(memory_space=pl.ANY)
     vmem = pl.BlockSpec(memory_space=pltpu.VMEM)
     V = pltpu.VMEM
@@ -865,7 +891,7 @@
     return pl.pallas_call(
         grads_kernel,
         out_shape=(jax.ShapeDtypeStruct((ROUNDS, UNIT, 16, 128), BF16), jax.ShapeDtypeStruct((8, 128), F32)),
-        in_specs=[hbm] * 3,
+        in_specs=[hbm] * 2 + [pl.BlockSpec(memory_space=pltpu.SMEM)] * 2,
         out_specs=(hbm, vmem),
         scratch_shapes=[
             V((NTILES, 16, 128), BF16),
@@ -880,6 +906,7 @@
             dma((12,)),
             dma((12,)),
             V(patches.shape, BF16),
+            V((8, 128), F32),
             V((8, 128), F32),
             V((8, 128), F32),
             V((FROWS, 128), F32),
@@ -899,7 +926,7 @@
             V((TOK, D), BF16),
             V((D, TOK), BF16),
             V((TOK, 3 * D), BF16),
-            V((24, ROWS, ROWS), BF16),
+            V((12, 2, ROWS, ROWS), BF16),
             V((TOK, D), BF16),
             V((TOK, D), F32),
             V((TOK, D), BF16),
@@ -908,11 +935,12 @@
             V((TOK, D), F32),
             V((TOK, D), F32),
             V((TOK, D), BF16),
+            V((TOK, 128), F32),
             dma,
         ],
         compiler_params=pltpu.CompilerParams(collective_id=0, has_side_effects=True, vmem_limit_bytes=60 * 1024 * 1024),
         name="grads",
-    )(weights, patches, meta)
+    )(weights, patches, labels, counts)
 
 
 EDGE = 24
@@ -1107,13 +1135,14 @@
             lax.fori_loop(jnp.minimum(g0, groups), jnp.minimum(g1, groups), head_group, 0)
         else:
 
-            def tile(t, carry):
-                g = lax.div(t - start, c)
-                j = lax.rem(t - start, c)
-                flat[pl.ds(base + 16 * c * g + j - origin, 16, stride=c), :] = window[t - low_tile].astype(F32)
+            def unit(n, carry):
+                t = UNIT * n - start
+                row = base + 16 * c * lax.div(t, c) + lax.rem(t, c) - origin
+                for m in range(UNIT):
+                    flat[pl.ds(row + m, 16, stride=c), :] = window[UNIT * n - low_tile + m].astype(F32)
                 return carry
 
-            lax.fori_loop(jnp.maximum(low_tile, start), jnp.minimum(high_tile, start + c * groups), tile, 0)
+            lax.fori_loop(lax.div(jnp.maximum(low_tile, start), UNIT), lax.div(jnp.minimum(high_tile, start + c * groups), UNIT), unit, 0)
 
     fix_one = 1.0 / (1.0 - BETA_ONE**STEP)
     fix_two = 1.0 / (1.0 - BETA_TWO**STEP)
@@ -1274,14 +1303,9 @@
 
 
 def body(patches, labels, counts, weights, first_moments, second_moments, outer_momentum):
-    rank = lax.axis_index("fsdp")
-    total_count = jnp.sum(counts[0, 0]).astype(jnp.float32)
-    valid = (rank < counts[0, 0]).astype(jnp.float32)
-    fields = jnp.concatenate([labels[0, 0, :, 0].astype(jnp.float32), valid / total_count, valid, jnp.zeros((2,), jnp.float32)])
-    meta = jnp.broadcast_to(fields[:, None], (8, 128))
     flat = weights.reshape(SHARD, 128)
     first, second = move(first_moments, second_moments, (SHARD, 128), "as_rows")
-    reduced, losses = grads(flat, patches.reshape(2, P_SIZE, D), meta)
+    reduced, losses = grads(flat, patches.reshape(2, P_SIZE, D), labels.reshape(2), counts.reshape(2))
     averaged, momentum, new_weights, first, second = update(reduced, flat, first, second, outer_momentum.reshape(SHARD, 128))
     first, second = move(first, second, (1, SHARD * 128), "as_flat")
     return (

time: 261 us -> 224 us (0.86)
  Pallas kernels: 247 us -> 215 us
  other arithmetic: 3.35 us -> 0 us
    pallas_call x1, Pallas kernels: 205 us -> 172 us  [grads(): pl.pallas_call(grads_kernel, out_shape=(jax.ShapeDtypeStruct((ROUNDS, UNI...]
where the time goes in v4:
time: 224 us
  Pallas kernels  215 us (96%)
  local copies, waits for them, and re-layouts  7.42 us (3%)
    pallas_call x1, Pallas kernels, grads(): pl.pallas_call(grads_kernel, out_shape=(jax.ShapeDtypeStruct((ROUNDS, UNI...  172 us
    pallas_call x1, Pallas kernels, update(): pl.pallas_call(update_kernel, out_shape=(flat,) * 5, in_specs=[hbm] * 5,...  38.2 us
    unnamed x10, local copies, waits for them, and re-layouts  6.25 us
    pallas_call x2, Pallas kernels, move(): pl.pallas_call(move_kernel, out_shape=(shape,) * 2, in_specs=[hbm] * 2, o...  5.29 us

profile of v4, /device:TPU:24, one launch (start us, length us, event | category | flops | bytes accessed | tf_op | source)
XLA Modules:
  0.0 223.5 jit_solution(12259163009366535589)
XLA Ops:
  0.6 2.0 copy.15
  2.6 171.9 %grads.1 = (bf16[22,6,16,128]{3,2,1,0:T(8,128)(2,1)}, f32[8,128]{1,0:T(8,128)}) custom-call(f32[2098,128]{1,0:T(8,128)} %bitcast.10, bf16[2,196,768]{2,1,0:T(8,128)(2,1)} %bitcast.12, s32[2]{0:T(128)} %bitcast.17, s32[2]{0:T(128)} %bitcast.18), custom_call_target="tpu_custom_call" | custom-call | tf_op jit(solution)/shard_map/grads/pallas_call | solution.py:891
  174.4 1.2 slice.3
  175.6 2.6 %as_rows.1 = (f32[2098,128]{1,0:T(8,128)}, f32[2098,128]{1,0:T(8,128)}) custom-call(f32[1,268544]{1,0:T(1,128)} %refs_0_.1, f32[1,268544]{1,0:T(1,128)} %refs_1_.1), custom_call_target="tpu_custom_call" | custom-call | tf_op jit(solution)/shard_map/as_rows/pallas_call | solution.py:1294
  178.2 38.2 %update.1 = (f32[2098,128]{1,0:T(8,128)}, f32[2098,128]{1,0:T(8,128)}, f32[2098,128]{1,0:T(8,128)}, f32[2098,128]{1,0:T(8,128)}, f32[2098,128]{1,0:T(8,128)}) custom-call(bf16[22,6,16,128]{3,2,1,0:T(8,128)(2,1)} %get-tuple-element.17.red_ref, f32[2098,128]{1,0:T(8,128)} %bitcast.11, f32[2098,128]{1,0:T(8,128)} %get-tuple-element.18.first_ref, ...), custom_call_target="tpu_custom_call" | custom-call | tf_op jit(solution)/shard_map/update/pallas_call | solution.py:1240
  216.5 0.0 copy-start.2
  216.5 2.7 %as_flat.1 = (f32[1,268544]{1,0:T(1,128)}, f32[1,268544]{1,0:T(1,128)}) custom-call(f32[2098,128]{1,0:T(8,128)} %get-tuple-element.23.refs_0_, f32[2098,128]{1,0:T(8,128)} %get-tuple-element.24.refs_1_), custom_call_target="tpu_custom_call" | custom-call | tf_op jit(solution)/shard_map/as_flat/pallas_call | solution.py:1294
  219.2 0.0 copy-done.2
  219.2 0.0 copy-start.1
  219.2 1.1 copy.19
  220.3 0.6 copy-done.1
  220.8 0.0 copy-start
  220.8 1.0 copy.20
  221.9 0.6 copy-done
  222.5 1.0 copy.21
Async XLA Ops:
  216.5 2.7 %copy-start.2 = (f32[2098,128]{1,0:T(8,128)S(1)}, f32[2098,128]{1,0:T(8,128)}, u32[]{:S(2)}) copy-start(f32[2098,128]{1,0:T(8,128)} %get-tuple-element.20) | copy-start | bytes 3222532
  219.2 1.6 copy-start.1
  220.8 1.6 copy-start

commit v5 on v4

--- a/solution.py
+++ b/solution.py
@@ -789,18 +789,17 @@
     "fc_out0": ((3, 0, 0),),
     "fc_out1": ((3, 1, 0), (3, 0, 1)),
     "fc_in0": ((3, 1, 1),),
-    "fc_in1": ((3, 0, 2),),
-    "fc_in2": ((2, 0, 0), (3, 1, 2)),
-    "fc_in3": ((2, 1, 0), (2, 0, 1), (3, 0, 3)),
-    "normed2": ((2, 1, 1), (3, 1, 3)),
-    "out": ((3, 0, 4), (2, 0, 2), (3, 1, 4)),
-    "back0": ((2, 1, 2), (3, 0, 5)),
-    "back1": ((2, 0, 3), (3, 1, 5)),
-    "back2": ((2, 1, 3),),
-    "back3": ((2, 0, 4), (2, 1, 4)),
-    "qkv_back": ((1, 0, 0), (1, 1, 0), (2, 0, 5), (2, 1, 5)),
-    "norms": ((0, 1, 0), (1, 0, 1), (1, 1, 1)),
-    "embed": ((0, 0, 0), (0, 1, 1), (0, 0, 1), (1, 0, 2), (1, 1, 2), (0, 1, 2), (0, 0, 2), (1, 0, 3), (1, 1, 3), (0, 1, 3), (0, 0, 3), (1, 0, 4), (1, 1, 4), (0, 1, 4), (0, 0, 4), (1, 0, 5), (1, 1, 5), (0, 1, 5), (0, 0, 5)),
+    "fc_in2": ((2, 0, 0),),
+    "fc_in3": ((2, 1, 0), (2, 0, 1)),
+    "normed2": ((2, 1, 1),),
+    "out": ((3, 0, 2), (3, 1, 2)),
+    "back3": ((2, 0, 2), (2, 1, 2)),
+    "qkv_back": ((1, 0, 0), (1, 1, 0), (1, 0, 1), (1, 1, 1), (3, 0, 3), (3, 1, 3)),
+    "norms": ((0, 1, 0),),
+    "embed": (
+        (0, 0, 0), (0, 1, 1), (0, 0, 1), (2, 0, 3), (2, 1, 3), (1, 0, 2), (1, 1, 2), (3, 0, 4), (3, 1, 4), (0, 1, 2), (0, 0, 2), (2, 0, 4), (2, 1, 4),
+        (1, 0, 3), (1, 1, 3), (3, 0, 5), (3, 1, 5), (0, 1, 3), (0, 0, 3), (2, 0, 5), (2, 1, 5), (1, 0, 4), (1, 1, 4), (0, 1, 4), (0, 0, 4), (1, 0, 5), (1, 1, 5), (0, 1, 5), (0, 0, 5),
+    ),
 }
 
 
@@ -960,9 +959,9 @@
 
 
 def update_kernel(
-    red_ref, w_ref, first_ref, second_ref, mom_ref,
-    avg_out, mom_out, new_out, first_out, second_out,
-    red, window, flat, headrows, w, first, second, mom, upd, low, low2, pair, pair2, total, total2,
+    red_ref, first_ref, second_ref,
+    sum_out, first_out, second_out,
+    red, window, flat, headrows, first_row, second_row, first, second, upd, low, low2, pair, pair2, total, total2,
     load_sem, x_send, x_recv, o_send, e_send, w_recv,
 ):
     xl, b, z, a, y = coords()
@@ -970,7 +969,7 @@
     holder = z * 8 + b * 4 + y
     sibling = device(xl, a, 1 - b, z, y)
     across = device(1 - xl, a, b, z, y)
-    extra = [pltpu.make_async_copy(src, dst, load_sem.at[i]) for i, (src, dst) in enumerate(((w_ref, w), (first_ref, first), (second_ref, second), (mom_ref, mom)))]
+    extra = [pltpu.make_async_copy(src, dst, load_sem.at[i]) for i, (src, dst) in enumerate(((first_ref, first_row), (second_ref, second_row)))]
     load = pltpu.make_async_copy(red_ref, red, load_sem.at[4])
     load.start()
     for copy in extra:
@@ -1080,6 +1079,18 @@
 
     lax.fori_loop(0, BACK_ROWS // 32, clear, 0)
 
+    for copy in extra:
+        copy.wait()
+    for source, rows_of in ((first_row, first), (second_row, second)):
+
+        def eight(i, carry):
+            rows_of[pl.ds(pl.multiple_of(i * 8, 8), 8), :] = source[0, pl.ds(pl.multiple_of(i * 1024, 1024), 1024)].reshape(8, 128)
+            return carry
+
+        whole = SHARD // 8
+        lax.fori_loop(0, whole, eight, 0, unroll=2)
+        rows_of[pl.ds(whole * 8, SHARD - whole * 8), :] = source[0, pl.ds(whole * 1024, (SHARD - whole * 8) * 128)].reshape(SHARD - whole * 8, 128)
+
     def got(p, carry):
         inside, mine, source = window_unit(p)
         place = window.at[pl.ds(UNIT * p, UNIT)]
@@ -1095,8 +1106,6 @@
         return carry
 
     lax.fori_loop(0, WINDOW, got, 0)
-    for copy in extra:
-        copy.wait()
     sends = []
 
     def go(src, dst, send, recv, k, target):
@@ -1194,34 +1203,9 @@
     in_rows(fours, 0, half)
     go(total, total2, x_send, x_recv, 2, sibling)
 
-    def outer(source, shift):
-        def rows_of(r, n):
-            at = pl.ds(shift + r, n)
-            t = source[pl.ds(r, n), :]
-            old = w[at, :]
-            averaged = INNER_RATE * (t * 0.25 + DECAY * old)
-            momentum = OUTER_MU * mom[at, :] + averaged
-            upd[at, :] = averaged
-            mom[at, :] = momentum
-            w[at, :] = old - OUTER_RATE * (averaged + OUTER_MU * momentum)
-
-        return rows_of
-
-    def both(here, there):
-        in_rows(outer(here, 0), 0, half)
-        in_rows(outer(there, half), 0, SHARD - half)
-
     arrive(total2, x_recv, 2)
-
-    @pl.when(b == 0)
-    def _():
-        both(total, total2)
-
-    @pl.when(b == 1)
-    def _():
-        both(total2, total)
-
-    final = [(upd.at[pl.ds(0, SHARD)], avg_out), (mom, mom_out), (w, new_out)]
+    other = half - b * half
+    final = [(total, sum_out.at[pl.ds(pl.multiple_of(b * half, 16), half)]), (total2, sum_out.at[pl.ds(pl.multiple_of(other, 16), half)])]
     final = [pltpu.make_async_copy(src, dst, load_sem.at[7 + i]) for i, (src, dst) in enumerate(final)]
     for copy in final:
         copy.start()
@@ -1232,23 +1216,23 @@
         copy.wait()
 
 
-def update(red, weights, first, second, momentum):
+def update(red, first, second):
     hbm = pl.BlockSpec(memory_space=pl.ANY)
     V = pltpu.VMEM
     flat = jax.ShapeDtypeStruct((SHARD, 128), F32)
     dma = pltpu.SemaphoreType.DMA
     return pl.pallas_call(
         update_kernel,
-        out_shape=(flat,) * 5,
-        in_specs=[hbm] * 5,
-        out_specs=(hbm,) * 5,
+        out_shape=(jax.ShapeDtypeStruct((PADDED, 128), F32), flat, flat),
+        in_specs=[hbm] * 3,
+        out_specs=(hbm,) * 3,
         scratch_shapes=[
             V((ROUNDS, UNIT, 16, 128), BF16),
             V((EDGE + SLOT + EDGE, 16, 128), BF16),
             V((BACK_ROWS, 128), F32),
             V((128, 128), F32),
-            V((SHARD, 128), F32),
-            V((SHARD, 128), F32),
+            V((1, SHARD * 128), F32),
+            V((1, SHARD * 128), F32),
             V((SHARD, 128), F32),
             V((SHARD, 128), F32),
             V((PADDED, 128), F32),
@@ -1267,54 +1251,91 @@
         ],
         compiler_params=pltpu.CompilerParams(collective_id=1, has_side_effects=True, vmem_limit_bytes=60 * 1024 * 1024),
         name="update",
-    )(red, weights, first, second, momentum)
-
-
-def move_kernel(*refs):
-    one, two, out_one, out_two, buf_one, buf_two, sem = refs
-
-    def rows(ref):
-        return ref.reshape(SHARD, 128) if ref.shape[0] == 1 else ref
-
-    ins = [pltpu.make_async_copy(rows(src), dst, sem.at[i]) for i, (src, dst) in enumerate(((one, buf_one), (two, buf_two)))]
-    outs = [pltpu.make_async_copy(src, rows(dst), sem.at[2 + i]) for i, (src, dst) in enumerate(((buf_one, out_one), (buf_two, out_two)))]
-    for copy in ins:
+    )(red, first, second)
+
+
+def finish_kernel(
+    sum_ref, w_ref, mom_ref, first_ref, second_ref, loss_ref,
+    avg_out, mom_out, new_out, first_out, second_out, loss_out,
+    total, w, mom, first, second, averaged, sem, out_sem,
+):
+    cut = PADDED // 2
+    pieces = [pl.ds(0, cut), pl.ds(cut, SHARD - cut)]
+    loads = []
+    for i, at in enumerate(pieces):
+        loads.append([pltpu.make_async_copy(src.at[at], dst.at[at], sem.at[3 * i + k]) for k, (src, dst) in enumerate(((sum_ref, total), (w_ref, w), (mom_ref, mom)))])
+    moments = [pltpu.make_async_copy(src, dst, sem.at[6 + i]) for i, (src, dst) in enumerate(((first_ref, first), (second_ref, second)))]
+    for copy in loads[0] + loads[1] + moments:
         copy.start()
-    for i in range(2):
-        ins[i].wait()
-        outs[i].start()
+    outs = []
+
+    def send(src, dst):
+        copy = pltpu.make_async_copy(src, dst, out_sem.at[len(outs)])
+        copy.start()
+        outs.append(copy)
+
+    loss_out[...] = loss_ref[0:1, 0:1]
+
+    def outer(r, n):
+        at = pl.ds(r, n)
+        old = w[at, :]
+        mean = INNER_RATE * (total[at, :] * 0.25 + DECAY * old)
+        momentum = OUTER_MU * mom[at, :] + mean
+        averaged[at, :] = mean
+        mom[at, :] = momentum
+        w[at, :] = old - OUTER_RATE * (mean + OUTER_MU * momentum)
+
+    def block(i, carry):
+        outer(pl.multiple_of(i * 96, 96), 96)
+        return carry
+
+    for i, at in enumerate(pieces):
+        for copy in loads[i]:
+            copy.wait()
+        if i == 0:
+            lax.fori_loop(0, cut // 96, block, 0)
+        else:
+            lax.fori_loop(cut // 96, SHARD // 96, block, 0)
+            outer(SHARD // 96 * 96, SHARD - SHARD // 96 * 96)
+        for src, dst in ((averaged, avg_out), (mom, mom_out), (w, new_out)):
+            send(src.at[at], dst.at[at])
+        if i == 0:
+            for copy, src, dst in zip(moments, (first, second), (first_out, second_out)):
+                copy.wait()
+                send(src, dst.reshape(SHARD, 128))
     for copy in outs:
         copy.wait()
 
 
-def move(one, two, shape, name):
+def finish(total, weights, momentum, first, second, loss):
     hbm = pl.BlockSpec(memory_space=pl.ANY)
-    shape = jax.ShapeDtypeStruct(shape, F32)
-    rows = pltpu.VMEM((SHARD, 128), F32)
+    vmem = pl.BlockSpec(memory_space=pltpu.VMEM)
+    V = pltpu.VMEM
+    rows = jax.ShapeDtypeStruct((SHARD, 128), F32)
+    row = jax.ShapeDtypeStruct((1, SHARD * 128), F32)
     return pl.pallas_call(
-        move_kernel,
-        out_shape=(shape,) * 2,
-        in_specs=[hbm] * 2,
-        out_specs=(hbm,) * 2,
-        scratch_shapes=[rows, rows, pltpu.SemaphoreType.DMA((4,))],
+        finish_kernel,
+        out_shape=(rows,) * 3 + (row,) * 2 + (jax.ShapeDtypeStruct((1, 1), F32),),
+        in_specs=[hbm] * 5 + [vmem],
+        out_specs=(hbm,) * 5 + (vmem,),
+        scratch_shapes=[V((PADDED, 128), F32)] + [V((SHARD, 128), F32)] * 5 + [pltpu.SemaphoreType.DMA((8,)), pltpu.SemaphoreType.DMA((8,))],
         compiler_params=pltpu.CompilerParams(vmem_limit_bytes=60 * 1024 * 1024),
-        name=name,
-    )(one, two)
+        name="finish",
+    )(total, weights, momentum, first, second, loss)
 
 
 def body(patches, labels, counts, weights, first_moments, second_moments, outer_momentum):
     flat = weights.reshape(SHARD, 128)
-    first, second = move(first_moments, second_moments, (SHARD, 128), "as_rows")
-    reduced, losses = grads(flat, patches.reshape(2, P_SIZE, D), labels.reshape(2), counts.reshape(2))
-    averaged, momentum, new_weights, first, second = update(reduced, flat, first, second, outer_momentum.reshape(SHARD, 128))
-    first, second = move(first, second, (1, SHARD * 128), "as_flat")
+    reduced, loss = grads(flat, patches.reshape(2, P_SIZE, D), labels.reshape(2), counts.reshape(2))
+    total, first, second = update(reduced, first_moments, second_moments)
+    averaged, momentum, new_weights, first, second, loss = finish(total, flat, outer_momentum.reshape(SHARD, 128), first, second, loss)
     return (
         averaged.reshape(-1),
         momentum.reshape(-1),
         new_weights.reshape(-1),
         first,
         second,
-        losses[:1, :1],
+        loss,
     )
 
 

time: 224 us -> 213 us (0.951)
  local copies, waits for them, and re-layouts: 7.42 us -> 1.95 us
  Pallas kernels: 215 us -> 210 us
    unnamed x10 -> x1, local copies, waits for them, and re-layouts: 6.25 us -> 1.95 us
    pallas_call x1, Pallas kernels: 172 us -> 168 us  [grads(): pl.pallas_call(grads_kernel, out_shape=(jax.ShapeDtypeStruct((ROUNDS, UNI...]
    pallas_call x3 -> x2, Pallas kernels: 43.5 us -> 41.5 us  [the longest x1 36.1 us: update(): pl.pallas_call(update_kernel, out_shape=(jax.ShapeDtypeStruct((PADDED, 12...]
where the time goes in v5:
time: 213 us
  Pallas kernels  210 us (99%)
    pallas_call x1, Pallas kernels, grads(): pl.pallas_call(grads_kernel, out_shape=(jax.ShapeDtypeStruct((ROUNDS, UNI...  168 us
    pallas_call x1, Pallas kernels, update(): pl.pallas_call(update_kernel, out_shape=(jax.ShapeDtypeStruct((PADDED, 12...  36.1 us
    pallas_call x1, Pallas kernels, finish(): pl.pallas_call(finish_kernel, out_shape=(rows,) * 3 + (row,) * 2 + (jax.S...  5.38 us

profile of v5, /device:TPU:24, one launch (start us, length us, event | category | flops | bytes accessed | tf_op | source)
XLA Modules:
  0.0 212.7 jit_solution(7831596032841603258)
XLA Ops:
  0.6 2.0 copy.15
  2.6 168.4 %grads.1 = (bf16[22,6,16,128]{3,2,1,0:T(8,128)(2,1)}, f32[8,128]{1,0:T(8,128)}) custom-call(f32[2098,128]{1,0:T(8,128)} %bitcast.10, bf16[2,196,768]{2,1,0:T(8,128)(2,1)} %bitcast.12, s32[2]{0:T(128)} %bitcast.14, s32[2]{0:T(128)} %bitcast.15), custom_call_target="tpu_custom_call" | custom-call | tf_op jit(solution)/shard_map/grads/pallas_call | solution.py:890
  171.0 36.1 %update.1 = (f32[2112,128]{1,0:T(8,128)}, f32[2098,128]{1,0:T(8,128)}, f32[2098,128]{1,0:T(8,128)}) custom-call(bf16[22,6,16,128]{3,2,1,0:T(8,128)(2,1)} %get-tuple-element.17.red_ref, f32[1,268544]{1,0:T(1,128)} %first_ref.1, f32[1,268544]{1,0:T(1,128)} %second_ref.1), custom_call_target="tpu_custom_call" | custom-call | tf_op jit(solution)/shard_map/update/pallas_call | solution.py:1224
  207.2 5.4 %finish.1 = (f32[2098,128]{1,0:T(8,128)}, f32[2098,128]{1,0:T(8,128)}, f32[2098,128]{1,0:T(8,128)}, f32[1,268544]{1,0:T(1,128)}, f32[1,268544]{1,0:T(1,128)}, /*index=5*/f32[1,1]{1,0:T(1,128)}) custom-call(f32[2112,128]{1,0:T(8,128)} %get-tuple-element.18.sum_ref, f32[2098,128]{1,0:T(8,128)} %bitcast.11, f32[2098,128]{1,0:T(8,128)} %bitcast.13, ...), custom_call_target="tpu_custom_call" | custom-call | tf_op jit(solution)/shard_map/finish/pallas_call | solution.py:1316

commit v6 on v5

--- a/solution.py
+++ b/solution.py
@@ -59,6 +59,10 @@
     def at_z(self, k):
         return device(self.xl, self.a, self.b, lax.rem(self.z + k, 4), self.y)
 
+    def at_x(self, k):
+        a = lax.rem(self.a + (self.xl if k == 1 else 1 - self.xl), 2)
+        return device(1 - self.xl, a, self.b, self.z, self.y)
+
     def go(self, src, dst, send, recv, target):
         copy = pltpu.make_async_remote_copy(src_ref=src, dst_ref=dst, send_sem=send, recv_sem=recv, device_id=target, device_id_type=MESH)
         copy.start()
@@ -83,15 +87,26 @@
     def second_axis(self, h, k):
         return (self.at_z if h == 0 else self.at_y)(k)
 
+    def gathered(self, i, h):
+        lo, hi = STAGES[i]
+        n = (hi - lo) // 2
+        if i == 0:
+            return pl.ds(lo + h * n, n)
+        return pl.ds(lo + h * n + self.xl, 2)
+
+    def single(self, i, h, own):
+        lo, hi = STAGES[i]
+        parity = self.xl if own else 1 - self.xl
+        return pl.ds(lo + h * ((hi - lo) // 2) + 2 * parity, 1)
+
     def one(self, i, h, k, q=None):
-        rd = self.span(i, h)
+        rd = self.gathered(i, h)
         t = pl.ds(0, UNIT) if q is None else pl.ds(3 * q, 3)
         if h == 0:
             return self.T5.at[rd, self.z, self.b, lax.rem(self.y + k, 4), t]
         return self.T5.at[rd, lax.rem(self.z + k, 4), self.b, self.y, t]
 
-    def row(self, i, h, k, core=None, p=None):
-        rd = self.span(i, h)
+    def row(self, rd, h, k, core=None, p=None):
         core = self.b if core is None else core
         t = pl.ds(0, 4) if p is None else pl.ds(2 * p, 2)
         if h == 0:
@@ -99,7 +114,7 @@
         return self.T5.at[rd, t, core, lax.rem(self.y + k, 4)]
 
     def gsem(self, i, h, k):
-        n = (i * 2 + h) * 12 + k
+        n = (i * 2 + h) * 24 + k
         return self.g_send.at[n], self.g_recv.at[n]
 
     def gather_go(self, i, h, k, view, target):
@@ -108,8 +123,16 @@
     def gather_wait(self, i, h, k, view):
         self.landed(view, *self.gsem(i, h, k))
 
+    def share(self, i, h, m, k):
+        self.gather_go(i, h, 8 + m, self.row(self.gathered(i, h), h, k), self.sibling)
+        if i > 0:
+            rd = self.single(i, h, True)
+            self.gather_go(i, h, 12 + m, self.row(rd, h, k, p=0), self.at_x(1))
+            self.gather_go(i, h, 16 + m, self.row(rd, h, k, p=1), self.at_x(3))
+
     def gather_step(self, i, step):
         for h in range(2):
+            rd = self.gathered(i, h)
             if step == 0:
                 self.gather_go(i, h, 0, self.one(i, h, 0), self.first_axis(h, 1))
                 self.gather_go(i, h, 1, self.one(i, h, 0), self.first_axis(h, 3))
@@ -121,23 +144,32 @@
             elif step == 2:
                 self.gather_wait(i, h, 2, self.one(i, h, 2, 0))
                 self.gather_wait(i, h, 3, self.one(i, h, 2, 1))
-                self.gather_go(i, h, 4, self.row(i, h, 0), self.second_axis(h, 1))
-                self.gather_go(i, h, 5, self.row(i, h, 0), self.second_axis(h, 3))
-                self.gather_go(i, h, 8, self.row(i, h, 0), self.sibling)
+                self.gather_go(i, h, 4, self.row(rd, h, 0), self.second_axis(h, 1))
+                self.gather_go(i, h, 5, self.row(rd, h, 0), self.second_axis(h, 3))
+                self.share(i, h, 0, 0)
             elif step == 3:
-                self.gather_wait(i, h, 4, self.row(i, h, 3))
-                self.gather_go(i, h, 6, self.row(i, h, 3, p=0), self.second_axis(h, 1))
-                self.gather_go(i, h, 9, self.row(i, h, 3), self.sibling)
-                self.gather_wait(i, h, 5, self.row(i, h, 1))
-                self.gather_go(i, h, 7, self.row(i, h, 1, p=1), self.second_axis(h, 3))
-                self.gather_go(i, h, 10, self.row(i, h, 1), self.sibling)
+                self.gather_wait(i, h, 4, self.row(rd, h, 3))
+                self.gather_go(i, h, 6, self.row(rd, h, 3, p=0), self.second_axis(h, 1))
+                self.share(i, h, 1, 3)
+                self.gather_wait(i, h, 5, self.row(rd, h, 1))
+                self.gather_go(i, h, 7, self.row(rd, h, 1, p=1), self.second_axis(h, 3))
+                self.share(i, h, 2, 1)
             elif step == 4:
-                self.gather_wait(i, h, 6, self.row(i, h, 2, p=0))
-                self.gather_wait(i, h, 7, self.row(i, h, 2, p=1))
-                self.gather_go(i, h, 11, self.row(i, h, 2), self.sibling)
+                self.gather_wait(i, h, 6, self.row(rd, h, 2, p=0))
+                self.gather_wait(i, h, 7, self.row(rd, h, 2, p=1))
+                self.share(i, h, 3, 2)
+            elif step == 5:
+                if i > 0:
+                    other = self.single(i, h, False)
+                    for m, k in enumerate((0, 3, 1, 2)):
+                        self.gather_wait(i, h, 12 + m, self.row(other, h, k, p=0))
+                        self.gather_wait(i, h, 16 + m, self.row(other, h, k, p=1))
+                        self.gather_go(i, h, 20 + m, self.row(other, h, k), self.sibling)
             else:
-                for k, offset in ((8, 0), (9, 3), (10, 1), (11, 2)):
-                    self.gather_wait(i, h, k, self.row(i, h, offset, core=1 - self.b))
+                for m, k in enumerate((0, 3, 1, 2)):
+                    self.gather_wait(i, h, 8 + m, self.row(rd, h, k, core=1 - self.b))
+                    if i > 0:
+                        self.gather_wait(i, h, 20 + m, self.row(self.single(i, h, False), h, k, core=1 - self.b))
 
     def rsem(self, i, h, k):
         n = (i * 2 + h) * 13 + k
@@ -172,7 +204,7 @@
         T5 = self.T5
 
         def send_a(k, ka, p, shift):
-            self.go(self.row(i, h, ka, p=p), self.RA.at[k, rd], *self.rsem(i, h, 1 + k), self.second_axis(h, shift))
+            self.go(self.row(rd, h, ka, p=p), self.RA.at[k, rd], *self.rsem(i, h, 1 + k), self.second_axis(h, shift))
 
         def wait_a(k):
             self.landed(self.RA.at[k, rd], *self.rsem(i, h, 1 + k))
@@ -204,16 +236,16 @@
             send_a(3, 3, 0, 3)
         elif step == 2:
             wait_a(0)
-            self.add(self.row(i, h, 1, p=0), self.RA.at[0, rd], inner=2)
+            self.add(self.row(rd, h, 1, p=0), self.RA.at[0, rd], inner=2)
             send_a(4, 1, 0, 1)
             wait_a(1)
-            self.add(self.row(i, h, 3, p=1), self.RA.at[1, rd], inner=2)
+            self.add(self.row(rd, h, 3, p=1), self.RA.at[1, rd], inner=2)
             send_a(5, 3, 1, 3)
         elif step == 3:
             for k in (2, 3, 4, 5):
                 wait_a(k)
-            self.add(self.row(i, h, 0, p=0), self.RA.at[3, rd], self.RA.at[4, rd], inner=2)
-            self.add(self.row(i, h, 0, p=1), self.RA.at[2, rd], self.RA.at[5, rd], inner=2)
+            self.add(self.row(rd, h, 0, p=0), self.RA.at[3, rd], self.RA.at[4, rd], inner=2)
+            self.add(self.row(rd, h, 0, p=1), self.RA.at[2, rd], self.RA.at[5, rd], inner=2)
             send_b(0, 2, 0, 1)
             send_b(1, 2, 1, 3)
             send_b(2, 1, 1, 1)
@@ -255,7 +287,10 @@
     def greet(target):
         pl.semaphore_signal(barrier, inc=1, device_id=target, device_id_type=MESH)
 
-    for target in (up, down, links.at_y(1), links.at_y(3), links.at_z(1), links.at_z(3), links.sibling):
+    def wanted(j, parity):
+        return jnp.logical_or(j < STAGES[0][1], lax.rem(j + 3 - STAGES[0][1] % 3, 3) != 2 * (1 - parity))
+
+    for target in (up, down, links.at_x(1), links.at_x(3), links.at_y(1), links.at_y(3), links.at_z(1), links.at_z(3), links.sibling):
         greet(target)
 
     @pl.when(swap)
@@ -269,14 +304,20 @@
         s = lax.div(32 * j + holder, ROUNDS)
         sa = lax.rem(lax.div(s, 4), 2)
 
-        @pl.when(jnp.logical_not(jnp.logical_and(keeps, s == fs)))
+        @pl.when(jnp.logical_and(wanted(j, xl), jnp.logical_not(jnp.logical_and(keeps, s == fs))))
         def _():
             greet(device(lax.rem(xl + sa + a, 2), sa, a, lax.div(s, 8), lax.rem(s, 4)))
 
         return carry
 
     lax.fori_loop(0, ROUNDS, greet_source, 0)
-    pl.semaphore_wait(barrier, 7 + ROUNDS + jnp.where(swap, 1, 0) - jnp.where(keeps, 1, 0))
+    def unit_goes(i):
+        there = wanted(lax.div(ROUNDS * fs + i, 32), xo)
+        stays = jnp.logical_and(keeps, i == own_index)
+        return jnp.logical_and(there, jnp.logical_not(stays)), jnp.logical_and(there, stays)
+
+    outgoing = lax.fori_loop(0, ROUNDS, lambda i, n: n + jnp.where(unit_goes(i)[0], 1, 0), 9)
+    pl.semaphore_wait(barrier, outgoing + jnp.where(swap, 1, 0))
     load.wait()
 
     def remote(src, dst, k, target):
@@ -301,18 +342,18 @@
         src = slot.at[pl.ds(UNIT * i, UNIT)]
         dst = T.at[pl.ds(UNIT * k, UNIT)]
         target = device(xo, b, lax.rem(lax.div(d, 4), 2), lax.div(d, 8), lax.rem(d, 4))
-        mine = jnp.logical_and(keeps, i == own_index)
         away = pltpu.make_async_remote_copy(src_ref=src, dst_ref=dst, send_sem=u_send.at[i], recv_sem=u_recv.at[lax.div(k, 32)], device_id=target, device_id_type=MESH)
-        return mine, away, (src, dst)
+        return away, (src, dst)
 
     def send_unit(i):
-        mine, away, (src, dst) = unit_copy(i)
-
-        @pl.when(mine)
+        away, (src, dst) = unit_copy(i)
+        goes, stays = unit_goes(i)
+
+        @pl.when(stays)
         def _():
             pltpu.make_async_copy(src, dst, local_sem.at[3]).start()
 
-        @pl.when(jnp.logical_not(mine))
+        @pl.when(goes)
         def _():
             away.start()
 
@@ -403,11 +444,11 @@
             place = T.at[pl.ds(UNIT * (32 * j + holder), UNIT)]
             mine = jnp.logical_and(keeps, lax.div(32 * j + holder, ROUNDS) == fs)
 
-            @pl.when(mine)
+            @pl.when(jnp.logical_and(wanted(j, xl), mine))
             def _():
                 pltpu.make_async_copy(place, place, local_sem.at[3]).wait()
 
-            @pl.when(jnp.logical_not(mine))
+            @pl.when(jnp.logical_and(wanted(j, xl), jnp.logical_not(mine)))
             def _():
                 pltpu.make_async_remote_copy(src_ref=place, dst_ref=place, send_sem=u_send.at[0], recv_sem=u_recv.at[j], device_id=links.sibling, device_id_type=MESH).wait_recv()
 
@@ -417,9 +458,9 @@
 
     def finish_start():
         def wait(i, carry):
-            mine, away, unused = unit_copy(i)
-
-            @pl.when(jnp.logical_not(mine))
+            away, unused = unit_copy(i)
+
+            @pl.when(unit_goes(i)[0])
             def _():
                 away.wait_send()
 
@@ -776,14 +817,13 @@
 
 
 FORWARD = {
-    "start": ((0, 0), (1, 0), (0, 1), (0, 2), (1, 1), (2, 0), (0, 3), (1, 2), (0, 4), (2, 1), (3, 0), (0, 5)),
-    "embedded": ((1, 3), (2, 2), (3, 1)),
-    "qkv": ((1, 4), (1, 5), (3, 2)),
-    "attend0": ((2, 3),),
-    "attend1": ((3, 3), (2, 4)),
-    "attend2": ((3, 4),),
-    "up": ((2, 5),),
-    "down": ((3, 5),),
+    "start": ((0, 0), (1, 0), (0, 1), (0, 2), (1, 1), (2, 0), (0, 3), (1, 2), (0, 4), (2, 1), (3, 0), (1, 3), (0, 6)),
+    "embedded": ((2, 2), (3, 1)),
+    "qkv": ((1, 4), (3, 2), (2, 3), (1, 5), (2, 4), (1, 6)),
+    "attend0": ((3, 3),),
+    "attend1": ((3, 4), (2, 5)),
+    "up": ((2, 6), (3, 5)),
+    "down": ((3, 6),),
 }
 BACKWARD = {
     "fc_out0": ((3, 0, 0),),
@@ -792,13 +832,12 @@
     "fc_in2": ((2, 0, 0),),
     "fc_in3": ((2, 1, 0), (2, 0, 1)),
     "normed2": ((2, 1, 1),),
-    "out": ((3, 0, 2), (3, 1, 2)),
-    "back3": ((2, 0, 2), (2, 1, 2)),
-    "qkv_back": ((1, 0, 0), (1, 1, 0), (1, 0, 1), (1, 1, 1), (3, 0, 3), (3, 1, 3)),
+    "back1": ((3, 0, 2), (3, 1, 2)),
+    "qkv_back": ((1, 0, 0), (1, 1, 0), (2, 0, 2), (2, 1, 2), (1, 0, 1), (1, 1, 1), (3, 0, 3), (3, 1, 3)),
     "norms": ((0, 1, 0),),
     "embed": (
-        (0, 0, 0), (0, 1, 1), (0, 0, 1), (2, 0, 3), (2, 1, 3), (1, 0, 2), (1, 1, 2), (3, 0, 4), (3, 1, 4), (0, 1, 2), (0, 0, 2), (2, 0, 4), (2, 1, 4),
-        (1, 0, 3), (1, 1, 3), (3, 0, 5), (3, 1, 5), (0, 1, 3), (0, 0, 3), (2, 0, 5), (2, 1, 5), (1, 0, 4), (1, 1, 4), (0, 1, 4), (0, 0, 4), (1, 0, 5), (1, 1, 5), (0, 1, 5), (0, 0, 5),
+        (0, 0, 0), (0, 1, 1), (0, 0, 1), (3, 0, 4), (3, 1, 4), (2, 0, 3), (2, 1, 3), (1, 0, 2), (1, 1, 2), (3, 0, 5), (3, 1, 5), (2, 0, 4), (2, 1, 4),
+        (0, 1, 2), (0, 0, 2), (1, 0, 3), (1, 1, 3), (2, 0, 5), (2, 1, 5), (0, 1, 3), (0, 0, 3), (1, 0, 4), (1, 1, 4), (0, 1, 4), (0, 0, 4), (1, 0, 5), (1, 1, 5), (0, 1, 5), (0, 0, 5),
     ),
 }
 
@@ -897,8 +936,8 @@
             V((ROUNDS, 4, 4, UNIT, 16, 128), BF16),
             V((6, ROUNDS, 2, UNIT, 16, 128), BF16),
             V((6, ROUNDS, 3, 16, 128), BF16),
-            dma((96,)),
-            dma((96,)),
+            dma((192,)),
+            dma((192,)),
             dma((104,)),
             dma((104,)),
             V((12, 8, 128), F32),

time: 213 us -> 209 us (0.981)
  Pallas kernels: 210 us -> 206 us
    pallas_call x1, Pallas kernels: 168 us -> 165 us  [grads(): pl.pallas_call(grads_kernel, out_shape=(jax.ShapeDtypeStruct((ROUNDS, UNI...]
where the time goes in v6:
time: 209 us
  Pallas kernels  206 us (99%)
    pallas_call x1, Pallas kernels, grads(): pl.pallas_call(grads_kernel, out_shape=(jax.ShapeDtypeStruct((ROUNDS, UNI...  165 us
    pallas_call x1, Pallas kernels, update(): pl.pallas_call(update_kernel, out_shape=(jax.ShapeDtypeStruct((PADDED, 12...  35.5 us
    pallas_call x1, Pallas kernels, finish(): pl.pallas_call(finish_kernel, out_shape=(rows,) * 3 + (row,) * 2 + (jax.S...  5.38 us

profile of v6, /device:TPU:24, one launch (start us, length us, event | category | flops | bytes accessed | tf_op | source)
XLA Modules:
  0.0 209.1 jit_solution(16647408871367904034)
XLA Ops:
  0.6 2.0 copy.15
  2.6 165.5 %grads.1 = (bf16[22,6,16,128]{3,2,1,0:T(8,128)(2,1)}, f32[8,128]{1,0:T(8,128)}) custom-call(f32[2098,128]{1,0:T(8,128)} %bitcast.10, bf16[2,196,768]{2,1,0:T(8,128)(2,1)} %bitcast.12, s32[2]{0:T(128)} %bitcast.14, s32[2]{0:T(128)} %bitcast.15), custom_call_target="tpu_custom_call" | custom-call | tf_op jit(solution)/shard_map/grads/pallas_call | solution.py:929
  168.1 35.5 %update.1 = (f32[2112,128]{1,0:T(8,128)}, f32[2098,128]{1,0:T(8,128)}, f32[2098,128]{1,0:T(8,128)}) custom-call(bf16[22,6,16,128]{3,2,1,0:T(8,128)(2,1)} %get-tuple-element.17.red_ref, f32[1,268544]{1,0:T(1,128)} %first_ref.1, f32[1,268544]{1,0:T(1,128)} %second_ref.1), custom_call_target="tpu_custom_call" | custom-call | tf_op jit(solution)/shard_map/update/pallas_call | solution.py:1263
  203.6 5.4 %finish.1 = (f32[2098,128]{1,0:T(8,128)}, f32[2098,128]{1,0:T(8,128)}, f32[2098,128]{1,0:T(8,128)}, f32[1,268544]{1,0:T(1,128)}, f32[1,268544]{1,0:T(1,128)}, /*index=5*/f32[1,1]{1,0:T(1,128)}) custom-call(f32[2112,128]{1,0:T(8,128)} %get-tuple-element.18.sum_ref, f32[2098,128]{1,0:T(8,128)} %bitcast.11, f32[2098,128]{1,0:T(8,128)} %bitcast.13, ...), custom_call_target="tpu_custom_call" | custom-call | tf_op jit(solution)/shard_map/finish/pallas_call | solution.py:1355

commit v7 on v6

--- a/solution.py
+++ b/solution.py
@@ -817,13 +817,17 @@
 
 
 FORWARD = {
-    "start": ((0, 0), (1, 0), (0, 1), (0, 2), (1, 1), (2, 0), (0, 3), (1, 2), (0, 4), (2, 1), (3, 0), (1, 3), (0, 6)),
-    "embedded": ((2, 2), (3, 1)),
-    "qkv": ((1, 4), (3, 2), (2, 3), (1, 5), (2, 4), (1, 6)),
-    "attend0": ((3, 3),),
-    "attend1": ((3, 4), (2, 5)),
-    "up": ((2, 6), (3, 5)),
-    "down": ((3, 6),),
+    "start": (
+        (0, 0), (1, 0), (2, 0), (3, 0), (0, 1), (2, 1), (1, 1), (0, 2), (1, 2), (0, 3), (1, 3), (2, 2),
+        (1, 4), (0, 4), (0, 6), (3, 1), (2, 3),
+    ),
+    "embedded": ((1, 5), (3, 2),),
+    "qkv": ((1, 6),),
+    "attend0": ((2, 4),),
+    "attend2": ((3, 3),),
+    "attend3": ((2, 5),),
+    "up": ((2, 6), (3, 4),),
+    "down": ((3, 5), (3, 6),),
 }
 BACKWARD = {
     "fc_out0": ((3, 0, 0),),
@@ -897,7 +901,7 @@
                 loss_out[...] = LS[10]
 
     loss_swap = pltpu.make_async_remote_copy(src_ref=LS.at[10], dst_ref=LS.at[11], send_sem=l_send.at[11], recv_sem=l_recv.at[11], device_id=mirror, device_id_type=MESH)
-    losses = {"fc_out0": 0, "fc_in0": 1, "fc_in2": 2, "normed2": 3, "back0": 4, "back2": 5, "qkv_back": 6}
+    losses = {"fc_out0": 0, "fc_in2": 1, "out": 2, "back1": 3, "back3": 4, "norms": 5}
 
     def step(name):
         if name == "pool":
@@ -914,6 +918,7 @@
             loss_step(losses[name])
 
     compute(step, patch_in, meta_in, loss, T, *compute_refs)
+    loss_step(6)
     mine = T.reshape(ROUNDS, 32, UNIT, 16, 128).at[:, z * 8 + b * 4 + y]
     out = pltpu.make_async_copy(mine, red_ref, out_sem)
     out.start()
@@ -1000,7 +1005,7 @@
 def update_kernel(
     red_ref, first_ref, second_ref,
     sum_out, first_out, second_out,
-    red, window, flat, headrows, first_row, second_row, first, second, upd, low, low2, pair, pair2, total, total2,
+    red, window, flat, headrows, first_row, second_row, first, second, low, low2, pair, pair2, total, total2,
     load_sem, x_send, x_recv, o_send, e_send, w_recv,
 ):
     xl, b, z, a, y = coords()
@@ -1195,51 +1200,49 @@
     fix_one = 1.0 / (1.0 - BETA_ONE**STEP)
     fix_two = 1.0 / (1.0 - BETA_TWO**STEP)
 
-    def in_rows(fn, lo, hi, step=32):
-        def body(i, carry):
+    half = PADDED // 2
+    step = 96
+    for rows_of in (first, second):
+        rows_of[pl.ds(SHARD, PADDED - SHARD), :] = jnp.zeros((PADDED - SHARD, 128), F32)
+
+    def in_half(fn):
+        def rows_step(i, carry):
             fn(pl.multiple_of(i * step, step), step)
             return carry
 
-        n = (hi - lo) // step
-        lax.fori_loop(lo // step, lo // step + n, body, 0)
-        if lo + n * step < hi:
-            fn(lo + n * step, hi - lo - n * step)
-
-    def adam(r, n):
-        grad = flat[pl.ds(FRONT + r, n), :]
-        m = BETA_ONE * first[pl.ds(r, n), :] + (1.0 - BETA_ONE) * grad
-        s = BETA_TWO * second[pl.ds(r, n), :] + (1.0 - BETA_TWO) * grad * grad
-        first[pl.ds(r, n), :] = m
-        second[pl.ds(r, n), :] = s
-        u = (m * fix_one) / (jnp.sqrt(s * fix_two) + ADAM_EPS)
-        upd[pl.ds(r, n), :] = u
-
-    in_rows(adam, 0, SHARD)
-    upd[pl.ds(SHARD, PADDED - SHARD), :] = jnp.zeros((PADDED - SHARD, 128), F32)
-    outs = [pltpu.make_async_copy(src, dst, load_sem.at[5 + i]) for i, (src, dst) in enumerate(((first, first_out), (second, second_out)))]
+        lax.fori_loop(0, half // step, rows_step, 0)
+
+    def adam_half(q):
+        def adam(r, n):
+            at = pl.ds(pl.multiple_of(q * half + r, 16), n)
+            grad = flat[pl.ds(pl.multiple_of(FRONT + q * half + r, 16), n), :]
+            m = BETA_ONE * first[at, :] + (1.0 - BETA_ONE) * grad
+            s = BETA_TWO * second[at, :] + (1.0 - BETA_TWO) * grad * grad
+            first[at, :] = m
+            second[at, :] = s
+            low[at, :] = ((m * fix_one) / (jnp.sqrt(s * fix_two) + ADAM_EPS)).astype(BF16)
+
+        in_half(adam)
+
+    adam_half(1 - b)
+    go(low.at[pl.ds(pl.multiple_of((1 - b) * half, 16), half)], low2, x_send, x_recv, 0, sibling)
+    adam_half(b)
+    outs = [pltpu.make_async_copy(src.at[pl.ds(0, SHARD)], dst, load_sem.at[5 + i]) for i, (src, dst) in enumerate(((first, first_out), (second, second_out)))]
     for copy in outs:
         copy.start()
-
-    def lower(r, n):
-        low[pl.ds(r, n), :] = upd[pl.ds(r, n), :].astype(BF16)
-
-    in_rows(lower, 0, PADDED)
-    go(low, low2, x_send, x_recv, 0, sibling)
     arrive(low2, x_recv, 0)
-    half = PADDED // 2
 
     def pairs(r, n):
-        at = pl.ds(pl.multiple_of(b * half + r, 16), n)
-        pair[pl.ds(r, n), :] = low[at, :] + low2[at, :]
-
-    in_rows(pairs, 0, half)
+        pair[pl.ds(r, n), :] = low[pl.ds(pl.multiple_of(b * half + r, 16), n), :] + low2[pl.ds(r, n), :]
+
+    in_half(pairs)
     go(pair, pair2, x_send, x_recv, 1, across)
     arrive(pair2, x_recv, 1)
 
     def fours(r, n):
         total[pl.ds(r, n), :] = pair[pl.ds(r, n), :].astype(F32) + pair2[pl.ds(r, n), :].astype(F32)
 
-    in_rows(fours, 0, half)
+    in_half(fours)
     go(total, total2, x_send, x_recv, 2, sibling)
 
     arrive(total2, x_recv, 2)
@@ -1272,11 +1275,10 @@
             V((128, 128), F32),
             V((1, SHARD * 128), F32),
             V((1, SHARD * 128), F32),
-            V((SHARD, 128), F32),
-            V((SHARD, 128), F32),
+            V((PADDED, 128), F32),
             V((PADDED, 128), F32),
             V((PADDED, 128), BF16),
-            V((PADDED, 128), BF16),
+            V((PADDED // 2, 128), BF16),
             V((PADDED // 2, 128), BF16),
             V((PADDED // 2, 128), BF16),
             V((PADDED // 2, 128), F32),

time: 209 us -> 199 us (0.952); the launches traced: 209 us -> 196 us
  Pallas kernels: 206 us -> 193 us
    pallas_call x1, Pallas kernels: 165 us -> 156 us  [grads(): pl.pallas_call(grads_kernel, out_shape=(jax.ShapeDtypeStruct((ROUNDS, UNI...]
    pallas_call x1, Pallas kernels: 35.5 us -> 31.8 us  [update(): pl.pallas_call(update_kernel, out_shape=(jax.ShapeDtypeStruct((PADDED, 12...]
where the time goes in v7:
time: 199 us; the launch traced here: 196 us
  Pallas kernels  193 us (97%)
    pallas_call x1, Pallas kernels, grads(): pl.pallas_call(grads_kernel, out_shape=(jax.ShapeDtypeStruct((ROUNDS, UNI...  156 us
    pallas_call x1, Pallas kernels, update(): pl.pallas_call(update_kernel, out_shape=(jax.ShapeDtypeStruct((PADDED, 12...  31.8 us
    pallas_call x1, Pallas kernels, finish(): pl.pallas_call(finish_kernel, out_shape=(rows,) * 3 + (row,) * 2 + (jax.S...  5.38 us

profile of v7, /device:TPU:24, one launch (start us, length us, event | category | flops | bytes accessed | tf_op | source)
XLA Modules:
  0.0 195.9 jit_solution(11731872988093862328)
XLA Ops:
  0.6 2.0 copy.15
  2.6 155.9 %grads.1 = (bf16[22,6,16,128]{3,2,1,0:T(8,128)(2,1)}, f32[8,128]{1,0:T(8,128)}) custom-call(f32[2098,128]{1,0:T(8,128)} %bitcast.10, bf16[2,196,768]{2,1,0:T(8,128)(2,1)} %bitcast.12, s32[2]{0:T(128)} %bitcast.14, s32[2]{0:T(128)} %bitcast.15), custom_call_target="tpu_custom_call" | custom-call | tf_op jit(solution)/shard_map/grads/pallas_call | solution.py:934
  158.5 31.8 %update.1 = (f32[2112,128]{1,0:T(8,128)}, f32[2098,128]{1,0:T(8,128)}, f32[2098,128]{1,0:T(8,128)}) custom-call(bf16[22,6,16,128]{3,2,1,0:T(8,128)(2,1)} %get-tuple-element.17.red_ref, f32[1,268544]{1,0:T(1,128)} %first_ref.1, f32[1,268544]{1,0:T(1,128)} %second_ref.1), custom_call_target="tpu_custom_call" | custom-call | tf_op jit(solution)/shard_map/update/pallas_call | solution.py:1266
  190.3 5.4 %finish.1 = (f32[2098,128]{1,0:T(8,128)}, f32[2098,128]{1,0:T(8,128)}, f32[2098,128]{1,0:T(8,128)}, f32[1,268544]{1,0:T(1,128)}, f32[1,268544]{1,0:T(1,128)}, /*index=5*/f32[1,1]{1,0:T(1,128)}) custom-call(f32[2112,128]{1,0:T(8,128)} %get-tuple-element.18.sum_ref, f32[2098,128]{1,0:T(8,128)} %bitcast.11, f32[2098,128]{1,0:T(8,128)} %bitcast.13, ...), custom_call_target="tpu_custom_call" | custom-call | tf_op jit(solution)/shard_map/finish/pallas_call | solution.py:1357

commit v8 on v7

--- a/solution.py
+++ b/solution.py
@@ -830,18 +830,16 @@
     "down": ((3, 5), (3, 6),),
 }
 BACKWARD = {
-    "fc_out0": ((3, 0, 0),),
-    "fc_out1": ((3, 1, 0), (3, 0, 1)),
-    "fc_in0": ((3, 1, 1),),
-    "fc_in2": ((2, 0, 0),),
-    "fc_in3": ((2, 1, 0), (2, 0, 1)),
-    "normed2": ((2, 1, 1),),
-    "back1": ((3, 0, 2), (3, 1, 2)),
-    "qkv_back": ((1, 0, 0), (1, 1, 0), (2, 0, 2), (2, 1, 2), (1, 0, 1), (1, 1, 1), (3, 0, 3), (3, 1, 3)),
-    "norms": ((0, 1, 0),),
+    "fc_out1": ((3, 0, 0), (3, 1, 0),),
+    "fc_in3": ((3, 1, 1), (2, 0, 0), (2, 1, 0), (3, 0, 1),),
+    "back0": ((2, 1, 1), (2, 0, 1),),
+    "back3": ((3, 1, 2), (3, 0, 2),),
+    "qkv_back": ((1, 0, 0), (2, 1, 2),),
+    "norms": ((0, 1, 0), (1, 1, 0), (2, 0, 2),),
     "embed": (
-        (0, 0, 0), (0, 1, 1), (0, 0, 1), (3, 0, 4), (3, 1, 4), (2, 0, 3), (2, 1, 3), (1, 0, 2), (1, 1, 2), (3, 0, 5), (3, 1, 5), (2, 0, 4), (2, 1, 4),
-        (0, 1, 2), (0, 0, 2), (1, 0, 3), (1, 1, 3), (2, 0, 5), (2, 1, 5), (0, 1, 3), (0, 0, 3), (1, 0, 4), (1, 1, 4), (0, 1, 4), (0, 0, 4), (1, 0, 5), (1, 1, 5), (0, 1, 5), (0, 0, 5),
+        (3, 0, 3), (1, 0, 1), (0, 1, 1), (1, 1, 1), (0, 0, 0), (0, 0, 1), (1, 0, 2), (3, 1, 3), (0, 1, 2), (2, 0, 3), (1, 1, 2), (0, 0, 2),
+        (0, 1, 3), (2, 1, 3), (1, 0, 3), (1, 1, 3), (0, 0, 3), (3, 0, 4), (3, 1, 4), (2, 1, 4), (2, 0, 4), (0, 1, 4), (1, 0, 4), (1, 1, 4),
+        (0, 0, 4), (3, 1, 5), (1, 0, 5), (2, 1, 5), (2, 0, 5), (3, 0, 5), (0, 1, 5), (0, 0, 5), (1, 1, 5),
     ),
 }
 

time: 199 us -> 194 us (0.975)
  Pallas kernels: 193 us -> 189 us
    pallas_call x1, Pallas kernels: 156 us -> 150 us  [grads(): pl.pallas_call(grads_kernel, out_shape=(jax.ShapeDtypeStruct((ROUNDS, UNI...]
where the time goes in v8:
time: 194 us; the launch traced here: 192 us
  Pallas kernels  189 us (97%)
  local copies, waits for them, and re-layouts  1.95 us (1%)
    pallas_call x1, Pallas kernels, grads(): pl.pallas_call(grads_kernel, out_shape=(jax.ShapeDtypeStruct((ROUNDS, UNI...  150 us
    pallas_call x1, Pallas kernels, update(): pl.pallas_call(update_kernel, out_shape=(jax.ShapeDtypeStruct((PADDED, 12...  33.3 us
    pallas_call x1, Pallas kernels, finish(): pl.pallas_call(finish_kernel, out_shape=(rows,) * 3 + (row,) * 2 + (jax.S...  5.38 us

profile of v8, /device:TPU:24, one launch (start us, length us, event | category | flops | bytes accessed | tf_op | source)
XLA Modules:
  0.0 191.8 jit_solution(6979453235664952672)
XLA Ops:
  0.6 2.0 %copy.15 = bf16[1,1,2,1,196,768]{5,4,2,3,1,0:T(8,128)(2,1)} copy(bf16[1,1,2,1,196,768]{5,2,4,3,1,0:T(2,128)(2,1)} %param.7) | data formatting | bytes 1204224 | tf_op args[0]
  2.6 150.3 %grads.1 = (bf16[22,6,16,128]{3,2,1,0:T(8,128)(2,1)}, f32[8,128]{1,0:T(8,128)}) custom-call(f32[2098,128]{1,0:T(8,128)} %bitcast.10, bf16[2,196,768]{2,1,0:T(8,128)(2,1)} %bitcast.12, s32[2]{0:T(128)} %bitcast.14, s32[2]{0:T(128)} %bitcast.15), custom_call_target="tpu_custom_call" | custom-call | tf_op jit(solution)/shard_map/grads/pallas_call | solution.py:932
  152.9 33.3 %update.1 = (f32[2112,128]{1,0:T(8,128)}, f32[2098,128]{1,0:T(8,128)}, f32[2098,128]{1,0:T(8,128)}) custom-call(bf16[22,6,16,128]{3,2,1,0:T(8,128)(2,1)} %get-tuple-element.17.red_ref, f32[1,268544]{1,0:T(1,128)} %first_ref.1, f32[1,268544]{1,0:T(1,128)} %second_ref.1), custom_call_target="tpu_custom_call" | custom-call | tf_op jit(solution)/shard_map/update/pallas_call | solution.py:1264
  186.2 5.4 %finish.1 = (f32[2098,128]{1,0:T(8,128)}, f32[2098,128]{1,0:T(8,128)}, f32[2098,128]{1,0:T(8,128)}, f32[1,268544]{1,0:T(1,128)}, f32[1,268544]{1,0:T(1,128)}, /*index=5*/f32[1,1]{1,0:T(1,128)}) custom-call(f32[2112,128]{1,0:T(8,128)} %get-tuple-element.18.sum_ref, f32[2098,128]{1,0:T(8,128)} %bitcast.11, f32[2098,128]{1,0:T(8,128)} %bitcast.13, ...), custom_call_target="tpu_custom_call" | custom-call | tf_op jit(solution)/shard_map/finish/pallas_call | solution.py:1355

commit v9 on v8

--- a/solution.py
+++ b/solution.py
@@ -818,16 +818,16 @@
 
 FORWARD = {
     "start": (
-        (0, 0), (1, 0), (2, 0), (3, 0), (0, 1), (2, 1), (1, 1), (0, 2), (1, 2), (0, 3), (1, 3), (2, 2),
-        (1, 4), (0, 4), (0, 6), (3, 1), (2, 3),
+        (1, 0), (3, 0), (1, 1), (0, 0), (2, 0), (1, 2), (0, 1), (0, 2), (2, 1), (1, 3), (2, 2), (1, 4),
+        (0, 3), (3, 1), (2, 3), (3, 2), (0, 4), (1, 5), (0, 6),
     ),
-    "embedded": ((1, 5), (3, 2),),
-    "qkv": ((1, 6),),
-    "attend0": ((2, 4),),
-    "attend2": ((3, 3),),
-    "attend3": ((2, 5),),
-    "up": ((2, 6), (3, 4),),
-    "down": ((3, 5), (3, 6),),
+    "qkv": ((1, 6), (2, 4),),
+    "attend0": ((3, 3),),
+    "attend1": ((2, 5),),
+    "attend2": ((3, 4),),
+    "attend3": ((2, 6),),
+    "up": ((3, 5),),
+    "down": ((3, 6),),
 }
 BACKWARD = {
     "fc_out1": ((3, 0, 0), (3, 1, 0),),

time: 194 us -> 191 us (0.985)
  Pallas kernels: 189 us -> 186 us
where the time goes in v9:
time: 191 us; the launch traced here: 189 us
  Pallas kernels  186 us (97%)
  local copies, waits for them, and re-layouts  1.95 us (1%)
    pallas_call x1, Pallas kernels, grads(): pl.pallas_call(grads_kernel, out_shape=(jax.ShapeDtypeStruct((ROUNDS, UNI...  149 us
    pallas_call x1, Pallas kernels, update(): pl.pallas_call(update_kernel, out_shape=(jax.ShapeDtypeStruct((PADDED, 12...  31.5 us
    pallas_call x1, Pallas kernels, finish(): pl.pallas_call(finish_kernel, out_shape=(rows,) * 3 + (row,) * 2 + (jax.S...  5.38 us

profile of v9, /device:TPU:24, one launch (start us, length us, event | category | flops | bytes accessed | tf_op | source)
XLA Modules:
  0.0 189.1 jit_solution(806030576448770020)
XLA Ops:
  0.6 2.0 %copy.15 = bf16[1,1,2,1,196,768]{5,4,2,3,1,0:T(8,128)(2,1)} copy(bf16[1,1,2,1,196,768]{5,2,4,3,1,0:T(2,128)(2,1)} %param.7) | data formatting | bytes 1204224 | tf_op args[0]
  2.6 149.4 %grads.1 = (bf16[22,6,16,128]{3,2,1,0:T(8,128)(2,1)}, f32[8,128]{1,0:T(8,128)}) custom-call(f32[2098,128]{1,0:T(8,128)} %bitcast.10, bf16[2,196,768]{2,1,0:T(8,128)(2,1)} %bitcast.12, s32[2]{0:T(128)} %bitcast.14, s32[2]{0:T(128)} %bitcast.15), custom_call_target="tpu_custom_call" | custom-call | tf_op jit(solution)/shard_map/grads/pallas_call | solution.py:932
  152.0 31.5 %update.1 = (f32[2112,128]{1,0:T(8,128)}, f32[2098,128]{1,0:T(8,128)}, f32[2098,128]{1,0:T(8,128)}) custom-call(bf16[22,6,16,128]{3,2,1,0:T(8,128)(2,1)} %get-tuple-element.17.red_ref, f32[1,268544]{1,0:T(1,128)} %first_ref.1, f32[1,268544]{1,0:T(1,128)} %second_ref.1), custom_call_target="tpu_custom_call" | custom-call | tf_op jit(solution)/shard_map/update/pallas_call | solution.py:1264
  183.5 5.4 %finish.1 = (f32[2098,128]{1,0:T(8,128)}, f32[2098,128]{1,0:T(8,128)}, f32[2098,128]{1,0:T(8,128)}, f32[1,268544]{1,0:T(1,128)}, f32[1,268544]{1,0:T(1,128)}, /*index=5*/f32[1,1]{1,0:T(1,128)}) custom-call(f32[2112,128]{1,0:T(8,128)} %get-tuple-element.18.sum_ref, f32[2098,128]{1,0:T(8,128)} %bitcast.11, f32[2098,128]{1,0:T(8,128)} %bitcast.13, ...), custom_call_target="tpu_custom_call" | custom-call | tf_op jit(solution)/shard_map/finish/pallas_call | solution.py:1355

commit v10 on v9

--- a/solution.py
+++ b/solution.py
@@ -1199,7 +1199,7 @@
     fix_two = 1.0 / (1.0 - BETA_TWO**STEP)
 
     half = PADDED // 2
-    step = 96
+    step = 176
     for rows_of in (first, second):
         rows_of[pl.ds(SHARD, PADDED - SHARD), :] = jnp.zeros((PADDED - SHARD, 128), F32)
 

time: 191 us -> 191 us (level)
  no operation moved by 1% of the time
where the time goes in v10:
time: 191 us; the launch traced here: 189 us
  Pallas kernels  186 us (97%)
  local copies, waits for them, and re-layouts  1.95 us (1%)
    pallas_call x1, Pallas kernels, grads(): pl.pallas_call(grads_kernel, out_shape=(jax.ShapeDtypeStruct((ROUNDS, UNI...  149 us
    pallas_call x1, Pallas kernels, update(): pl.pallas_call(update_kernel, out_shape=(jax.ShapeDtypeStruct((PADDED, 12...  31.5 us
    pallas_call x1, Pallas kernels, finish(): pl.pallas_call(finish_kernel, out_shape=(rows,) * 3 + (row,) * 2 + (jax.S...  5.38 us

profile of v10, /device:TPU:24, one launch (start us, length us, event | category | flops | bytes accessed | tf_op | source)
XLA Modules:
  0.0 189.1 jit_solution(12965502226340294287)
XLA Ops:
  0.6 2.0 %copy.15 = bf16[1,1,2,1,196,768]{5,4,2,3,1,0:T(8,128)(2,1)} copy(bf16[1,1,2,1,196,768]{5,2,4,3,1,0:T(2,128)(2,1)} %param.7) | data formatting | bytes 1204224 | tf_op args[0]
  2.6 149.4 %grads.1 = (bf16[22,6,16,128]{3,2,1,0:T(8,128)(2,1)}, f32[8,128]{1,0:T(8,128)}) custom-call(f32[2098,128]{1,0:T(8,128)} %bitcast.10, bf16[2,196,768]{2,1,0:T(8,128)(2,1)} %bitcast.12, s32[2]{0:T(128)} %bitcast.14, s32[2]{0:T(128)} %bitcast.15), custom_call_target="tpu_custom_call" | custom-call | tf_op jit(solution)/shard_map/grads/pallas_call | solution.py:932
  152.0 31.5 %update.1 = (f32[2112,128]{1,0:T(8,128)}, f32[2098,128]{1,0:T(8,128)}, f32[2098,128]{1,0:T(8,128)}) custom-call(bf16[22,6,16,128]{3,2,1,0:T(8,128)(2,1)} %get-tuple-element.17.red_ref, f32[1,268544]{1,0:T(1,128)} %first_ref.1, f32[1,268544]{1,0:T(1,128)} %second_ref.1), custom_call_target="tpu_custom_call" | custom-call | tf_op jit(solution)/shard_map/update/pallas_call | solution.py:1264
  183.5 5.4 %finish.1 = (f32[2098,128]{1,0:T(8,128)}, f32[2098,128]{1,0:T(8,128)}, f32[2098,128]{1,0:T(8,128)}, f32[1,268544]{1,0:T(1,128)}, f32[1,268544]{1,0:T(1,128)}, /*index=5*/f32[1,1]{1,0:T(1,128)}) custom-call(f32[2112,128]{1,0:T(8,128)} %get-tuple-element.18.sum_ref, f32[2098,128]{1,0:T(8,128)} %bitcast.11, f32[2098,128]{1,0:T(8,128)} %bitcast.13, ...), custom_call_target="tpu_custom_call" | custom-call | tf_op jit(solution)/shard_map/finish/pallas_call | solution.py:1355
